TPU v7x, 32 devices: a whole 2x2x4 slice. The times are simulated.
32 devices in a mesh: rep: 16 (over z, y, x), shard: 2 (over core).
Axes of the slice: x: 2, y: 2, z: 4, core: 2. Of those that a mesh axis runs over, the one named last changes fastest.
Arguments:
- tokens: bfloat16 [16384, 1024], P(('rep', 'shard')), may hold values from -6 to 6
- cotangent: bfloat16 [16384, 1024], P(('rep', 'shard')), may hold values from -6 to 6
- doc_blocks: int32 [16, 8], P('rep'), may hold values from 0 to 1, as said below
- gain_in: bfloat16 [1024], P('shard'), may hold values from 0.5 to 1.5
- w_query: bfloat16 [1024, 512], P('shard'), may hold values from -0.1875 to 0.1875
- w_kv: bfloat16 [1024, 256], P('shard'), may hold values from -0.1875 to 0.1875
- w_attn_out: bfloat16 [512, 1024], P('shard'), may hold values from -0.25 to 0.25
- gain_attn: bfloat16 [1024], P('shard'), may hold values from 0.5 to 1.5
- w_ssm_in: bfloat16 [1024, 3072], P('shard'), may hold values from -0.1875 to 0.1875
- w_ssm_aux: bfloat16 [1024, 280], P('shard'), may hold values from -0.1875 to 0.1875
- dt_bias: float32 [24], replicated, may hold values from -9 to -2.3
- decay_log: float32 [24], replicated, may hold values from 0 to 2.77
- w_ssm_out: bfloat16 [1536, 1024], P('shard'), may hold values from -0.15625 to 0.15625
- gain_ssm: bfloat16 [1024], P('shard'), may hold values from 0.5 to 1.5
- gain_ff: bfloat16 [1024], P('shard'), may hold values from 0.5 to 1.5
- w_gate: bfloat16 [1024, 2048], P('shard'), may hold values from -0.1875 to 0.1875
- w_up: bfloat16 [1024, 2048], P('shard'), may hold values from -0.1875 to 0.1875
- w_down: bfloat16 [2048, 1024], P('shard'), may hold values from -0.125 to 0.125
Outputs:
- output: bfloat16 [16384, 1024], P(('rep', 'shard'))
- grad_tokens: float32 [16384, 1024], P(('rep', 'shard'))
- grad_gain_in: float32 [1024], P('shard')
- grad_w_query: float32 [1024, 512], P('shard')
- grad_w_kv: float32 [1024, 256], P('shard')
- grad_w_attn_out: float32 [512, 1024], P('shard')
- grad_gain_attn: float32 [1024], P('shard')
- grad_w_ssm_in: float32 [1024, 3072], P('shard')
- grad_w_ssm_aux: float32 [1024, 280], P('shard')
- grad_dt_bias: float32 [24], replicated
- grad_decay_log: float32 [24], replicated
- grad_w_ssm_out: float32 [1536, 1024], P('shard')
- grad_gain_ssm: float32 [1024], P('shard')
- grad_gain_ff: float32 [1024], P('shard')
- grad_w_gate: float32 [1024, 2048], P('shard')
- grad_w_up: float32 [1024, 2048], P('shard')
- grad_w_down: float32 [2048, 1024], P('shard')
Inputs may be any that keep to these rules, and one draw needn't show every extreme that they name: `doc_blocks`: each group holds two documents: a row is 0 on the blocks before one cut block and 1 from the cut block on. The cut block lies at 1 to 2 or at 6 to 7, so that one document runs across the middle of the group.
All inputs are finite; a program needn't handle non-finite values.
Results may differ from a plain program's by a relative error of at most 0.015.
The roundings to bfloat16 on the way count: a program that leaves them out, or rounds other values in their place, can miss the bound.
Values may be sent and summed in bfloat16 or wider, within the bound.
No kernel may reach another device: no remote copies, remote signals or barrier semaphores. Data moves between devices by JAX's collectives and lax.ppermute only.
A program may use at most 256 MiB of HBM per device.

v0:
```python
from functools import partial

import jax
import jax.numpy as jnp
from jax import lax
from jax.sharding import PartitionSpec as P

HD = 64
QH = 8
KVH = 2
SH = 24
SP = 64
STATE = 128
WIN = 1024
BLOCK = 128
INNER = 1536


HIGHEST = lax.Precision.HIGHEST
EPSILON = 1e-05
NEGATIVE = -1e30


def from_behind(value, axis, steps):
    count = lax.axis_size(axis)
    initial, last = (max(0, -steps), min(count, count - steps))
    return lax.ppermute(value, axis, [(source, source + steps) for source in range(initial, last)])


def matmul_plain(left, right):
    return jnp.dot(left, right, preferred_element_type=jnp.float32)


def matmul_left(left, right):
    return lax.dot_general(
        left, right, (((0,), (0,)), ((), ())), preferred_element_type=jnp.float32
    )


def matmul_right(left, right):
    return lax.dot_general(
        left, right, (((1,), (1,)), ((), ())), preferred_element_type=jnp.float32
    )


def rms_norm(values, gain):
    return values * lax.rsqrt(jnp.mean(values * values, axis=-1, keepdims=True) + EPSILON) * gain


def ssm_inputs(mixed_in, aux_out, dt_bias, decay_log):
    row_count = mixed_in.shape[0]
    step_size = jax.nn.softplus(aux_out[:, 2 * STATE :] + dt_bias)
    log_decay = -step_size * jnp.exp(decay_log)
    scaled = mixed_in[:, :INNER].reshape(row_count, SH, SP) * step_size[:, :, None]
    return (scaled, aux_out[:, :STATE], aux_out[:, STATE : 2 * STATE], log_decay)


def block_step(state_now, pieces):
    scaled, b_in, c_out, log_decay, reset_flag = pieces
    state_now = jnp.where(reset_flag, 0.0, state_now)
    cumulated = jnp.cumsum(log_decay, axis=0)
    places = jnp.arange(BLOCK, dtype=jnp.int32)
    lower_mask = (places[:, None] >= places[None, :])[:, :, None]
    spread = jnp.where(lower_mask, cumulated[:, None, :] - cumulated[None, :, :], 0.0)
    weight = (
        jnp.where(lower_mask, jnp.exp(spread), 0.0)
        * jnp.dot(c_out, b_in.T, precision=HIGHEST)[:, :, None]
    )
    inner_part = jnp.einsum("tsh,shp->thp", weight, scaled, precision=HIGHEST)
    outer_part = jnp.exp(cumulated)[:, :, None] * jnp.einsum(
        "tn,hpn->thp", c_out, state_now, precision=HIGHEST
    )
    tail_decay = jnp.exp(cumulated[-1:] - cumulated)
    fresh_state = jnp.einsum("sh,shp,sn->hpn", tail_decay, scaled, b_in, precision=HIGHEST)
    return (
        jnp.exp(cumulated[-1])[:, None, None] * state_now + fresh_state,
        inner_part + outer_part,
    )


def scan_blocks(scaled, b_in, c_out, log_decay, state_in, block_docs, prior_doc):
    count = block_docs.shape[0]
    earlier = jnp.concatenate([prior_doc, block_docs[:-1]])
    resets = block_docs != earlier
    state_out, outputs = lax.scan(
        jax.checkpoint(block_step),
        state_in,
        (
            scaled.reshape(count, BLOCK, SH, SP),
            b_in.reshape(count, BLOCK, STATE),
            c_out.reshape(count, BLOCK, STATE),
            log_decay.reshape(count, BLOCK, SH),
            resets,
        ),
    )
    return (outputs.reshape(count * BLOCK, SH, SP), state_out)


def carry_in(c_out, log_decay, state_in, alive):
    cumulated = jnp.cumsum(log_decay, axis=0)
    return (
        alive[:, None, None]
        * jnp.exp(cumulated)[:, :, None]
        * jnp.einsum("tn,hpn->thp", c_out, state_in, precision=HIGHEST)
    )


def gate_ssm(ssm_out, mixed_in):
    return ssm_out.reshape(ssm_out.shape[0], INNER) * jax.nn.silu(mixed_in[:, INNER:])


def join_branches(attn_branch, ssm_branch, gain_attn, gain_ssm, hidden):
    return hidden + 0.5 * (rms_norm(attn_branch, gain_attn) + rms_norm(ssm_branch, gain_ssm))


def swish_gate(gate_val, up_val):
    return jax.nn.silu(gate_val) * up_val


def block_mask(q_docs, k_docs, row_start, halo_rows):
    q_place = halo_rows + row_start + jnp.arange(q_docs.shape[0], dtype=jnp.int32)
    k_place = row_start + jnp.arange(k_docs.shape[0], dtype=jnp.int32)
    return (
        (q_docs[:, None] == k_docs[None, :])
        & (k_place[None, :] <= q_place[:, None])
        & (k_place[None, :] > q_place[:, None] - WIN)
    )


def score_block(q_part, k_part, allowed, score_scale):
    raw = jnp.einsum("igd,jd->gij", q_part, k_part, preferred_element_type=jnp.float32)
    return jnp.where(allowed[None], raw * score_scale, NEGATIVE)


def local(
    tokens,
    cotangent,
    doc_blocks,
    gain_in,
    w_query,
    w_kv,
    w_attn_out,
    gain_attn,
    w_ssm_in,
    w_ssm_aux,
    dt_bias,
    decay_log,
    w_ssm_out,
    gain_ssm,
    gain_ff,
    w_gate,
    w_up,
    w_down,
):
    row_count = tokens.shape[0]
    position = lax.axis_index("shard")
    block_rows = min(512, row_count)
    halo_rows = min(WIN, row_count)
    group_size = QH // KVH
    score_scale = HD ** (-0.5)
    blocks_here = row_count // BLOCK
    group_docs = doc_blocks[0]
    block_docs = lax.dynamic_slice_in_dim(group_docs, position * blocks_here, blocks_here, 0)
    prior_doc = lax.dynamic_slice_in_dim(
        group_docs, jnp.maximum(position * blocks_here - 1, 0), 1, 0
    )
    halo_docs = lax.dynamic_slice_in_dim(
        group_docs,
        jnp.maximum(position * blocks_here - halo_rows // BLOCK, 0),
        halo_rows // BLOCK,
        0,
    )
    halo_docs = jnp.where(position > 0, halo_docs, -1)
    token_docs = jnp.repeat(block_docs, BLOCK)
    key_docs = jnp.concatenate([jnp.repeat(halo_docs, BLOCK), token_docs])
    alive = ((token_docs == prior_doc[0]) & (position > 0)).astype(jnp.float32)
    mixer_full = (
        lax.all_gather(gain_in, "shard", axis=0, tiled=True),
        lax.all_gather(w_query, "shard", axis=0, tiled=True),
        lax.all_gather(w_kv, "shard", axis=0, tiled=True),
        lax.all_gather(w_attn_out, "shard", axis=0, tiled=True),
        lax.all_gather(gain_attn, "shard", axis=0, tiled=True),
        lax.all_gather(w_ssm_in, "shard", axis=0, tiled=True),
        lax.all_gather(w_ssm_aux, "shard", axis=0, tiled=True),
        lax.all_gather(w_ssm_out, "shard", axis=0, tiled=True),
        lax.all_gather(gain_ssm, "shard", axis=0, tiled=True),
    )
    ffn_full = (
        lax.all_gather(gain_ff, "shard", axis=0, tiled=True),
        lax.all_gather(w_gate, "shard", axis=0, tiled=True),
        lax.all_gather(w_up, "shard", axis=0, tiled=True),
        lax.all_gather(w_down, "shard", axis=0, tiled=True),
    )
    (
        gain_in_full,
        query_full,
        kv_full,
        attn_out_full,
        gain_attn_full,
        ssm_in_full,
        ssm_aux_full,
        ssm_out_full,
        gain_ssm_full,
    ) = mixer_full
    gain_ff_full, gate_full, up_full, down_full = ffn_full
    hidden = tokens.astype(jnp.float32)
    normed32, norm_in_back = jax.vjp(rms_norm, hidden, gain_in_full.astype(jnp.float32))
    normed = normed32.astype(jnp.bfloat16)
    queries = matmul_plain(normed, query_full).astype(jnp.bfloat16)
    key_vals = matmul_plain(normed, kv_full).astype(jnp.bfloat16)
    key_prior = from_behind(key_vals, "shard", 1)
    key_ext = jnp.concatenate([key_prior, key_vals])
    q_heads = queries.reshape(row_count, KVH, group_size, HD)
    k_heads = key_ext[:, : KVH * HD].reshape(halo_rows + row_count, KVH, HD)
    v_heads = key_ext[:, KVH * HD :].reshape(halo_rows + row_count, KVH, HD)
    log_totals = []
    row_start = 0
    allowed = block_mask(token_docs, key_docs, row_start, halo_rows)
    mask_list = [allowed]
    head_outs = []
    for head_index in range(KVH):
        scores = score_block(
            q_heads[row_start : row_start + block_rows, head_index],
            k_heads[row_start : row_start + halo_rows + block_rows, head_index],
            allowed,
            score_scale,
        )
        top_score = jnp.max(scores, axis=-1, keepdims=True)
        log_total = top_score + jnp.log(
            jnp.sum(jnp.exp(scores - top_score), axis=-1, keepdims=True)
        )
        prob_low = jnp.exp(scores - log_total).astype(jnp.bfloat16)
        head_outs.append(
            jnp.einsum(
                "gij,jd->igd",
                prob_low,
                v_heads[row_start : row_start + halo_rows + block_rows, head_index],
                preferred_element_type=jnp.float32,
            )
        )
        log_totals.append(log_total)
    attended_parts = jnp.stack(head_outs, axis=1).reshape(block_rows, QH * HD)
    attended = attended_parts.astype(jnp.bfloat16)
    attn_branch = matmul_plain(attended, attn_out_full)
    mixed_in = matmul_plain(normed, ssm_in_full)
    aux_out = matmul_plain(normed, ssm_aux_full)
    ssm_values, ssm_in_back = jax.vjp(ssm_inputs, mixed_in, aux_out, dt_bias, decay_log)
    scaled, b_in, c_out, log_decay = ssm_values
    local_scan = partial(
        scan_blocks,
        state_in=jnp.zeros((SH, SP, STATE), jnp.float32),
        block_docs=block_docs,
        prior_doc=prior_doc,
    )
    (ssm_local, state_end), scan_back = jax.vjp(local_scan, scaled, b_in, c_out, log_decay)
    state_prior = from_behind(state_end, "shard", 1)
    incoming, carry_back = jax.vjp(partial(carry_in, alive=alive), c_out, log_decay, state_prior)
    ssm_out = ssm_local + incoming
    gated32, gate_back = jax.vjp(gate_ssm, ssm_out, mixed_in)
    gated = gated32.astype(jnp.bfloat16)
    ssm_branch = matmul_plain(gated, ssm_out_full)
    middle, join_back = jax.vjp(
        join_branches,
        attn_branch,
        ssm_branch,
        gain_attn_full.astype(jnp.float32),
        gain_ssm_full.astype(jnp.float32),
        hidden,
    )
    normed_ff32, norm_ff_back = jax.vjp(rms_norm, middle, gain_ff_full.astype(jnp.float32))
    normed_ff = normed_ff32.astype(jnp.bfloat16)
    gate_val = matmul_plain(normed_ff, gate_full)
    up_val = matmul_plain(normed_ff, up_full)
    activated32, swish_back = jax.vjp(swish_gate, gate_val, up_val)
    activated = activated32.astype(jnp.bfloat16)
    output = (middle + matmul_plain(activated, down_full)).astype(jnp.bfloat16)
    grad_down = matmul_left(activated, cotangent)
    d_activated = matmul_right(cotangent, down_full)
    d_gate, d_up = swish_back(d_activated)
    d_gate_low = d_gate.astype(jnp.bfloat16)
    d_up_low = d_up.astype(jnp.bfloat16)
    grad_gate = matmul_left(normed_ff, d_gate_low)
    grad_up = matmul_left(normed_ff, d_up_low)
    d_normed_ff = matmul_right(d_gate_low, gate_full) + matmul_right(d_up_low, up_full)
    d_middle_norm, grad_gain_ff = norm_ff_back(d_normed_ff)
    d_middle = cotangent.astype(jnp.float32) + d_middle_norm
    d_attn_branch, d_ssm_branch, grad_gain_attn, grad_gain_ssm, d_hidden = join_back(d_middle)
    d_attn_low = d_attn_branch.astype(jnp.bfloat16)
    d_ssm_low = d_ssm_branch.astype(jnp.bfloat16)
    grad_attn_out = matmul_left(attended, d_attn_low)
    d_attended = matmul_right(d_attn_low, attn_out_full).astype(jnp.bfloat16)
    d_heads = d_attended.reshape(row_count, KVH, group_size, HD)
    d_keys = jnp.zeros((halo_rows + row_count, KVH, HD), jnp.float32)
    d_values = jnp.zeros((halo_rows + row_count, KVH, HD), jnp.float32)
    d_query_parts = []
    for number, row_start in enumerate(range(0, row_count, block_rows)):
        head_grads = []
        for head_index in range(KVH):
            q_part = q_heads[row_start : row_start + block_rows, head_index]
            k_part = k_heads[row_start : row_start + halo_rows + block_rows, head_index]
            v_part = v_heads[row_start : row_start + halo_rows + block_rows, head_index]
            d_part = d_heads[row_start : row_start + block_rows, head_index]
            scores = score_block(q_part, k_part, mask_list[number], score_scale)
            prob_full = jnp.exp(scores - log_totals[number * KVH + head_index])
            prob_low = prob_full.astype(jnp.bfloat16)
            d_values = d_values.at[row_start : row_start + halo_rows + block_rows, head_index].add(
                jnp.einsum("gij,igd->jd", prob_low, d_part, preferred_element_type=jnp.float32)
            )
            d_probs = jnp.einsum("igd,jd->gij", d_part, v_part, preferred_element_type=jnp.float32)
            d_scores = (
                prob_full * (d_probs - jnp.sum(prob_full * d_probs, axis=-1, keepdims=True))
            ).astype(jnp.bfloat16)
            head_grads.append(
                jnp.einsum("gij,jd->igd", d_scores, k_part, preferred_element_type=jnp.float32)
                * score_scale
            )
            d_keys = d_keys.at[row_start : row_start + halo_rows + block_rows, head_index].add(
                jnp.einsum("gij,igd->jd", d_scores, q_part, preferred_element_type=jnp.float32)
                * score_scale
            )
        d_query_parts.append(jnp.stack(head_grads, axis=1).reshape(block_rows, QH * HD))
    d_query_low = d_query_parts[0].astype(jnp.bfloat16)
    d_kv_ext = jnp.concatenate(
        [
            d_keys.reshape(halo_rows + row_count, KVH * HD),
            d_values.reshape(halo_rows + row_count, KVH * HD),
        ],
        axis=1,
    )
    d_kv_next = from_behind(d_kv_ext[:halo_rows].astype(jnp.bfloat16), "shard", -1).astype(
        jnp.float32
    )
    d_kv = d_kv_ext[halo_rows:] + d_kv_next
    d_kv_low = d_kv.astype(jnp.bfloat16)
    grad_ssm_out = matmul_left(gated, d_ssm_low)
    d_gated = matmul_right(d_ssm_low, ssm_out_full)
    d_ssm_out, d_mixed_gate = gate_back(d_gated)
    d_c_carry, d_decay_carry, d_state_prior = carry_back(d_ssm_out)
    d_state_end = from_behind(d_state_prior.astype(jnp.bfloat16), "shard", -1).astype(
        d_state_prior.dtype
    )
    d_scaled, d_b_in, d_c_out, d_decay = scan_back((d_ssm_out, d_state_end))
    d_mixed_pre, d_aux, grad_dt_bias, grad_decay_log = ssm_in_back(
        (d_scaled, d_b_in, d_c_out + d_c_carry, d_decay + d_decay_carry)
    )
    d_mixed_low = (d_mixed_gate + d_mixed_pre).astype(jnp.bfloat16)
    d_aux_low = d_aux.astype(jnp.bfloat16)
    grad_query = matmul_left(normed, d_query_low)
    grad_kv = matmul_left(normed, d_kv_low)
    grad_ssm_in = matmul_left(normed, d_mixed_low)
    grad_ssm_aux = matmul_left(normed, d_aux_low)
    d_normed = (
        matmul_right(d_query_low, query_full)
        + matmul_right(d_kv_low, kv_full)
        + matmul_right(d_mixed_low, ssm_in_full)
        + matmul_right(d_aux_low, ssm_aux_full)
    )
    d_hidden_norm, grad_gain_in = norm_in_back(d_normed)
    grad_tokens = d_hidden + d_hidden_norm
    shares = (
        lax.psum_scatter(
            grad_gain_in.astype(jnp.bfloat16), "shard", scatter_dimension=0, tiled=True
        ).astype(jnp.float32),
        lax.psum_scatter(
            grad_query.astype(jnp.bfloat16), "shard", scatter_dimension=0, tiled=True
        ).astype(jnp.float32),
        lax.psum_scatter(
            grad_kv.astype(jnp.bfloat16), "shard", scatter_dimension=0, tiled=True
        ).astype(jnp.float32),
        lax.psum_scatter(
            grad_attn_out.astype(jnp.bfloat16), "shard", scatter_dimension=0, tiled=True
        ).astype(jnp.float32),
        lax.psum_scatter(
            grad_gain_attn.astype(jnp.bfloat16), "shard", scatter_dimension=0, tiled=True
        ).astype(jnp.float32),
        lax.psum_scatter(
            grad_ssm_in.astype(jnp.bfloat16), "shard", scatter_dimension=0, tiled=True
        ).astype(jnp.float32),
        lax.psum_scatter(
            grad_ssm_aux.astype(jnp.bfloat16), "shard", scatter_dimension=0, tiled=True
        ).astype(jnp.float32),
        lax.psum_scatter(
            grad_ssm_out.astype(jnp.bfloat16), "shard", scatter_dimension=0, tiled=True
        ).astype(jnp.float32),
        lax.psum_scatter(
            grad_gain_ssm.astype(jnp.bfloat16), "shard", scatter_dimension=0, tiled=True
        ).astype(jnp.float32),
        lax.psum_scatter(
            grad_gain_ff.astype(jnp.bfloat16), "shard", scatter_dimension=0, tiled=True
        ).astype(jnp.float32),
        lax.psum_scatter(
            grad_gate.astype(jnp.bfloat16), "shard", scatter_dimension=0, tiled=True
        ).astype(jnp.float32),
        lax.psum_scatter(
            grad_up.astype(jnp.bfloat16), "shard", scatter_dimension=0, tiled=True
        ).astype(jnp.float32),
        lax.psum_scatter(
            grad_down.astype(jnp.bfloat16), "shard", scatter_dimension=0, tiled=True
        ).astype(jnp.float32),
    )
    summed = lax.psum(
        (
            shares[0],
            shares[1],
            shares[2],
            shares[3],
            shares[4],
            shares[5],
            shares[6],
            shares[7],
            shares[8],
            shares[9],
            shares[10],
            shares[11],
            shares[12],
        ),
        "rep",
    )
    mixer_sums = summed[:9]
    ffn_sums = summed[9:]
    head_totals = lax.psum((grad_dt_bias, grad_decay_log), ("rep", "shard"))
    return (
        output,
        grad_tokens,
        mixer_sums[0],
        mixer_sums[1],
        mixer_sums[2],
        mixer_sums[3],
        mixer_sums[4],
        mixer_sums[5],
        mixer_sums[6],
        head_totals[0],
        head_totals[1],
        mixer_sums[7],
        mixer_sums[8],
        ffn_sums[0],
        ffn_sums[1],
        ffn_sums[2],
        ffn_sums[3],
    )


def solution(mesh):
    return jax.shard_map(
        local,
        mesh=mesh,
        in_specs=(
            P(("rep", "shard"), None),
            P(("rep", "shard"), None),
            P("rep", None),
            P("shard"),
            P("shard", None),
            P("shard", None),
            P("shard", None),
            P("shard"),
            P("shard", None),
            P("shard", None),
            P(),
            P(),
            P("shard", None),
            P("shard"),
            P("shard"),
            P("shard", None),
            P("shard", None),
            P("shard", None),
        ),
        out_specs=(
            P(("rep", "shard"), None),
            P(("rep", "shard"), None),
            P("shard"),
            P("shard", None),
            P("shard", None),
            P("shard", None),
            P("shard"),
            P("shard", None),
            P("shard", None),
            P(),
            P(),
            P("shard", None),
            P("shard"),
            P("shard"),
            P("shard", None),
            P("shard", None),
            P("shard", None),
        ),
        check_vma=False,
    )
```

profile of v0, /device:TPU:1, one launch (start us, length us, event | category | flops | bytes accessed | tf_op | source)
XLA Modules:
  0.0 1725.5 jit_solution(8381360605015080301)
XLA Ops:
  53.3 5.7 fusion.189
  67.7 4.9 reshape.572
  77.2 137.3 %while.45 = (s32[]{:T(128)}, f32[24,64,128]{2,1,0:T(8,128)S(1)}, f32[4,128,24,64]{1,0,3,2:T(4,128)}, f32[4,24,64,128]{3,2,1,0:T(8,128)}, f32[4,128,24]{2,1,0:T(8...) while((s32[]{:T(128)}, f32[24,64,128]{2,1,0:T(8,128)S(1)}, ...), condition=%wide.region_8.9_spmd.clone.clone, body=%wide.region_6.8_spmd.clone.clone.sunk | while | flops 935067648 | bytes 10061435 | solution.py:85
  87.4 20.2 %dynamic_update_slice.72 = f32[4,128,24,64]{1,0,3,2:T(4,128)} dynamic-update-slice(f32[4,128,24,64]{1,0,3,2:T(4,128)} %get-tuple-element.938, f32[1,128,24,64]{1,0,3,2:T(1,128)S(1)} %bitcast.497, s32[]{:T(128)} %get-tuple-element.936, s32[]{:T(128)} %constant.246.clone.1..sunk, s32[]{:T(128)} %constant.246.clone.1..sunk, s32[]{:T(128)} %constant.246.clone.1..sunk) | dynamic-update-slice | bytes 1572868 | tf_op jit(solution)/shard_map/jvp()/while/body/jit(dynamic_update_index_in_dim)/dynamic_update_slice | solution.py:85
  121.9 20.1 %dynamic_update_slice.72 = f32[4,128,24,64]{1,0,3,2:T(4,128)} dynamic-update-slice(f32[4,128,24,64]{1,0,3,2:T(4,128)} %get-tuple-element.938, f32[1,128,24,64]{1,0,3,2:T(1,128)S(1)} %bitcast.497, s32[]{:T(128)} %get-tuple-element.936, s32[]{:T(128)} %constant.246.clone.1..sunk, s32[]{:T(128)} %constant.246.clone.1..sunk, s32[]{:T(128)} %constant.246.clone.1..sunk) | dynamic-update-slice | bytes 1572868 | tf_op jit(solution)/shard_map/jvp()/while/body/jit(dynamic_update_index_in_dim)/dynamic_update_slice | solution.py:85
  156.2 20.1 %dynamic_update_slice.72 = f32[4,128,24,64]{1,0,3,2:T(4,128)} dynamic-update-slice(f32[4,128,24,64]{1,0,3,2:T(4,128)} %get-tuple-element.938, f32[1,128,24,64]{1,0,3,2:T(1,128)S(1)} %bitcast.497, s32[]{:T(128)} %get-tuple-element.936, s32[]{:T(128)} %constant.246.clone.1..sunk, s32[]{:T(128)} %constant.246.clone.1..sunk, s32[]{:T(128)} %constant.246.clone.1..sunk) | dynamic-update-slice | bytes 1572868 | tf_op jit(solution)/shard_map/jvp()/while/body/jit(dynamic_update_index_in_dim)/dynamic_update_slice | solution.py:85
  190.4 20.1 %dynamic_update_slice.72 = f32[4,128,24,64]{1,0,3,2:T(4,128)} dynamic-update-slice(f32[4,128,24,64]{1,0,3,2:T(4,128)} %get-tuple-element.938, f32[1,128,24,64]{1,0,3,2:T(1,128)S(1)} %bitcast.497, s32[]{:T(128)} %get-tuple-element.936, s32[]{:T(128)} %constant.246.clone.1..sunk, s32[]{:T(128)} %constant.246.clone.1..sunk, s32[]{:T(128)} %constant.246.clone.1..sunk) | dynamic-update-slice | bytes 1572868 | tf_op jit(solution)/shard_map/jvp()/while/body/jit(dynamic_update_index_in_dim)/dynamic_update_slice | solution.py:85
  214.6 14.3 collective-permute-start.1
  228.9 5.6 fusion.139
  237.6 5.0 reshape.575
  242.7 7.7 multiply_add_fusion
  253.9 4.9 multiply_convert_fusion.2
  267.0 6.9 fusion.201
  273.9 6.9 fusion.202
  280.7 10.2 multiply_convert_fusion
  305.8 5.6 fusion.111
  313.8 6.2 reshape.626
  322.4 6.5 convolution_bitcast_fusion.2
  328.9 6.3 convolution_bitcast_fusion.3
  335.3 4.6 fusion.164
  341.5 5.7 reduce-window.16
  347.8 6.1 copy.163
  353.9 13.8 fusion.99
  367.8 15.2 fusion.101
  404.5 129.8 %while.44 = (s32[]{:T(128)}, f32[24,64,128]{2,1,0:T(8,128)S(1)}, f32[4,128,24,64]{1,3,2,0:T(8,128)}, f32[4,128,128]{2,1,0:T(8,128)}, f32[4,128,128]{2,1,0:T(8,12...) while((s32[]{:T(128)}, f32[24,64,128]{2,1,0:T(8,128)S(1)}, ...), condition=%wide.region_27.28_spmd, body=%wide.region_18.27_spmd.sunk | while | flops 2199504896 | bytes 22173092 | solution.py:85
  563.2 4.4 convolution_convert_fusion.3
  589.8 6.5 reshape.627
  601.7 5.7 convolution_convert_fusion
  612.8 6.1 add_convert_fusion.1
  619.0 40.0 %all-reduce.11 = (f32[24]{0:T(128)}, f32[24]{0:T(128)}) all-reduce(f32[24]{0:T(128)S(1)} %get-tuple-element.682, f32[24]{0:T(128)S(1)} %exponential_multiply_fusion), channel_id=1, replica_groups=mesh['rep'=16,'shard'=2] {'rep','shard'}, use_global_device_ids=true, to_apply=%region_50.51 | all-reduce | flops 48 | bytes 384 | tf_op jit(solution)/shard_map/psum | solution.py:421
  661.5 6.9 fusion.155
  678.2 1040.4 %all-reduce.15 = (f32[512]{0:T(512)}, f32[512,512]{1,0:T(8,128)}, f32[512,256]{1,0:T(8,128)}, f32[256,1024]{1,0:T(8,128)}, f32[512]{0:T(512)}, /*index=5*/f32[51...) all-reduce(f32[512]{0:T(512)S(1)} %dynamic-slice_convert_fusion.3, ...), channel_id=1, replica_groups=mesh['rep'=16,'shard'=2] {'rep'}, use_global_device_ids=true, to_apply=%region_35.36 | all-reduce | flops 6305792 | bytes 37838848 | tf_op jit(solution)/shard_map/psum | solution.py:401
  (611 shorter events, 375.2 us)
Async XLA Ops:
  7.2 32.7 %all-gather.12.cloned.1.call-start = ((), (), s32[]{:S(2)}) async-start(), calls=%async_computation.9 | async-start | bytes 1572864 | tf_op jit(solution)/shard_map/all_gather | solution.py:179
  7.9 45.4 %all-gather.16.cloned.1.call-start = ((), (), s32[]{:S(2)}) async-start(), calls=%async_computation.11 | async-start | bytes 9437184 | tf_op jit(solution)/shard_map/all_gather | solution.py:183
  8.7 226.7 %all-gather.14.cloned.1.call-start = ((), (), s32[]{:S(2)}) async-start(), calls=%async_computation.10 | async-start | bytes 1572864 | tf_op jit(solution)/shard_map/all_gather | solution.py:181
  9.4 249.4 %all-gather.18.cloned.1.call-start = ((), (), s32[]{:S(2)}) async-start(), calls=%async_computation.12 | async-start | bytes 4718592 | tf_op jit(solution)/shard_map/all_gather | solution.py:185
  10.0 257.0 %all-gather.20.cloned.1.call-start = ((), (), s32[]{:S(2)}) async-start(), calls=%async_computation.13 | async-start | bytes 6291456 | tf_op jit(solution)/shard_map/all_gather | solution.py:190
  10.6 263.3 %all-gather.22.cloned.1.call-start = ((), (), s32[]{:S(2)}) async-start(), calls=%async_computation.14 | async-start | bytes 6291456 | tf_op jit(solution)/shard_map/all_gather | solution.py:191
  11.2 269.6 %all-gather.24.cloned.1.call-start = ((), (), s32[]{:S(2)}) async-start(), calls=%async_computation.15 | async-start | bytes 6291456 | tf_op jit(solution)/shard_map/all_gather | solution.py:192
  13.0 384.9 %copy-start.70 = (f32[2,1,512]{2,1,0:T(1,128)}, f32[2,1,512]{2,1,0:T(1,128)S(1)}, u32[]{:S(2)}) copy-start(f32[2,1,512]{2,1,0:T(1,128)S(1)} %convert_element_type.237) | copy-start | bytes 12292
  15.5 37.8 %copy-start.79 = (f32[512]{0:T(512)}, f32[512]{0:T(512)S(1)}, u32[]{:S(2)}) copy-start(f32[512]{0:T(512)S(1)} %fusion.171) | copy-start | bytes 6148
  16.6 21.6 %collective-permute-start = (bf16[512,256]{1,0:T(8,128)(2,1)S(1)}, bf16[512,256]{1,0:T(8,128)(2,1)}, u32[]{:S(2)}, u32[]{:S(2)}) collective-permute-start(bf16[512,256]{1,0:T(8,128)(2,1)S(1)} %convolution_convert_fusion.13), channel_id=1, source_target_pairs={{0,1},{2,3},{4,5},{6,7},{8,9},{10,11},{12,13},{14,15},{16,17},{18,... | collective-permute-start | bytes 786440 | tf_op jit(solution)/shard_map/ppermute | solution.py:27
  18.0 10.8 copy-start.99
  18.1 660.0 %reduce-scatter.12.cloned.1.call-start = ((), (), s32[]{:S(2)}) async-start(), calls=%async_computation.17 | async-start | bytes 786432 | tf_op jit(solution)/shard_map/reduce_scatter | solution.py:367
  24.0 11.1 copy-start.100
  25.5 14.2 copy-start.82
  25.6 16.3 copy-start.53
  38.1 190.8 %copy-start.22 = (pred[512,1024]{0,1:T(8,128)(4,1)}, pred[512,1024]{0,1:T(8,128)(4,1)S(1)}, u32[]{:S(2)}) copy-start(pred[512,1024]{0,1:T(8,128)(4,1)S(1)} %fusion.129) | copy-start | bytes 1572868
  214.5 20.0 %copy-start.28 = (f32[4,128,128]{2,1,0:T(8,128)}, f32[4,128,128]{2,1,0:T(8,128)S(1)}, u32[]{:S(2)}) copy-start(f32[4,128,128]{2,1,0:T(8,128)S(1)} %get-tuple-element.1030) | copy-start | bytes 786436
  214.5 20.0 %copy-start.64 = (bf16[512,1,4,64]{0,3,2,1:T(8,128)(2,1)S(1)}, bf16[512,1,4,64]{0,3,2,1:T(8,128)(2,1)}, u32[]{:S(2)}) copy-start(bf16[512,1,4,64]{0,3,2,1:T(8,128)(2,1)} %fusion.140) | copy-start | bytes 786436
  214.6 28.1 %collective-permute-start.1 = (f32[24,64,128]{2,1,0:T(8,128)S(1)}, f32[24,64,128]{2,1,0:T(8,128)}, u32[]{:S(2)}, u32[]{:S(2)}) collective-permute-start(f32[24,64,128]{2,1,0:T(8,128)S(1)} %get-tuple-element.463), channel_id=1, source_target_pairs={{0,1},{2,3},{4,5},{6,7},{8,9},{10,11},{12,13},{14,15},{16,17},{18,... | collective-permute-start | bytes 2359304 | tf_op jit(solution)/shard_map/ppermute | solution.py:27
  313.8 78.4 %copy-start.1 = (f32[512,1536]{0,1:T(8,128)}, f32[512,1536]{0,1:T(8,128)S(1)}, u32[]{:S(2)}) copy-start(f32[512,1536]{0,1:T(8,128)S(1)} %copy.156) | copy-start | bytes 9437188
  322.4 12.9 copy-start.55
  353.9 13.8 copy-start.24
  388.4 9.5 collective-permute-start.2
  396.5 3.7 collective-permute-start.3
  400.2 277.9 %reduce-scatter.18.cloned.1.call-start = ((), (), s32[]{:S(2)}) async-start(), calls=%async_computation.20 | async-start | bytes 860160 | tf_op jit(solution)/shard_map/reduce_scatter | solution.py:379
  547.2 130.8 %reduce-scatter.10.cloned.1.call-start = ((), (), s32[]{:S(2)}) async-start(), calls=%async_computation.16 | async-start | bytes 1572864 | tf_op jit(solution)/shard_map/reduce_scatter | solution.py:364
  554.4 123.6 %reduce-scatter.14.cloned.1.call-start = ((), (), s32[]{:S(2)}) async-start(), calls=%async_computation.18 | async-start | bytes 1572864 | tf_op jit(solution)/shard_map/reduce_scatter | solution.py:370
  557.7 120.4 %reduce-scatter.20.cloned.1.call-start = ((), (), s32[]{:S(2)}) async-start(), calls=%async_computation.21 | async-start | bytes 4718592 | tf_op jit(solution)/shard_map/reduce_scatter | solution.py:382
  561.3 116.8 %reduce-scatter.22.cloned.1.call-start = ((), (), s32[]{:S(2)}) async-start(), calls=%async_computation.22 | async-start | bytes 6291456 | tf_op jit(solution)/shard_map/reduce_scatter | solution.py:391
  567.6 110.5 %reduce-scatter.24.cloned.1.call-start = ((), (), s32[]{:S(2)}) async-start(), calls=%async_computation.23 | async-start | bytes 6291456 | tf_op jit(solution)/shard_map/reduce_scatter | solution.py:394
  573.6 104.5 %reduce-scatter.26.cloned.1.call-start = ((), (), s32[]{:S(2)}) async-start(), calls=%async_computation.24 | async-start | bytes 6291456 | tf_op jit(solution)/shard_map/reduce_scatter | solution.py:397
  580.0 98.2 %reduce-scatter.16.cloned.1.call-start = ((), (), s32[]{:S(2)}) async-start(), calls=%async_computation.19 | async-start | bytes 9437184 | tf_op jit(solution)/shard_map/reduce_scatter | solution.py:376
  (112 other events, 482.5 us)
Sparse Core Ops, SparseCore 0:
  9.6 11.4 all-gather.11
  22.6 17.9 all-gather.15
  42.1 10.1 all-gather.13
  53.8 13.2 all-gather.17
  68.5 14.8 all-gather.19
  84.8 14.8 all-gather.21
  101.2 14.8 all-gather.23
  400.3 10.0 reduce-scatter.11
  547.4 10.1 reduce-scatter.17
  559.7 9.6 reduce-scatter.9
  571.7 9.7 reduce-scatter.13
  583.6 12.0 reduce-scatter.19
  598.6 13.3 reduce-scatter.21
  614.7 13.3 reduce-scatter.23
  630.9 13.3 reduce-scatter.25
  647.0 15.6 reduce-scatter.15
where the time goes:
time: 1740 us; the launch traced here: 1730 us
  blocking collectives  1100 us (63%)
  matrix products  287 us (16%)
  local copies, waits for them, and re-layouts  213 us (12%)
  other arithmetic  86.2 us (5%)
  starting transfers between devices  21.7 us (1%)
    psum x1, blocking collectives, local(): lax.psum((shares[0], shares[1], shares[2], shares[3], shares[4], shares[5...  1040 us
    dynamic_update_slice x8, local copies, waits for them, and re-layouts, scan_blocks(): lax.scan(jax.checkpoint(block_step), state_in, (scaled.reshape(count, BLO...  83.1 us
    dot_general x12, matrix products, block_step(): inner_part = jnp.einsum('tsh,shp->thp', weight, scaled, precision=HIGHEST)  47 us
    psum x1, blocking collectives, local(): head_totals = lax.psum((grad_dt_bias, grad_decay_log), ('rep', 'shard'))  40 us
    dot_general x9, matrix products, matmul_right(): lax.dot_general(left, right, (((1,), (1,)), ((), ())), preferred_element_...  39.4 us
    dot_general x9, matrix products, matmul_plain(): return jnp.dot(left, right, preferred_element_type=jnp.float32)  35.2 us
  transfers between devices with their start and end apart: 20, of which 0 were waited for; matrix products, arithmetic and copies ran while one was open for 27% of the time, Pallas kernels for 0%

commit v1 on v0

v1 whole, which is shorter than its diff:
```python
import functools

import jax
import jax.numpy as jnp
from jax import lax
from jax.experimental import pallas as pl
from jax.experimental.pallas import tpu as pltpu
from jax.sharding import PartitionSpec as P

HD = 64
QH = 8
KVH = 2
SH = 24
SP = 64
STATE = 128
BLOCK = 128
INNER = 1536
LANES = 128
KV_AT = QH * HD
AUX_AT = KV_AT + 2 * KVH * HD
EPSILON = 1e-05
NEGATIVE = -1e30
BF = jnp.bfloat16
F32 = jnp.float32
SWAP = [(0, 1), (1, 0)]
VMEM_LIMIT = 56 * 1024 * 1024


def dot(left, right, over=((1,), (0,))):
    return lax.dot_general(left, right, (over, ((), ())), preferred_element_type=F32)


def split2(value):
    high = value.astype(BF)
    return high, (value - high.astype(F32)).astype(BF)


def split3(value):
    high = value.astype(BF)
    rest = value - high.astype(F32)
    middle = rest.astype(BF)
    return high, middle, (rest - middle.astype(F32)).astype(BF)


def dot3(left, right, over=((1,), (0,))):
    left_high, left_low = split2(left)
    right_high, right_low = split2(right)
    return dot(left_high, right_high, over) + (
        dot(left_high, right_low, over) + dot(left_low, right_high, over)
    )


def spread(value, ones):
    high, middle, low = split3(value)
    return dot(high, ones) + (dot(middle, ones) + dot(low, ones))


def gather_heads(value, ones):
    high, low = split2(value)
    return dot(high, ones, ((1,), (1,))) + dot(low, ones, ((1,), (1,)))


def head_ones():
    head = lax.broadcasted_iota(jnp.int32, (LANES, INNER), 0)
    column = lax.broadcasted_iota(jnp.int32, (LANES, INNER), 1)
    return ((column >= head * SP) & (column < (head + 1) * SP)).astype(BF)


def lower_ones():
    rows = lax.broadcasted_iota(jnp.int32, (BLOCK, BLOCK), 0)
    columns = lax.broadcasted_iota(jnp.int32, (BLOCK, BLOCK), 1)
    return rows >= columns


def cumulate(value, lower, over):
    high, middle, low = split3(value)
    return dot(lower, high, over) + (dot(lower, middle, over) + dot(lower, low, over))


def decays(aux, dt_bias, rate):
    raw = aux[:, 2 * STATE :] + dt_bias
    step = jnp.maximum(raw, 0.0) + jnp.log1p(jnp.exp(-jnp.abs(raw)))
    log_decay = -step * rate
    cumulated = cumulate(log_decay, lower_ones().astype(BF), ((1,), (0,)))
    return raw, step, log_decay, cumulated


def state_kernel(resets, mixed, aux, dt_bias, decay_log, state_out, state):
    number = pl.program_id(0)

    @pl.when((number == 0) | (resets[number] != 0))
    def _():
        state[...] = jnp.zeros_like(state)

    ones = head_ones()
    aux_now = aux[...]
    _, step, _, cumulated = decays(aux_now, dt_bias[...], jnp.exp(decay_log[...]))
    last = cumulated[BLOCK - 1 :, :]
    tail = spread(step * jnp.exp(last - cumulated), ones)
    carried = spread(jnp.exp(jnp.broadcast_to(last, (8, LANES))), ones)[:1]
    fresh = dot3(aux_now[:, :STATE], mixed[...] * tail, ((0,), (0,)))
    state[...] = carried * state[...] + fresh
    state_out[...] = state[...]


def forward_kernel(
    resets, mixed, gate, aux, dt_bias, decay_log, state_in, ssm_out, gated, states, state
):
    number = pl.program_id(0)

    @pl.when(number == 0)
    def _():
        state[...] = state_in[...]

    @pl.when(resets[number] != 0)
    def _():
        state[...] = jnp.zeros_like(state)

    ones = head_ones()
    aux_now = aux[...]
    b_in = aux_now[:, :STATE]
    c_out = aux_now[:, STATE : 2 * STATE]
    _, step, _, cumulated = decays(aux_now, dt_bias[...], jnp.exp(decay_log[...]))
    last = cumulated[BLOCK - 1 :, :]
    scaled = mixed[...] * spread(step, ones)
    tail = spread(jnp.exp(last - cumulated), ones)
    grown = spread(jnp.exp(cumulated), ones)
    before = state[...]
    states[...] = before[None]
    state[...] = grown[BLOCK - 1 :, :] * before + dot3(b_in, scaled * tail, ((0,), (0,)))
    outer = grown * dot3(c_out, before)
    both = dot3(c_out, b_in, ((1,), (1,)))
    lower = lower_ones()
    flipped = cumulated.T
    first_half = lax.broadcasted_iota(jnp.int32, (BLOCK, LANES), 1) < SP
    scaled_high, scaled_low = split2(scaled)
    zero = jnp.zeros((BLOCK, LANES), BF)
    for pair in range(SH // 2):
        weights = []
        for head in (2 * pair, 2 * pair + 1):
            spread_now = cumulated[:, head : head + 1] - flipped[head : head + 1, :]
            weights.append(jnp.exp(jnp.where(lower, spread_now, NEGATIVE)) * both)
        weight_high, weight_low = split2(jnp.concatenate(weights, axis=1))
        columns = slice(pair * LANES, (pair + 1) * LANES)
        high = scaled_high[:, columns]
        low = scaled_low[:, columns]
        high = jnp.concatenate([jnp.where(first_half, high, zero), jnp.where(first_half, zero, high)])
        low = jnp.concatenate([jnp.where(first_half, low, zero), jnp.where(first_half, zero, low)])
        inner = dot(weight_high, high) + (dot(weight_high, low) + dot(weight_low, high))
        total = inner + outer[:, columns]
        ssm_out[:, columns] = total
        gate_now = gate[:, columns]
        gated[:, columns] = (total * (gate_now / (1.0 + jnp.exp(-gate_now)))).astype(BF)


def silu_of(gate):
    chance = 1.0 / (1.0 + jnp.exp(-gate))
    return gate * chance, chance


def state_back_kernel(
    resets, d_gated, gate, aux, ssm_out, dt_bias, decay_log, d_state_out, d_gate, d_state
):
    number = pl.num_programs(0) - 1 - pl.program_id(0)

    @pl.when(pl.program_id(0) == 0)
    def _():
        d_state[...] = jnp.zeros_like(d_state)

    ones = head_ones()
    aux_now = aux[...]
    _, _, _, cumulated = decays(aux_now, dt_bias[...], jnp.exp(decay_log[...]))
    grown = spread(jnp.exp(cumulated), ones)
    gate_silu, chance = silu_of(gate[...])
    d_gated_now = d_gated[...]
    d_gate[...] = (d_gated_now * ssm_out[...] * (chance + gate_silu * (1.0 - chance))).astype(BF)
    d_grown = d_gated_now * gate_silu * grown
    c_out = aux_now[:, STATE : 2 * STATE]
    d_state[...] = grown[BLOCK - 1 :, :] * d_state[...] + dot3(c_out, d_grown, ((0,), (0,)))

    @pl.when(resets[number] != 0)
    def _():
        d_state[...] = jnp.zeros_like(d_state)

    d_state_out[...] = d_state[...].astype(BF)


def backward_kernel(
    resets,
    d_gated,
    mixed,
    gate,
    aux,
    ssm_out,
    states,
    dt_bias,
    decay_log,
    d_state_in,
    d_mixed,
    d_aux,
    d_heads,
    d_state,
):
    number = pl.num_programs(0) - 1 - pl.program_id(0)

    @pl.when(pl.program_id(0) == 0)
    def _():
        d_state[...] = d_state_in[...].astype(F32)
        d_heads[...] = jnp.zeros_like(d_heads)

    ones = head_ones()
    lower = lower_ones()
    aux_now = aux[...]
    b_in = aux_now[:, :STATE]
    c_out = aux_now[:, STATE : 2 * STATE]
    rate = jnp.exp(decay_log[...])
    raw, step, log_decay, cumulated = decays(aux_now, dt_bias[...], rate)
    last = cumulated[BLOCK - 1 :, :]
    step_wide = spread(step, ones)
    mixed_now = mixed[...]
    scaled = mixed_now * step_wide
    tail = spread(jnp.exp(last - cumulated), ones)
    grown = spread(jnp.exp(cumulated), ones)
    gate_now = gate[...]
    gate_silu, _ = silu_of(gate_now)
    d_gated_now = d_gated[...]
    ssm_now = ssm_out[...]
    d_out = d_gated_now * gate_silu
    before = states[0]
    d_after = d_state[...]
    d_grown = d_out * grown
    d_c = dot3(d_grown, before, ((1,), (1,)))
    d_before = grown[BLOCK - 1 :, :] * d_after + dot3(c_out, d_grown, ((0,), (0,)))
    tailed = scaled * tail
    d_b = dot3(tailed, d_after, ((1,), (1,)))
    d_tailed = dot3(b_in, d_after)
    ends = jnp.sum(tailed * d_tailed, axis=0, keepdims=True) + grown[BLOCK - 1 :, :] * jnp.sum(
        d_after * before, axis=0, keepdims=True
    )
    d_last = gather_heads(jnp.broadcast_to(ends, (8, INNER)), ones)[:1]
    both = dot3(c_out, b_in, ((1,), (1,)))
    flipped = cumulated.T
    first_half = lax.broadcasted_iota(jnp.int32, (BLOCK, LANES), 1) < SP
    scaled_high, scaled_low = split2(scaled)
    d_high, d_low = split2(d_out)
    zero = jnp.zeros((BLOCK, LANES), BF)
    d_both = jnp.zeros((BLOCK, BLOCK), F32)
    parts = []
    for pair in range(SH // 2):
        columns = slice(pair * LANES, (pair + 1) * LANES)
        falls = []
        for head in (2 * pair, 2 * pair + 1):
            spread_now = cumulated[:, head : head + 1] - flipped[head : head + 1, :]
            falls.append(jnp.exp(jnp.where(lower, spread_now, NEGATIVE)))
        weight_high, weight_low = split2(jnp.concatenate([falls[0] * both, falls[1] * both]))
        high = d_high[:, columns]
        low = d_low[:, columns]
        high = jnp.concatenate([jnp.where(first_half, high, zero), jnp.where(first_half, zero, high)])
        low = jnp.concatenate([jnp.where(first_half, low, zero), jnp.where(first_half, zero, low)])
        flat = ((1,), (1,))
        d_weight = dot(high, scaled_high[:, columns], flat) + (
            dot(high, scaled_low[:, columns], flat) + dot(low, scaled_high[:, columns], flat)
        )
        d_both = d_both + falls[0] * d_weight[:BLOCK] + falls[1] * d_weight[BLOCK:]
        down = ((0,), (0,))
        parts.append(
            dot(weight_high, high, down) + (dot(weight_high, low, down) + dot(weight_low, high, down))
        )
    d_scaled = jnp.concatenate(parts, axis=1) + tail * d_tailed
    d_mixed[...] = (d_scaled * step_wide).astype(BF)
    d_step = gather_heads(d_scaled * mixed_now, ones)
    d_cumulated = gather_heads(d_out * ssm_now, ones) - step * d_step
    d_decay = cumulate(d_cumulated, lower.astype(BF), ((0,), (0,))) + d_last
    d_raw = (d_step - d_decay * rate) * (1.0 / (1.0 + jnp.exp(-raw)))
    real = lax.broadcasted_iota(jnp.int32, (BLOCK, LANES), 1) < SH
    d_raw = jnp.where(real, d_raw, 0.0)
    d_c = d_c + dot3(d_both, b_in)
    d_b = d_b + dot3(d_both, c_out, ((0,), (0,)))
    d_aux[...] = jnp.concatenate([d_b, d_c, d_raw], axis=1).astype(BF)
    d_heads[...] += jnp.concatenate(
        [
            jnp.sum(d_raw, axis=0, keepdims=True),
            jnp.sum(jnp.where(real, d_decay * log_decay, 0.0), axis=0, keepdims=True),
            jnp.zeros((6, LANES), F32),
        ]
    )
    d_state[...] = d_before

    @pl.when(resets[number] != 0)
    def _():
        d_state[...] = jnp.zeros_like(d_state)


def scalars():
    return pl.BlockSpec(memory_space=pltpu.SMEM)


def whole(shape):
    return pl.BlockSpec(shape, lambda number: (0,) * len(shape))


def params_of():
    return pltpu.CompilerParams(
        dimension_semantics=("arbitrary",), vmem_limit_bytes=VMEM_LIMIT
    )


def run_state(resets, mixed, aux, dt_bias, decay_log):
    count = mixed.shape[0] // BLOCK
    return pl.pallas_call(
        state_kernel,
        grid=(count,),
        in_specs=[
            scalars(),
            pl.BlockSpec((BLOCK, INNER), lambda number: (number, 0)),
            pl.BlockSpec((BLOCK, 3 * LANES), lambda number: (number, 0)),
            whole((1, LANES)),
            whole((1, LANES)),
        ],
        out_specs=whole((STATE, INNER)),
        out_shape=jax.ShapeDtypeStruct((STATE, INNER), F32),
        scratch_shapes=[pltpu.VMEM((STATE, INNER), F32)],
        compiler_params=params_of(),
        cost_estimate=pl.CostEstimate(flops=count * 400_000_000, bytes_accessed=6_000_000, transcendentals=0),
        name="ssm_state",
    )(resets, mixed, aux, dt_bias, decay_log)


def run_forward(resets, mixed, aux, dt_bias, decay_log, state_in):
    rows = mixed.shape[0]
    count = rows // BLOCK
    return pl.pallas_call(
        forward_kernel,
        grid=(count,),
        in_specs=[
            scalars(),
            pl.BlockSpec((BLOCK, INNER), lambda number: (number, 0)),
            pl.BlockSpec((BLOCK, INNER), lambda number: (number, 1)),
            pl.BlockSpec((BLOCK, 3 * LANES), lambda number: (number, 0)),
            whole((1, LANES)),
            whole((1, LANES)),
            whole((STATE, INNER)),
        ],
        out_specs=[
            pl.BlockSpec((BLOCK, INNER), lambda number: (number, 0)),
            pl.BlockSpec((BLOCK, INNER), lambda number: (number, 0)),
            pl.BlockSpec((1, STATE, INNER), lambda number: (number, 0, 0)),
        ],
        out_shape=[
            jax.ShapeDtypeStruct((rows, INNER), F32),
            jax.ShapeDtypeStruct((rows, INNER), BF),
            jax.ShapeDtypeStruct((count, STATE, INNER), F32),
        ],
        scratch_shapes=[pltpu.VMEM((STATE, INNER), F32)],
        compiler_params=params_of(),
        cost_estimate=pl.CostEstimate(flops=count * 3_000_000_000, bytes_accessed=20_000_000, transcendentals=0),
        name="ssm_forward",
    )(resets, mixed, mixed, aux, dt_bias, decay_log, state_in)


def run_state_back(resets, d_gated, mixed, aux, ssm_out, dt_bias, decay_log):
    count = mixed.shape[0] // BLOCK
    turned = lambda number: (count - 1 - number, 0)
    return pl.pallas_call(
        state_back_kernel,
        grid=(count,),
        in_specs=[
            scalars(),
            pl.BlockSpec((BLOCK, INNER), turned),
            pl.BlockSpec((BLOCK, INNER), lambda number: (count - 1 - number, 1)),
            pl.BlockSpec((BLOCK, 3 * LANES), turned),
            pl.BlockSpec((BLOCK, INNER), turned),
            whole((1, LANES)),
            whole((1, LANES)),
        ],
        out_specs=[whole((STATE, INNER)), pl.BlockSpec((BLOCK, INNER), turned)],
        out_shape=[
            jax.ShapeDtypeStruct((STATE, INNER), BF),
            jax.ShapeDtypeStruct((mixed.shape[0], INNER), BF),
        ],
        scratch_shapes=[pltpu.VMEM((STATE, INNER), F32)],
        compiler_params=params_of(),
        cost_estimate=pl.CostEstimate(flops=count * 400_000_000, bytes_accessed=8_000_000, transcendentals=0),
        name="ssm_state_back",
    )(resets, d_gated, mixed, aux, ssm_out, dt_bias, decay_log)


def run_backward(resets, d_gated, mixed, aux, ssm_out, states, dt_bias, decay_log, d_state_in):
    rows = mixed.shape[0]
    count = rows // BLOCK
    turned = lambda number: (count - 1 - number, 0)
    return pl.pallas_call(
        backward_kernel,
        grid=(count,),
        in_specs=[
            scalars(),
            pl.BlockSpec((BLOCK, INNER), turned),
            pl.BlockSpec((BLOCK, INNER), turned),
            pl.BlockSpec((BLOCK, INNER), lambda number: (count - 1 - number, 1)),
            pl.BlockSpec((BLOCK, 3 * LANES), turned),
            pl.BlockSpec((BLOCK, INNER), turned),
            pl.BlockSpec((1, STATE, INNER), lambda number: (count - 1 - number, 0, 0)),
            whole((1, LANES)),
            whole((1, LANES)),
            whole((STATE, INNER)),
        ],
        out_specs=[
            pl.BlockSpec((BLOCK, INNER), turned),
            pl.BlockSpec((BLOCK, 3 * LANES), turned),
            whole((8, LANES)),
        ],
        out_shape=[
            jax.ShapeDtypeStruct((rows, INNER), BF),
            jax.ShapeDtypeStruct((rows, 3 * LANES), BF),
            jax.ShapeDtypeStruct((8, LANES), F32),
        ],
        scratch_shapes=[pltpu.VMEM((STATE, INNER), F32)],
        compiler_params=params_of(),
        cost_estimate=pl.CostEstimate(flops=count * 6_000_000_000, bytes_accessed=24_000_000, transcendentals=0),
        name="ssm_backward",
    )(resets, d_gated, mixed, mixed, aux, ssm_out, states, dt_bias, decay_log, d_state_in)


def head_rows(ref, start, group, width):
    return jnp.concatenate(
        [
            ref[start : start + BLOCK, (group * width + head) * HD : (group * width + head + 1) * HD]
            for head in range(width)
        ]
    )


def masked_scores(q_rows, k_rows, bias_row, lower, width):
    raw = dot(q_rows, k_rows, ((1,), (1,))) + bias_row
    edge = raw.shape[1] - BLOCK
    corner = jnp.where(jnp.concatenate([lower] * width), raw[:, edge:], NEGATIVE)
    return jnp.concatenate([raw[:, :edge], corner], axis=1)


def attend_kernel(q_ref, prior_ref, here_ref, bias_ref, out_ref, total_ref):
    width = QH // KVH
    rows = q_ref.shape[0]
    halo = prior_ref.shape[0]
    lower = lower_ones()
    for group in range(KVH):
        key_columns = slice(group * HD, (group + 1) * HD)
        value_columns = slice((KVH + group) * HD, (KVH + group + 1) * HD)
        keys = jnp.concatenate([prior_ref[:, key_columns], here_ref[:, key_columns]])
        values = jnp.concatenate([prior_ref[:, value_columns], here_ref[:, value_columns]])
        for block in range(rows // BLOCK):
            start = block * BLOCK
            reach = halo + start + BLOCK
            q_rows = head_rows(q_ref, start, group, width)
            scores = masked_scores(
                q_rows, keys[:reach], bias_ref[block : block + 1, :reach], lower, width
            )
            top = jnp.max(scores, axis=1, keepdims=True)
            powers = jnp.exp(scores - top)
            total = jnp.sum(powers, axis=1, keepdims=True)
            probs = (powers * (1.0 / total)).astype(BF)
            out = dot(probs, values[:reach])
            log_total = top + jnp.log(total)
            for head in range(width):
                place = group * width + head
                some = slice(head * BLOCK, (head + 1) * BLOCK)
                out_ref[start : start + BLOCK, place * HD : (place + 1) * HD] = out[some].astype(BF)
                total_ref[start : start + BLOCK, place : place + 1] = log_total[some]


def attend_back_kernel(
    q_ref, prior_ref, here_ref, bias_ref, total_ref, d_ref, dq_ref, d_prior_ref, d_here_ref, sums
):
    width = QH // KVH
    rows = q_ref.shape[0]
    halo = prior_ref.shape[0]
    lower = lower_ones()
    sums[...] = jnp.zeros_like(sums)
    for group in range(KVH):
        key_columns = slice(group * HD, (group + 1) * HD)
        value_columns = slice((KVH + group) * HD, (KVH + group + 1) * HD)
        keys = jnp.concatenate([prior_ref[:, key_columns], here_ref[:, key_columns]])
        values = jnp.concatenate([prior_ref[:, value_columns], here_ref[:, value_columns]])
        for block in range(rows // BLOCK):
            start = block * BLOCK
            reach = halo + start + BLOCK
            q_rows = head_rows(q_ref, start, group, width)
            d_rows = head_rows(d_ref, start, group, width)
            scores = masked_scores(
                q_rows, keys[:reach], bias_ref[block : block + 1, :reach], lower, width
            )
            log_total = jnp.concatenate(
                [
                    total_ref[start : start + BLOCK, group * width + head : group * width + head + 1]
                    for head in range(width)
                ]
            )
            probs = jnp.exp(scores - log_total)
            probs_low = probs.astype(BF)
            d_probs = dot(d_rows, values[:reach], ((1,), (1,)))
            weighed = probs * d_probs
            d_scores = (weighed - probs * jnp.sum(weighed, axis=1, keepdims=True)).astype(BF)
            d_queries = dot(d_scores, keys[:reach]) * HD**-0.5
            for head in range(width):
                place = group * width + head
                some = slice(head * BLOCK, (head + 1) * BLOCK)
                dq_ref[start : start + BLOCK, place * HD : (place + 1) * HD] = d_queries[some].astype(BF)
            sums[:reach, key_columns] += dot(d_scores, q_rows, ((0,), (0,)))
            sums[:reach, value_columns] += dot(probs_low, d_rows, ((0,), (0,)))
    d_prior_ref[...] = sums[:halo].astype(BF)
    d_here_ref[...] = sums[halo:]


def run_attend(queries, prior, here, bias):
    rows = queries.shape[0]
    return pl.pallas_call(
        attend_kernel,
        out_shape=[
            jax.ShapeDtypeStruct((rows, QH * HD), BF),
            jax.ShapeDtypeStruct((rows, QH), F32),
        ],
        compiler_params=pltpu.CompilerParams(vmem_limit_bytes=VMEM_LIMIT),
        cost_estimate=pl.CostEstimate(flops=6_000_000_000, bytes_accessed=2_000_000, transcendentals=4_000_000),
        name="attend",
    )(queries, prior, here, bias)


def run_attend_back(queries, prior, here, bias, log_total, d_attended):
    rows = queries.shape[0]
    halo = prior.shape[0]
    return pl.pallas_call(
        attend_back_kernel,
        out_shape=[
            jax.ShapeDtypeStruct((rows, QH * HD), BF),
            jax.ShapeDtypeStruct((halo, 2 * KVH * HD), BF),
            jax.ShapeDtypeStruct((rows, 2 * KVH * HD), F32),
        ],
        scratch_shapes=[pltpu.VMEM((halo + rows, 2 * KVH * HD), F32)],
        compiler_params=pltpu.CompilerParams(vmem_limit_bytes=VMEM_LIMIT),
        cost_estimate=pl.CostEstimate(flops=12_000_000_000, bytes_accessed=4_000_000, transcendentals=4_000_000),
        name="attend_back",
    )(queries, prior, here, bias, log_total, d_attended)


def swap(value):
    return lax.ppermute(value, "shard", SWAP)


def natural(mine, theirs, position, axis):
    return jnp.where(
        position == 0,
        jnp.concatenate([mine, theirs], axis=axis),
        jnp.concatenate([theirs, mine], axis=axis),
    )


def half_of(value, which, axis):
    size = value.shape[axis] // 2
    return lax.dynamic_slice_in_dim(value, which * size, size, axis)


class Stream:
    def __init__(self, terms):
        self.terms = terms
        self.count = lax.axis_size("rep")
        self.pairs = self.count % 4 == 0
        self.far = self.count // 4 if self.pairs else self.count
        rep = lax.axis_index("rep")
        core = lax.axis_index("shard")
        near = rep % 4 if self.pairs else 0
        self.far_at = rep // 4 if self.pairs else rep
        fast, slow = near % 2, near // 2
        self.bits = (jnp.where(core == 0, fast, slow), jnp.where(core == 0, slow, fast))
        around = [0, 1] if self.pairs else []
        self.steps = [("scatter", phase) for phase in around]
        if self.far > 1:
            self.steps += [("scatter", 2), ("gather", 2)]
        self.steps += [("gather", phase) for phase in reversed(around)]
        self.stack = None
        self.got = None
        self.operands = []

    def pair_list(self, phase):
        flips = (1, 2) if phase == 0 else (2, 1)
        return [
            (rep * 2 + core, (rep ^ flips[core]) * 2 + core)
            for rep in range(self.count)
            for core in range(2)
        ]

    def far_list(self, shift):
        near = 4 if self.pairs else 1
        return [
            (rep * 2 + core, ((rep + shift * near) % self.count) * 2 + core)
            for rep in range(self.count)
            for core in range(2)
        ]

    def part(self, start, size):
        total = lax.dynamic_slice_in_dim(self.terms[0], start, size, 0).astype(F32)
        for term in self.terms[1:]:
            total = total + lax.dynamic_slice_in_dim(term, start, size, 0).astype(F32)
        return total.astype(BF)

    def prepare(self):
        if not self.steps:
            self.operands = []
            return
        kind, phase = self.steps[0]
        if kind == "gather":
            if self.stack is None:
                self.stack = self.part(0, self.terms[0].shape[0])
            elif self.got is not None:
                self.stack = jnp.concatenate([self.stack, *self.got])
            self.operands = [self.stack]
        elif phase < 2:
            size = self.terms[0].shape[0] // 2
            self.operands = [self.part((1 - self.bits[phase]) * size, size)]
        else:
            size = self.terms[0].shape[0] // self.far
            self.operands = [
                self.part((self.far_at + shift) % self.far * size, size) for shift in range(1, self.far)
            ]

    def go(self):
        if not self.steps:
            return
        kind, phase = self.steps.pop(0)
        if phase < 2:
            lists = [self.pair_list(phase)]
        else:
            lists = [self.far_list(shift) for shift in range(1, self.far)]
        operands = self.operands * len(lists) if kind == "gather" else self.operands
        self.got = [
            lax.ppermute(operand, ("rep", "shard"), pairs) for operand, pairs in zip(operands, lists)
        ]
        if kind == "scatter":
            parts, at = (2, self.bits[phase]) if phase < 2 else (self.far, self.far_at)
            size = self.terms[0].shape[0] // parts
            self.terms = [
                lax.dynamic_slice_in_dim(term, at * size, size, 0) for term in self.terms
            ] + self.got
            self.got = None

    def places(self):
        at = (self.far_at - jnp.arange(self.far, dtype=jnp.int32)) % self.far
        for phase in (1, 0) if self.pairs else ():
            span = self.far * (1 if phase == 1 else 2)
            own = self.bits[phase]
            at = jnp.concatenate([own * span + at, (1 - own) * span + at])
        return at.astype(jnp.int32)

    def finish(self, outputs, started=None):
        if self.stack is None:
            self.stack = self.part(0, self.terms[0].shape[0])
        stacks = [self.stack, *(self.got or [])]
        places = self.places()
        blocks = places.shape[0]
        each = blocks // len(stacks)
        size = stacks[0].shape[0] // each
        width = stacks[0].shape[1]
        if size % 16:
            flat = jnp.concatenate(stacks).reshape(blocks, size, width)
            flat = jnp.zeros_like(flat).at[places].set(flat).reshape(blocks * size, width)
            made = []
            for shape, _, pieces in outputs:
                cuts = [flat[:, begin:end].astype(F32) for _, begin, end in pieces]
                whole_width = shape.shape[-1]
                if len(shape.shape) == 3:
                    value = jnp.stack(cuts)
                    value = jnp.pad(value, ((0, 0), (0, 0), (whole_width - value.shape[-1], 0)))
                else:
                    value = jnp.concatenate(cuts, axis=1)
                made.append(value)
            if started is not None:
                made[-1] = jnp.concatenate([made[-1], started[:, made[-1].shape[1] :]], axis=1)
            return made
        in_specs = [
            pl.BlockSpec((size, width), lambda step, places: (jnp.minimum(step, each - 1), 0))
        ]
        if len(stacks) == 2:
            in_specs.append(
                pl.BlockSpec((size, width), lambda step, places: (jnp.maximum(step - each, 0), 0))
            )
        out_specs = []
        for shape, block, _ in outputs:
            if len(shape.shape) == 3:
                last = shape.shape[2] // block[0] - 1
                out_specs.append(
                    pl.BlockSpec(
                        (shape.shape[0], size, block[0]),
                        lambda step, places, last=last: (0, places[step], last),
                    )
                )
            else:
                out_specs.append(
                    pl.BlockSpec((size, block[0]), lambda step, places: (places[step], 0))
                )
        aliases = {}
        inputs = list(stacks)
        if started is not None:
            aliases = {1 + len(inputs): len(outputs) - 1}
            inputs.append(started)
            in_specs.append(pl.BlockSpec(memory_space=pl.ANY))
        return pl.pallas_call(
            functools.partial(finish_kernel, len(stacks), [pieces for _, _, pieces in outputs]),
            grid_spec=pltpu.PrefetchScalarGridSpec(
                num_scalar_prefetch=1, grid=(blocks,), in_specs=in_specs, out_specs=out_specs
            ),
            out_shape=[shape for shape, _, _ in outputs],
            input_output_aliases=aliases,
            compiler_params=params_of(),
            name="unpack",
        )(places, *inputs)


def finish_kernel(count, layout, places, *refs):
    del places
    outputs = refs[-len(layout) :]
    steps = pl.num_programs(0)

    def write(ref):
        for out, pieces in zip(outputs, layout):
            for target, begin, end in pieces:
                value = ref[:, begin:end].astype(F32)
                if len(out.shape) == 3:
                    out[target] = value
                else:
                    out[:, target : target + end - begin] = value

    if count == 1:
        write(refs[0])
        return

    @pl.when(pl.program_id(0) < steps // 2)
    def _():
        write(refs[0])

    @pl.when(pl.program_id(0) >= steps // 2)
    def _():
        write(refs[1])


def after(value, *others):
    return lax.optimization_barrier((value, *others))[0]


def columns_of(ref, which, size):
    return ref[:, pl.ds(pl.multiple_of(which * size, size), size)]


def inverse_rms(values):
    return lax.rsqrt(jnp.mean(values * values, axis=-1, keepdims=True) + EPSILON)


def norm_back(values, inverse, gain, grad):
    scaled = grad * gain
    shared = jnp.mean(scaled * values, axis=-1, keepdims=True) * (inverse * inverse)
    return (
        inverse * (scaled - values * shared),
        jnp.sum(grad * (values * inverse), axis=0, keepdims=True),
    )


def project_kernel(
    position,
    tokens,
    gains,
    small_mine,
    small_theirs,
    ssm_mine,
    ssm_theirs,
    normed,
    queries,
    key_vals,
    aux,
    mixed,
):
    here = position[0]
    half = tokens.shape[1] // 2

    def product(mine, theirs, begin=0, end=None):
        return dot(columns_of(normed, here, half), mine[:, begin:end]) + dot(
            columns_of(normed, 1 - here, half), theirs[:, begin:end]
        )

    @pl.when(pl.program_id(0) == 0)
    def _():
        hidden = tokens[...].astype(F32)
        normed[...] = (hidden * inverse_rms(hidden) * gains[0:1]).astype(BF)
        low = product(small_mine, small_theirs, 0, AUX_AT)
        queries[...] = low[:, :KV_AT].astype(BF) * jnp.asarray(HD**-0.5, BF)
        key_vals[...] = low[:, KV_AT:].astype(BF)
        aux[...] = product(small_mine, small_theirs, AUX_AT)

    mixed[...] = product(ssm_mine, ssm_theirs)


CHUNK = 512


def run_project(position, tokens, gains, small, ssm):
    rows, width = tokens.shape
    half = width // 2
    inner = ssm[0].shape[1]
    aux_width = small[0].shape[1] - AUX_AT
    fixed = lambda shape: pl.BlockSpec(shape, lambda step, place: (0,) * len(shape))
    sliding = pl.BlockSpec((half, CHUNK), lambda step, place: (0, step))
    weights = [fixed(small[0].shape)] * 2
    return pl.pallas_call(
        project_kernel,
        grid_spec=pltpu.PrefetchScalarGridSpec(
            num_scalar_prefetch=1,
            grid=(inner // CHUNK,),
            in_specs=[fixed(tokens.shape), fixed(gains.shape), *weights, sliding, sliding],
            out_specs=[
                fixed((rows, width)),
                fixed((rows, KV_AT)),
                fixed((rows, AUX_AT - KV_AT)),
                fixed((rows, aux_width)),
                pl.BlockSpec((rows, CHUNK), lambda step, place: (0, step)),
            ],
        ),
        out_shape=[
            jax.ShapeDtypeStruct((rows, width), BF),
            jax.ShapeDtypeStruct((rows, KV_AT), BF),
            jax.ShapeDtypeStruct((rows, AUX_AT - KV_AT), BF),
            jax.ShapeDtypeStruct((rows, aux_width), F32),
            jax.ShapeDtypeStruct((rows, inner), F32),
        ],
        compiler_params=params_of(),
        cost_estimate=pl.CostEstimate(flops=6_000_000_000, bytes_accessed=20_000_000, transcendentals=0),
        name="project",
    )(position, tokens, gains, *small, *ssm)


def project_back_kernel(
    position,
    tokens,
    gains,
    d_middle,
    d_query,
    d_kv,
    d_aux,
    d_mixed,
    d_gate,
    small_mine,
    small_theirs,
    ssm_mine,
    ssm_theirs,
    grad_tokens,
    grad_gain,
    d_normed,
):
    here = position[0]
    step = pl.program_id(0)
    count = pl.num_programs(0)
    half = tokens.shape[1] // 2
    flat = ((1,), (1,))

    def place(which):
        return pl.ds(pl.multiple_of(which * half, half), half)

    @pl.when(step == 0)
    def _():
        for which, small in ((here, small_mine), (1 - here, small_theirs)):
            d_normed[:, place(which)] = (
                dot(d_query[...], small[:, :KV_AT], flat)
                + dot(d_kv[...], small[:, KV_AT:AUX_AT], flat)
                + dot(d_aux[...], small[:, AUX_AT:], flat)
            )

    d_now = jnp.where(step < count // 2, d_mixed[...], d_gate[...])
    d_normed[:, place(here)] += dot(d_now, ssm_mine[...], flat)
    d_normed[:, place(1 - here)] += dot(d_now, ssm_theirs[...], flat)

    @pl.when(step == count - 1)
    def _():
        hidden = tokens[...].astype(F32)
        d_hidden, d_gain = norm_back(hidden, inverse_rms(hidden), gains[0:1], d_normed[...])
        grad_tokens[...] = d_middle[...] + d_hidden
        grad_gain[...] = jnp.broadcast_to(d_gain, grad_gain.shape)


def run_project_back(
    position, tokens, gains, d_middle, d_query, d_kv, d_aux, d_mixed, d_gate, small, ssm
):
    rows, width = tokens.shape
    half = width // 2
    count = ssm[0].shape[1] // CHUNK
    fixed = lambda array: pl.BlockSpec(array.shape, lambda step, place: (0,) * len(array.shape))
    sliding = pl.BlockSpec((half, CHUNK), lambda step, place: (0, step))
    weights = small
    return pl.pallas_call(
        project_back_kernel,
        grid_spec=pltpu.PrefetchScalarGridSpec(
            num_scalar_prefetch=1,
            grid=(count,),
            in_specs=[
                *[fixed(item) for item in (tokens, gains, d_middle, d_query, d_kv, d_aux)],
                pl.BlockSpec(
                    (rows, CHUNK), lambda step, place: (0, jnp.minimum(step, count // 2 - 1))
                ),
                pl.BlockSpec(
                    (rows, CHUNK), lambda step, place: (0, jnp.maximum(step - count // 2, 0))
                ),
                *[fixed(item) for item in weights],
                sliding,
                sliding,
            ],
            out_specs=[
                pl.BlockSpec((rows, width), lambda step, place: (0, 0)),
                pl.BlockSpec((8, width), lambda step, place: (0, 0)),
            ],
            scratch_shapes=[pltpu.VMEM((rows, width), F32)],
        ),
        out_shape=[
            jax.ShapeDtypeStruct((rows, width), F32),
            jax.ShapeDtypeStruct((8, width), F32),
        ],
        compiler_params=params_of(),
        cost_estimate=pl.CostEstimate(flops=6_000_000_000, bytes_accessed=20_000_000, transcendentals=0),
        name="project_back",
    )(position, tokens, gains, d_middle, d_query, d_kv, d_aux, d_mixed, d_gate, *weights, *ssm)


def middle_kernel(
    position,
    tokens,
    attended,
    gated,
    cotangent,
    gains,
    attn_mine,
    attn_theirs,
    ssm_mine,
    ssm_theirs,
    gate,
    up,
    down,
    output,
    d_middle,
    d_attn_branch,
    d_ssm_branch,
    d_attended,
    d_gated,
    gain_grads,
    grad_down_theirs,
    grad_down_mine,
    grad_wide_theirs,
    grad_wide_mine,
    attn_branch,
    ssm_branch,
    middle,
    normed,
    flipped,
    out_sum,
    d_normed,
):
    here = position[0]
    step = pl.program_id(0)
    count = pl.num_programs(0)
    width = tokens.shape[1]
    half = width // 2
    attn_half = attended.shape[1] // 2
    ssm_half = gated.shape[1] // 2
    flat = ((1,), (1,))

    def place(which, size):
        return pl.ds(pl.multiple_of(which * size, size), size)

    @pl.when(step == 0)
    def _():
        attn = dot(columns_of(attended, here, attn_half), attn_mine[...]) + dot(
            columns_of(attended, 1 - here, attn_half), attn_theirs[...]
        )
        attn_branch[...] = attn
        ssm = dot(columns_of(gated, here, ssm_half), ssm_mine[...]) + dot(
            columns_of(gated, 1 - here, ssm_half), ssm_theirs[...]
        )
        ssm_branch[...] = ssm
        joined = tokens[...].astype(F32) + 0.5 * (
            attn * inverse_rms(attn) * gains[1:2] + ssm * inverse_rms(ssm) * gains[2:3]
        )
        middle[...] = joined
        out_sum[...] = joined
        scaled = joined * inverse_rms(joined) * gains[3:4]
        normed[...] = scaled.astype(BF)
        flipped[...] = scaled.T.astype(BF)
        d_normed[...] = jnp.zeros_like(d_normed)

    gate_val = dot(normed[...], gate[...])
    up_val = dot(normed[...], up[...])
    gate_silu, chance = silu_of(gate_val)
    activated = (gate_silu * up_val).astype(BF)
    d_activated = dot(cotangent[...], down[...], flat)
    out_sum[...] += dot(activated, down[...])
    d_up = (d_activated * gate_silu).astype(BF)
    d_gate = (d_activated * up_val * (chance + gate_silu * (1.0 - chance))).astype(BF)
    d_normed[...] += dot(d_gate, gate[...], flat) + dot(d_up, up[...], flat)
    grad_down = dot(activated, cotangent[...], ((0,), (0,))).astype(BF)
    first = step < count // 2

    @pl.when(first)
    def _():
        grad_down_theirs[...] = grad_down

    @pl.when(jnp.logical_not(first))
    def _():
        grad_down_mine[...] = grad_down

    for which, ref in ((here, grad_wide_mine), (1 - here, grad_wide_theirs)):
        turned = flipped[place(which, half), :]
        ref[:, :CHUNK] = dot(turned, d_gate).astype(BF)
        ref[:, CHUNK:] = dot(turned, d_up).astype(BF)

    @pl.when(step == count - 1)
    def _():
        output[...] = out_sum[...].astype(BF)
        joined = middle[...]
        d_joined, d_gain_ff = norm_back(joined, inverse_rms(joined), gains[3:4], d_normed[...])
        d_joined = cotangent[...].astype(F32) + d_joined
        d_middle[...] = d_joined
        attn = attn_branch[...]
        d_attn, d_gain_attn = norm_back(attn, inverse_rms(attn), gains[1:2], 0.5 * d_joined)
        d_attn_low = d_attn.astype(BF)
        d_attn_branch[...] = d_attn_low
        ssm = ssm_branch[...]
        d_ssm, d_gain_ssm = norm_back(ssm, inverse_rms(ssm), gains[2:3], 0.5 * d_joined)
        d_ssm_low = d_ssm.astype(BF)
        d_ssm_branch[...] = d_ssm_low
        gain_grads[...] = jnp.concatenate(
            [d_gain_attn, d_gain_ssm, d_gain_ff, jnp.zeros((5, width), F32)]
        )
        for which, attn_weight, ssm_weight in (
            (here, attn_mine, ssm_mine),
            (1 - here, attn_theirs, ssm_theirs),
        ):
            d_attended[:, place(which, attn_half)] = dot(d_attn_low, attn_weight[...], flat).astype(BF)
            d_gated[:, place(which, ssm_half)] = dot(d_ssm_low, ssm_weight[...], flat)


def run_middle(position, tokens, attended, gated, cotangent, gains, attn, ssm, gate, up, down):
    rows, width = tokens.shape
    half = width // 2
    hidden = gate.shape[1]
    count = hidden // CHUNK
    fixed = lambda shape: pl.BlockSpec(shape, lambda step, place: (0,) * len(shape))

    def chunk(step, place):
        first = step < count // 2
        return jnp.where(first, 1 - place[0], place[0]) * (count // 2) + step % (count // 2)

    sliding = pl.BlockSpec((width, CHUNK), lambda step, place: (0, chunk(step, place)))
    early = lambda step, place: (jnp.minimum(step, count // 2 - 1), 0)
    late = lambda step, place: (jnp.maximum(step - count // 2, 0), 0)
    wide = pl.BlockSpec((half, 2 * CHUNK), lambda step, place: (0, chunk(step, place)))
    low = lambda shape: jax.ShapeDtypeStruct(shape, BF)
    full = lambda shape: jax.ShapeDtypeStruct(shape, F32)
    return pl.pallas_call(
        middle_kernel,
        grid_spec=pltpu.PrefetchScalarGridSpec(
            num_scalar_prefetch=1,
            grid=(count,),
            in_specs=[
                *[fixed(item.shape) for item in (tokens, attended, gated, cotangent, gains)],
                *[fixed(item.shape) for item in (*attn, *ssm)],
                *[sliding] * 2,
                pl.BlockSpec((CHUNK, width), lambda step, place: (chunk(step, place), 0)),
            ],
            out_specs=[
                *[fixed((rows, width))] * 4,
                fixed(attended.shape),
                fixed(gated.shape),
                fixed((8, width)),
                pl.BlockSpec((CHUNK, width), early),
                pl.BlockSpec((CHUNK, width), late),
                wide,
                wide,
            ],
            scratch_shapes=[
                *[pltpu.VMEM((rows, width), F32)] * 3,
                pltpu.VMEM((rows, width), BF),
                pltpu.VMEM((width, rows), BF),
                *[pltpu.VMEM((rows, width), F32)] * 2,
            ],
        ),
        out_shape=[
            low((rows, width)),
            full((rows, width)),
            low((rows, width)),
            low((rows, width)),
            low(attended.shape),
            full(gated.shape),
            full((8, width)),
            low((hidden // 2, width)),
            low((hidden // 2, width)),
            low((half, 2 * hidden)),
            low((half, 2 * hidden)),
        ],
        compiler_params=params_of(),
        cost_estimate=pl.CostEstimate(flops=30_000_000_000, bytes_accessed=40_000_000, transcendentals=0),
        name="middle",
    )(position, tokens, attended, gated, cotangent, gains, *attn, *ssm, gate, up, down)


def local(
    tokens,
    cotangent,
    doc_blocks,
    gain_in,
    w_query,
    w_kv,
    w_attn_out,
    gain_attn,
    w_ssm_in,
    w_ssm_aux,
    dt_bias,
    decay_log,
    w_ssm_out,
    gain_ssm,
    gain_ff,
    w_gate,
    w_up,
    w_down,
):
    rows, width = tokens.shape
    half = width // 2
    position = lax.axis_index("shard")
    here = position.astype(jnp.int32).reshape(1)
    blocks_here = rows // BLOCK
    docs = doc_blocks[0]
    here_docs = lax.dynamic_slice_in_dim(docs, position * blocks_here, blocks_here, 0)
    prior_docs = jnp.where(position > 0, docs[:blocks_here], -1)
    earlier = jnp.concatenate([prior_docs[-1:], here_docs[:-1]])
    resets = (here_docs != earlier).astype(jnp.int32)
    key_docs = jnp.repeat(jnp.concatenate([prior_docs, here_docs]), BLOCK)
    bias = jnp.where(here_docs[:, None] == key_docs[None, :], 0.0, NEGATIVE)
    lane_pad = LANES - SH
    dt_row = jnp.pad(dt_bias, (0, lane_pad))[None]
    decay_row = jnp.pad(decay_log, (0, lane_pad))[None]

    gains = jnp.stack([gain_in, gain_attn, gain_ssm, gain_ff])
    gains_theirs = swap(gains)
    small = jnp.concatenate([w_query, w_kv, jnp.pad(w_ssm_aux, ((0, 0), (0, lane_pad)))], axis=1)
    ssm_in = (w_ssm_in, swap(w_ssm_in))
    small = (small, swap(small))
    attn_out = (w_attn_out, swap(w_attn_out))
    ssm_back = (w_ssm_out, swap(w_ssm_out))
    gate = lax.all_gather(w_gate, "shard", axis=0, tiled=True)
    up = lax.all_gather(w_up, "shard", axis=0, tiled=True)
    down = lax.all_gather(w_down, "shard", axis=0, tiled=True)
    gains_all = jnp.pad(natural(gains, gains_theirs, position, 1).astype(F32), ((0, 4), (0, 0)))

    normed, scaled_queries, key_vals, aux, mixed = run_project(
        here, tokens, gains_all, small, ssm_in
    )
    key_prior = lax.ppermute(key_vals, "shard", [(0, 1)])
    state_end = run_state(resets, mixed, aux, dt_row, decay_row)
    state_prior = lax.ppermute(state_end, "shard", [(0, 1)])
    attended, log_total = run_attend(scaled_queries, key_prior, key_vals, bias)
    ssm_out, gated, states = run_forward(resets, mixed, aux, dt_row, decay_row, state_prior)

    (
        output,
        d_middle,
        d_attn_low,
        d_ssm_low,
        d_attended,
        d_gated,
        gain_grads,
        down_theirs,
        down_mine,
        wide_theirs,
        wide_mine,
    ) = run_middle(
        here, tokens, attended, gated, cotangent, gains_all, attn_out, ssm_back, gate, up, down
    )
    down_got = swap(down_theirs)
    wide_got = swap(wide_theirs)

    wide = Stream([wide_mine, wide_got])
    d_state_start, d_mixed_gate = run_state_back(
        resets, d_gated, mixed, aux, ssm_out, dt_row, decay_row
    )
    d_state_end = lax.ppermute(d_state_start, "shard", [(1, 0)])
    outs_rows = w_attn_out.shape[0]

    def grads_of(left, right):
        return (
            dot(half_of(left, 1 - position, 1), right, ((0,), (0,))).astype(BF),
            dot(half_of(left, position, 1), right, ((0,), (0,))).astype(BF),
        )

    def beside(*arrays):
        return jnp.concatenate(
            [
                array[start : start + outs_rows]
                for array in arrays
                for start in range(0, array.shape[0], outs_rows)
            ],
            axis=1,
        )

    outs_theirs, outs_mine = zip(
        grads_of(attended, d_attn_low), grads_of(gated, d_ssm_low), grads_of(normed, d_mixed_gate)
    )
    outs_mine = beside(*outs_mine)
    outs_got = swap(beside(*outs_theirs))
    down_sum = (down_mine.astype(F32) + down_got.astype(F32)).astype(BF)
    grad_down = lax.psum(down_sum, "rep")
    wide.prepare()
    d_mixed, d_aux, d_heads = run_backward(
        resets,
        after(d_gated, down_sum, *wide.operands),
        mixed,
        aux,
        ssm_out,
        states,
        dt_row,
        decay_row,
        d_state_end,
    )
    wide.go()
    outs = Stream([outs_mine, outs_got])
    outs.prepare()
    wide.prepare()
    d_query, d_prior, d_here = run_attend_back(
        scaled_queries,
        key_prior,
        key_vals,
        bias,
        log_total,
        after(d_attended, d_aux, *outs.operands, *wide.operands),
    )
    wide.go()
    outs.go()
    d_kv = (d_here + lax.ppermute(d_prior, "shard", [(1, 0)]).astype(F32)).astype(BF)

    d_rest = jnp.concatenate([d_query, d_kv, d_mixed, d_aux], axis=1)
    rest_theirs, rest_mine = grads_of(normed, d_rest)
    wide.prepare()
    outs.prepare()
    grad_tokens, gain_in_grads = run_project_back(
        here,
        tokens,
        gains_all,
        d_middle,
        d_query,
        d_kv,
        d_aux,
        d_mixed,
        after(d_mixed_gate, rest_theirs, *wide.operands, *outs.operands),
        small,
        ssm_in,
    )
    wide.go()
    outs.go()
    head_column = jnp.pad(d_heads[:2, :SH].reshape(2 * SH), (0, half - 2 * SH))[:, None]
    spare = AUX_AT + INNER + 2 * STATE + SH

    def with_extra(array, which):
        extra = half_of(jnp.concatenate([gain_in_grads[:1], gain_grads[:3]]), which, 1).T
        extra = jnp.concatenate([extra, head_column], axis=1).astype(BF)
        extra = jnp.pad(extra, ((0, 0), (0, lane_pad - extra.shape[1])))
        return jnp.concatenate([array[:, :spare], extra], axis=1)

    rest = Stream([with_extra(rest_mine, position), swap(with_extra(rest_theirs, 1 - position))])
    rest.prepare()
    rest.go()
    for stream in (wide, outs):
        stream.prepare()
        stream.go()
    rest.prepare()
    rest.go()
    for stream in (wide, outs):
        stream.prepare()
        stream.go()
    rest.prepare()
    rest.go()
    for stream in (wide, outs):
        stream.prepare()
        stream.go()
    for stream in (wide, outs, rest):
        while stream.steps:
            stream.prepare()
            stream.go()

    full = lambda *shape: jax.ShapeDtypeStruct(shape, F32)
    pieces = [
        [
            (column, 2 * column + offset, 2 * column + offset + CHUNK)
            for column in range(0, w_gate.shape[1], CHUNK)
        ]
        for offset in (0, CHUNK)
    ]
    grad_gate, grad_up = wide.finish(
        [
            (full(half, w_gate.shape[1]), (w_gate.shape[1],), pieces[0]),
            (full(half, w_gate.shape[1]), (w_gate.shape[1],), pieces[1]),
        ]
    )
    ssm_pieces = w_ssm_out.shape[0] // outs_rows
    gate_at = width * (1 + ssm_pieces)
    grad_attn_out, grad_ssm_out, grad_ssm_in = outs.finish(
        [
            (full(outs_rows, width), (width,), [(0, 0, width)]),
            (
                full(ssm_pieces, outs_rows, width),
                (width,),
                [(piece, width * (1 + piece), width * (2 + piece)) for piece in range(ssm_pieces)],
            ),
            (
                full(half // outs_rows, outs_rows, 2 * INNER),
                (INNER,),
                [
                    (piece, gate_at + INNER * piece, gate_at + INNER * (piece + 1))
                    for piece in range(half // outs_rows)
                ],
            ),
        ]
    )
    aux_at = AUX_AT + INNER
    grad_query, grad_kv, grad_aux, extras, grad_ssm_in = rest.finish(
        [
            (full(half, KV_AT), (KV_AT,), [(0, 0, KV_AT)]),
            (full(half, AUX_AT - KV_AT), (AUX_AT - KV_AT,), [(0, KV_AT, AUX_AT)]),
            (full(half, spare - aux_at), (spare - aux_at,), [(0, aux_at, spare)]),
            (full(half, LANES), (LANES,), [(0, aux_at + 2 * STATE, aux_at + 3 * LANES)]),
            (full(half, 2 * INNER), (INNER,), [(0, AUX_AT, aux_at)]),
        ],
        grad_ssm_in.reshape(half, 2 * INNER),
    )
    return (
        output,
        grad_tokens,
        extras[:, SH],
        grad_query,
        grad_kv,
        grad_attn_out,
        extras[:, SH + 1],
        grad_ssm_in,
        grad_aux,
        extras[:SH, SH + 4],
        extras[SH : 2 * SH, SH + 4],
        grad_ssm_out.reshape(w_ssm_out.shape),
        extras[:, SH + 2],
        extras[:, SH + 3],
        grad_gate,
        grad_up,
        grad_down.astype(F32),
    )


def solution(mesh):
    halves = P("shard", None)
    half = P("shard")
    tokens = P(("rep", "shard"), None)
    return jax.shard_map(
        local,
        mesh=mesh,
        in_specs=(
            tokens,
            tokens,
            P("rep", None),
            half,
            halves,
            halves,
            halves,
            half,
            halves,
            halves,
            P(),
            P(),
            halves,
            half,
            half,
            halves,
            halves,
            halves,
        ),
        out_specs=(
            tokens,
            tokens,
            half,
            halves,
            halves,
            halves,
            half,
            halves,
            halves,
            P(),
            P(),
            halves,
            half,
            half,
            halves,
            halves,
            halves,
        ),
        check_vma=False,
    )
```

time: 1740 us -> 530 us (0.30)
  blocking collectives: 1100 us -> 0 us
  matrix products: 287 us -> 17.8 us
  Pallas kernels: 0 us -> 184 us
  local copies, waits for them, and re-layouts: 213 us -> 36 us
  waiting for transfers between devices: 3.95 us -> 168 us
  other arithmetic: 86.2 us -> 41.9 us
  starting transfers between devices: 21.7 us -> 57.3 us
    psum x2 -> x0, blocking collectives: 1080 us -> none  [the longest x1 1040 us: local(): lax.psum((shares[0], shares[1], shares[2], shares[3], shares[4], shares[5...]
    dot_general x98 -> x8, matrix products: 287 us -> 17.8 us  [dot(): lax.dot_general(left, right, (over, ((), ())), preferred_element_type=F32)]
    pallas_call x0 -> x12, Pallas kernels: none -> 184 us  [the longest x1 41 us: run_middle(): pl.pallas_call(middle_kernel, grid_spec=pltpu.PrefetchScalarGridSpec(num_...]
    ppermute x4 -> x43, waiting for transfers between devices: 0.01 us -> 167 us  [the longest x30 162 us: go(): lax.ppermute(operand, ('rep', 'shard'), pairs)]
    dynamic_update_slice x8 -> x0, local copies, waits for them, and re-layouts: 83.1 us -> none  [scan_blocks(): lax.scan(jax.checkpoint(block_step), state_in, (scaled.reshape(count, BLO...]
    ppermute x4 -> x43, starting transfers between devices: 20.9 us -> 57.1 us  [the longest x30 46.8 us: go(): lax.ppermute(operand, ('rep', 'shard'), pairs)]
    reshape x10 -> x1, local copies, waits for them, and re-layouts: 33.5 us -> 0.09 us  [local(): d_heads[:2, :SH].reshape(2 * SH)]
    squeeze x24 -> x0, local copies, waits for them, and re-layouts: 21.1 us -> none  [the longest x20 21 us: scan_blocks(): lax.scan(jax.checkpoint(block_step), state_in, (scaled.reshape(count, BLO...]
  transfers between devices with their start and end apart: 20 -> 47, of which waited for: 0 -> 17; matrix products, arithmetic and copies ran while one was open for 27% -> 14% of each run, Pallas kernels for 0% -> 24%
where the time goes in v1:
time: 530 us; the launch traced here: 520 us
  Pallas kernels  184 us (35%)
  waiting for transfers between devices  168 us (32%)
  starting transfers between devices  57.3 us (11%)
  other arithmetic  41.9 us (8%)
  local copies, waits for them, and re-layouts  36 us (7%)
  matrix products  17.8 us (3%)
  between operations  14.6 us (3%)
    ppermute x30, waiting for transfers between devices, go(): lax.ppermute(operand, ('rep', 'shard'), pairs)  162 us
    ppermute x30, starting transfers between devices, go(): lax.ppermute(operand, ('rep', 'shard'), pairs)  46.8 us
    pallas_call x1, Pallas kernels, run_middle(): pl.pallas_call(middle_kernel, grid_spec=pltpu.PrefetchScalarGridSpec(num_...  41 us
    pallas_call x3, Pallas kernels, finish(): pl.pallas_call(functools.partial(finish_kernel, len(stacks), [pieces for...  34.3 us
    pallas_call x1, Pallas kernels, run_backward(): pl.pallas_call(backward_kernel, grid=(count,), in_specs=[scalars(), pl.Bl...  26 us
    unnamed x91, local copies, waits for them, and re-layouts  21.2 us
    convert_element_type x9, other arithmetic, part(): return total.astype(BF)  20.5 us
    dot_general x8, matrix products, dot(): lax.dot_general(left, right, (over, ((), ())), preferred_element_type=F32)  17.8 us
  transfers between devices with their start and end apart: 47, of which 17 were waited for; matrix products, arithmetic and copies ran while one was open for 14% of the time, Pallas kernels for 24%

profile of v1, /device:TPU:1, one launch (start us, length us, event | category | flops | bytes accessed | tf_op | source)
XLA Modules:
  0.0 519.9 jit_solution(6601012555326497465)
XLA Ops:
  14.9 3.6 collective-permute-done.1.small_theirs
  18.5 12.6 %project.1 = (bf16[512,1024]{1,0:T(8,128)(2,1)}, bf16[512,512]{1,0:T(8,128)(2,1)}, bf16[512,256]{1,0:T(8,128)(2,1)}, f32[512,384]{1,0:T(8,128)}, f32[512,3072]{1,0:T(8,128)}) custom-call(s32[1]{0:T(128)} %bitcast.position, bf16[512,1024]{1,0:T(8,128)(2,1)} %tokens.5, f32[8,1024]{1,0:T(8,128)} %pad_convert_fusion.gains, bf16[512,1152]{1,0:T(8,128)(2,1)} %copy-done.5, ...), custom_call_target="tpu_custom_call" | custom-call | flops 6000000000 | bytes 20000000 | tf_op jit(solution)/shard_map/project/pallas_call | solution.py:809
  32.3 7.2 %ssm_state.1 = f32[128,1536]{1,0:T(8,128)} custom-call(s32[4]{0:T(128)} %compare_convert_fusion.resets, f32[512,3072]{1,0:T(8,128)} %get-tuple-element.64.mixed.gate, f32[512,384]{1,0:T(8,128)} %get-tuple-element.65.aux, f32[1,128]{1,0:T(1,128)} %get-tuple-element.186.dt_bias, f32[1,128]{1,0:T(1,128)} %get-tuple-element.185.decay_log), custom_call_target="tpu_custom_call" | custom-call | flops 1600000000 | bytes 6000000 | tf_op jit(solution)/shard_map/ssm_state/pallas_call | solution.py:310
  42.4 9.6 %attend.1 = (bf16[512,512]{1,0:T(8,128)(2,1)}, f32[512,8]{1,0:T(8,128)}) custom-call(bf16[512,512]{1,0:T(8,128)(2,1)} %get-tuple-element.61.q_ref, bf16[512,256]{1,0:T(8,128)(2,1)} %copy-done.26, bf16[512,256]{1,0:T(8,128)(2,1)} %get-tuple-element.62.here_ref, f32[4,1024]{1,0:T(4,128)} %compare_select_fusion.bias_ref), custom_call_target="tpu_custom_call" | custom-call | flops 6000000000 | bytes 2000000 | tf_op jit(solution)/shard_map/attend/pallas_call | solution.py:515
  52.8 15.1 %ssm_forward.1 = (f32[512,1536]{1,0:T(8,128)}, bf16[512,1536]{1,0:T(8,128)(2,1)}, f32[4,128,1536]{2,1,0:T(8,128)}) custom-call(s32[4]{0:T(128)} %compare_convert_fusion.resets, f32[512,3072]{1,0:T(8,128)} %get-tuple-element.64.mixed.gate, f32[512,3072]{1,0:T(8,128)} %get-tuple-element.64.mixed.gate, f32[512,384]{1,0:T(8,128)} %get-tuple-element.65.aux, ...), custom_call_target="tpu_custom_call" | custom-call | flops 12000000000 | bytes 20000000 | tf_op jit(solution)/shard_map/ssm_forward/pallas_call | solution.py:332
  68.7 41.0 %middle.1 = (bf16[512,1024]{1,0:T(8,128)(2,1)}, f32[512,1024]{1,0:T(8,128)}, bf16[512,1024]{1,0:T(8,128)(2,1)}, bf16[512,1024]{1,0:T(8,128)(2,1)}, bf16[512,512]...) custom-call(s32[1]{0:T(128)} %bitcast.position, ...), custom_call_target="tpu_custom_call" | custom-call | flops 30000001024 | bytes 40000000 | tf_op jit(solution)/shard_map/middle/pallas_call | solution.py:1059
  117.1 8.9 %ssm_state_back.1 = (bf16[128,1536]{1,0:T(8,128)(2,1)}, bf16[512,1536]{1,0:T(8,128)(2,1)}) custom-call(s32[4]{0:T(128)} %compare_convert_fusion.resets, f32[512,1536]{1,0:T(8,128)} %get-tuple-element.76.d_gated, f32[512,3072]{1,0:T(8,128)} %get-tuple-element.64.mixed.gate, f32[512,384]{1,0:T(8,128)} %get-tuple-element.65.aux, ...), custom_call_target="tpu_custom_call" | custom-call | flops 1600000000 | bytes 8000000 | tf_op jit(solution)/shard_map/ssm_state_back/pallas_call | solution.py:364
  146.6 3.9 add_convert_fusion.2
  150.5 2.9 collective-permute-start.14
  153.4 3.7 add_convert_fusion
  157.9 26.0 %ssm_backward.1 = (bf16[512,1536]{1,0:T(8,128)(2,1)}, bf16[512,384]{1,0:T(8,128)(2,1)}, f32[8,128]{1,0:T(8,128)}) custom-call(s32[4]{0:T(128)} %compare_convert_fusion.resets, f32[512,1536]{1,0:T(8,128)} %get-tuple-element.76.d_gated, f32[512,3072]{1,0:T(8,128)} %get-tuple-element.64.mixed.gate, f32[512,3072]{1,0:T(8,128)} %get-tuple-element.64.mixed.gate, ...), custom_call_target="tpu_custom_call" | custom-call | flops 24000000000 | bytes 24000000 | tf_op jit(solution)/shard_map/ssm_backward/pallas_call | solution.py:392
  188.5 27.8 %collective-permute-done.11 = bf16[256,4096]{1,0:T(8,128)(2,1)S(1)} collective-permute-done((bf16[256,4096]{1,0:T(8,128)(2,1)}, bf16[256,4096]{1,0:T(8,128)(2,1)S(1)}, u32[]{:S(2)}, u32[]{:S(2)}) %collective-permute-start.11) | collective-permute-done | bytes 2097184 | tf_op jit(solution)/shard_map/ppermute | solution.py:634
  216.3 3.0 add_convert_fusion.4
  220.8 16.1 %attend_back.1 = (bf16[512,512]{1,0:T(8,128)(2,1)}, bf16[512,256]{1,0:T(8,128)(2,1)}, f32[512,256]{1,0:T(8,128)}) custom-call(bf16[512,512]{1,0:T(8,128)(2,1)} %get-tuple-element.61.q_ref, bf16[512,256]{1,0:T(8,128)(2,1)} %copy-done.26, bf16[512,256]{1,0:T(8,128)(2,1)} %get-tuple-element.62.here_ref, f32[4,1024]{1,0:T(4,128)} %compare_select_fusion.bias_ref, ...), custom_call_target="tpu_custom_call" | custom-call | flops 12000000000 | bytes 4000000 | tf_op jit(solution)/shard_map/attend_back/pallas_call | solution.py:530
  241.9 3.1 collective-permute-start.29
  248.2 3.8 collective-permute-done.29
  251.9 17.1 %collective-permute-done.28 = bf16[16,7168]{1,0:T(8,128)(2,1)S(1)} collective-permute-done((bf16[16,7168]{1,0:T(8,128)(2,1)S(1)}, bf16[16,7168]{1,0:T(8,128)(2,1)S(1)}, u32[]{:S(2)}, u32[]{:S(2)}) %collective-permute-start.28) | collective-permute-done | bytes 229408 | tf_op jit(solution)/shard_map/ppermute | solution.py:634
  276.4 3.2 fusion.10
  279.8 20.3 %collective-permute-done.31 = bf16[16,7168]{1,0:T(8,128)(2,1)S(1)} collective-permute-done((bf16[16,7168]{1,0:T(8,128)(2,1)S(1)}, bf16[16,7168]{1,0:T(8,128)(2,1)S(1)}, u32[]{:S(2)}, u32[]{:S(2)}) %collective-permute-start.31) | collective-permute-done | bytes 229408 | tf_op jit(solution)/shard_map/ppermute | solution.py:634
  302.4 3.7 add_convert_fusion.8
  306.1 13.4 %project_back.1 = (f32[512,1024]{1,0:T(8,128)}, f32[8,1024]{1,0:T(8,128)}) custom-call(s32[1]{0:T(128)} %bitcast.position, bf16[512,1024]{1,0:T(8,128)(2,1)} %tokens.5, f32[8,1024]{1,0:T(8,128)} %pad_convert_fusion.gains, f32[512,1024]{1,0:T(8,128)} %get-tuple-element.68.d_middle, bf16[512,512]{1,0:T(8,128)(2,1)} %get-tuple-element.86.d_query, ...), custom_call_target="tpu_custom_call" | custom-call | flops 6000000000 | bytes 20000000 | tf_op jit(solution)/shard_map/project_back/pallas_call | solution.py:893
  326.2 11.9 %collective-permute-start.37 = (bf16[32,4096]{1,0:T(8,128)(2,1)}, bf16[32,4096]{1,0:T(8,128)(2,1)S(1)}, u32[]{:S(2)}, u32[]{:S(2)}) collective-permute-start(bf16[32,4096]{1,0:T(8,128)(2,1)} %get-tuple-element.168), channel_id=1, source_target_pairs={{0,24},{1,25},{2,26},{3,27},{4,28},{5,29},{6,30},{7,31},{8,0},{9,1... | collective-permute-start | bytes 786440 | tf_op jit(solution)/shard_map/ppermute | solution.py:634
  344.4 17.7 %collective-permute-done.36 = bf16[32,4096]{1,0:T(8,128)(2,1)S(1)} collective-permute-done((bf16[32,4096]{1,0:T(8,128)(2,1)}, bf16[32,4096]{1,0:T(8,128)(2,1)S(1)}, u32[]{:S(2)}, u32[]{:S(2)}) %collective-permute-start.36) | collective-permute-done | bytes 262176 | tf_op jit(solution)/shard_map/ppermute | solution.py:634
  372.9 11.1 %collective-permute-done.39 = bf16[32,4096]{1,0:T(8,128)(2,1)S(1)} collective-permute-done((bf16[32,4096]{1,0:T(8,128)(2,1)S(1)}, bf16[32,4096]{1,0:T(8,128)(2,1)S(1)}, u32[]{:S(2)}, u32[]{:S(2)}) %collective-permute-start.39) | collective-permute-done | bytes 262176 | tf_op jit(solution)/shard_map/ppermute | solution.py:634
  387.6 25.6 %collective-permute-done.17 = bf16[128,2688]{1,0:T(8,128)(2,1)S(1)} collective-permute-done((bf16[128,2688]{1,0:T(8,128)(2,1)S(1)}, bf16[128,2688]{1,0:T(8,128)(2,1)S(1)}, u32[]{:S(2)}, u32[]{:S(2)}) %collective-permute-start.17) | collective-permute-done | bytes 688160 | tf_op jit(solution)/shard_map/ppermute | solution.py:634
  419.2 12.1 %collective-permute-done.19 = bf16[32,2688]{1,0:T(8,128)(2,1)S(1)} collective-permute-done((bf16[32,2688]{1,0:T(8,128)(2,1)S(1)}, bf16[32,2688]{1,0:T(8,128)(2,1)S(1)}, u32[]{:S(2)}, u32[]{:S(2)}) %collective-permute-start.19) | collective-permute-done | bytes 172064 | tf_op jit(solution)/shard_map/ppermute | solution.py:634
  439.3 6.6 %collective-permute-done.22 = bf16[32,2688]{1,0:T(8,128)(2,1)S(1)} collective-permute-done((bf16[32,2688]{1,0:T(8,128)(2,1)S(1)}, bf16[32,2688]{1,0:T(8,128)(2,1)S(1)}, u32[]{:S(2)}, u32[]{:S(2)}) %collective-permute-start.22) | collective-permute-done | bytes 172064 | tf_op jit(solution)/shard_map/ppermute | solution.py:634
  448.5 15.0 %collective-permute-done.24 = bf16[128,2688]{1,0:T(8,128)(2,1)S(1)} collective-permute-done((bf16[128,2688]{1,0:T(8,128)(2,1)S(1)}, bf16[128,2688]{1,0:T(8,128)(2,1)S(1)}, u32[]{:S(2)}, u32[]{:S(2)}) %collective-permute-start.24) | collective-permute-done | bytes 688160 | tf_op jit(solution)/shard_map/ppermute | solution.py:634
  466.1 4.1 convert_element_type.434
  470.1 11.6 %unpack.3 = (f32[256,1024]{1,0:T(8,128)}, f32[3,256,1024]{2,1,0:T(8,128)}, f32[2,256,3072]{2,1,0:T(8,128)}) custom-call(s32[16]{0:T(128)} %pad_add_fusion.2.places, bf16[128,7168]{1,0:T(8,128)(2,1)} %constant_dynamic-update-slice_fusion.5.refs_0_, bf16[128,7168]{1,0:T(8,128)(2,1)} %collective-permute-done.34.refs_1_), custom_call_target="tpu_custom_call" | custom-call | tf_op jit(solution)/shard_map/unpack/pallas_call | solution.py:704
  483.1 11.6 %unpack.5 = (f32[512,2048]{1,0:T(8,128)}, f32[512,2048]{1,0:T(8,128)}) custom-call(s32[16]{0:T(128)} %pad_add_fusion.2.places, bf16[256,4096]{1,0:T(8,128)(2,1)} %constant_dynamic-update-slice_fusion.10.refs_0_, bf16[256,4096]{1,0:T(8,128)(2,1)} %copy-done.3), custom_call_target="tpu_custom_call" | custom-call | tf_op jit(solution)/shard_map/unpack/pallas_call | solution.py:704
  495.8 11.1 %unpack.4 = (f32[512,512]{1,0:T(8,128)}, f32[512,256]{1,0:T(8,128)}, f32[512,280]{1,0:T(8,128)}, f32[512,128]{1,0:T(8,128)}, f32[512,3072]{1,0:T(8,128)}) custom-call(s32[16]{0:T(128)} %pad_add_fusion.2.places, bf16[256,2688]{1,0:T(8,128)(2,1)} %constant_dynamic-update-slice_fusion.refs_0_, ...), custom_call_target="tpu_custom_call", output_to_operand_aliasing={{4}: (3, {})} | custom-call | tf_op jit(solution)/shard_map/unpack/pallas_call | solution.py:704
  (234 shorter events, 120.8 us)
Async XLA Ops:
  7.2 60.7 %all-gather.4.cloned.1.call-start = ((), (), s32[]{:S(2)}) async-start(), calls=%async_computation | async-start | bytes 6291456 | tf_op jit(solution)/shard_map/all_gather | solution.py:1149
  8.0 60.0 %all-gather.6.cloned.1.call-start = ((), (), s32[]{:S(2)}) async-start(), calls=%async_computation.1 | async-start | bytes 6291456 | tf_op jit(solution)/shard_map/all_gather | solution.py:1150
  8.7 59.3 %all-gather.8.cloned.1.call-start = ((), (), s32[]{:S(2)}) async-start(), calls=%async_computation.2 | async-start | bytes 6291456 | tf_op jit(solution)/shard_map/all_gather | solution.py:1151
  9.6 456.5 %all-reduce.9.cloned.1.call-start = ((), (), s32[]{:S(2)}) async-start(), calls=%async_computation.3 | async-start | bytes 4194304 | tf_op jit(solution)/shard_map/psum | solution.py:1210
  10.1 57.8 %collective-permute-start.5 = (bf16[256,1024]{1,0:T(8,128)(2,1)S(1)}, bf16[256,1024]{1,0:T(8,128)(2,1)S(1)}, u32[]{:S(2)}, u32[]{:S(2)}) collective-permute-start(bf16[256,1024]{1,0:T(8,128)(2,1)S(1)} %copy-done.22), channel_id=1, source_target_pairs={{0,1},{1,0},{2,3},{3,2},{4,5},{5,4},{6,7},{7,6},{8,9},{9,8},{10,11... | collective-permute-start | bytes 1572872 | tf_op jit(solution)/shard_map/ppermute | solution.py:545
  10.6 57.4 %collective-permute-start.6 = (bf16[768,1024]{1,0:T(8,128)(2,1)}, bf16[768,1024]{1,0:T(8,128)(2,1)}, u32[]{:S(2)}, u32[]{:S(2)}) collective-permute-start(bf16[768,1024]{1,0:T(8,128)(2,1)} %ssm_mine.4), channel_id=1, source_target_pairs={{0,1},{1,0},{2,3},{3,2},{4,5},{5,4},{6,7},{7,6},{8,9},{9,8},{10,11... | collective-permute-start | bytes 4718600 | tf_op jit(solution)/shard_map/ppermute | solution.py:545
  130.4 16.2 %collective-permute-start.10 = (bf16[256,7168]{1,0:T(8,128)(2,1)}, bf16[256,7168]{1,0:T(8,128)(2,1)}, u32[]{:S(2)}, u32[]{:S(2)}) collective-permute-start(bf16[256,7168]{1,0:T(8,128)(2,1)} %slice_dynamic-update-slice_fusion), channel_id=1, source_target_pairs={{0,1},{1,0},{2,3},{3,2},{4,5},{5,4},{6,7},{7,6},{8,9},{9,8},{10,11... | collective-permute-start | bytes 11010056 | tf_op jit(solution)/shard_map/ppermute | solution.py:545
  131.5 21.9 %collective-permute-start.8 = (bf16[512,4096]{1,0:T(8,128)(2,1)}, bf16[512,4096]{1,0:T(8,128)(2,1)}, u32[]{:S(2)}, u32[]{:S(2)}) collective-permute-start(bf16[512,4096]{1,0:T(8,128)(2,1)} %get-tuple-element.75), channel_id=1, source_target_pairs={{0,1},{1,0},{2,3},{3,2},{4,5},{5,4},{6,7},{7,6},{8,9},{9,8},{10,11... | collective-permute-start | bytes 12582920 | tf_op jit(solution)/shard_map/ppermute | solution.py:545
  132.0 25.1 %collective-permute-start.9 = (bf16[128,1536]{1,0:T(8,128)(2,1)S(1)}, bf16[128,1536]{1,0:T(8,128)(2,1)S(1)}, u32[]{:S(2)}, u32[]{:S(2)}) collective-permute-start(bf16[128,1536]{1,0:T(8,128)(2,1)S(1)} %copy-done.24), channel_id=1, source_target_pairs={{1,0},{3,2},{5,4},{7,6},{9,8},{11,10},{13,12},{15,14},{17,16},{19,... | collective-permute-start | bytes 1179656 | tf_op jit(solution)/shard_map/ppermute | solution.py:1185
  150.5 34.2 %collective-permute-start.14 = (bf16[128,7168]{1,0:T(8,128)(2,1)}, bf16[128,7168]{1,0:T(8,128)(2,1)}, u32[]{:S(2)}, u32[]{:S(2)}) collective-permute-start(bf16[128,7168]{1,0:T(8,128)(2,1)} %add_convert_fusion.2), channel_id=1, source_target_pairs={{0,2},{1,5},{2,0},{3,7},{4,6},{5,1},{6,4},{7,3},{8,10},{9,13},{10,... | collective-permute-start | bytes 5505032 | tf_op jit(solution)/shard_map/ppermute | solution.py:634
  157.1 59.3 %collective-permute-start.11 = (bf16[256,4096]{1,0:T(8,128)(2,1)}, bf16[256,4096]{1,0:T(8,128)(2,1)S(1)}, u32[]{:S(2)}, u32[]{:S(2)}) collective-permute-start(bf16[256,4096]{1,0:T(8,128)(2,1)} %add_convert_fusion), channel_id=1, source_target_pairs={{0,2},{1,5},{2,0},{3,7},{4,6},{5,1},{6,4},{7,3},{8,10},{9,13},{10,... | collective-permute-start | bytes 6291464 | tf_op jit(solution)/shard_map/ppermute | solution.py:634
  187.1 52.3 %collective-permute-start.26 = (bf16[64,7168]{1,0:T(8,128)(2,1)S(1)}, bf16[64,7168]{1,0:T(8,128)(2,1)S(1)}, u32[]{:S(2)}, u32[]{:S(2)}) collective-permute-start(bf16[64,7168]{1,0:T(8,128)(2,1)S(1)} %add_convert_fusion.5), channel_id=1, source_target_pairs={{0,4},{1,3},{2,6},{3,1},{4,0},{5,7},{6,2},{7,5},{8,12},{9,11},{10,... | collective-permute-start | bytes 2752520 | tf_op jit(solution)/shard_map/ppermute | solution.py:634
  219.3 83.0 %collective-permute-start.13 = (bf16[128,4096]{1,0:T(8,128)(2,1)S(1)}, bf16[128,4096]{1,0:T(8,128)(2,1)S(1)}, u32[]{:S(2)}, u32[]{:S(2)}) collective-permute-start(bf16[128,4096]{1,0:T(8,128)(2,1)S(1)} %add_convert_fusion.4), channel_id=1, source_target_pairs={{0,4},{1,3},{2,6},{3,1},{4,0},{5,7},{6,2},{7,5},{8,12},{9,11},{10,... | collective-permute-start | bytes 3145736 | tf_op jit(solution)/shard_map/ppermute | solution.py:634
  245.0 24.0 %collective-permute-start.28 = (bf16[16,7168]{1,0:T(8,128)(2,1)S(1)}, bf16[16,7168]{1,0:T(8,128)(2,1)S(1)}, u32[]{:S(2)}, u32[]{:S(2)}) collective-permute-start(bf16[16,7168]{1,0:T(8,128)(2,1)S(1)} %get-tuple-element.173), channel_id=1, source_target_pairs={{0,16},{1,17},{2,18},{3,19},{4,20},{5,21},{6,22},{7,23},{8,24},{9,... | collective-permute-start | bytes 688136 | tf_op jit(solution)/shard_map/ppermute | solution.py:634
  245.0 24.0 %collective-permute-start.27 = (bf16[16,7168]{1,0:T(8,128)(2,1)S(1)}, bf16[16,7168]{1,0:T(8,128)(2,1)S(1)}, u32[]{:S(2)}, u32[]{:S(2)}) collective-permute-start(bf16[16,7168]{1,0:T(8,128)(2,1)S(1)} %get-tuple-element.171), channel_id=1, source_target_pairs={{0,8},{1,9},{2,10},{3,11},{4,12},{5,13},{6,14},{7,15},{8,16},{9,17... | collective-permute-start | bytes 688136 | tf_op jit(solution)/shard_map/ppermute | solution.py:634
  272.1 28.0 %collective-permute-start.31 = (bf16[16,7168]{1,0:T(8,128)(2,1)S(1)}, bf16[16,7168]{1,0:T(8,128)(2,1)S(1)}, u32[]{:S(2)}, u32[]{:S(2)}) collective-permute-start(bf16[16,7168]{1,0:T(8,128)(2,1)S(1)} %get-tuple-element.165), channel_id=1, source_target_pairs={{0,16},{1,17},{2,18},{3,19},{4,20},{5,21},{6,22},{7,23},{8,24},{9,... | collective-permute-start | bytes 688136 | tf_op jit(solution)/shard_map/ppermute | solution.py:634
  274.0 26.1 %collective-permute-start.32 = (bf16[16,7168]{1,0:T(8,128)(2,1)S(1)}, bf16[16,7168]{1,0:T(8,128)(2,1)S(1)}, u32[]{:S(2)}, u32[]{:S(2)}) collective-permute-start(bf16[16,7168]{1,0:T(8,128)(2,1)S(1)} %get-tuple-element.165), channel_id=1, source_target_pairs={{0,24},{1,25},{2,26},{3,27},{4,28},{5,29},{6,30},{7,31},{8,0},{9,1... | collective-permute-start | bytes 688136 | tf_op jit(solution)/shard_map/ppermute | solution.py:634
  301.2 66.6 %collective-permute-start.33 = (bf16[64,7168]{1,0:T(8,128)(2,1)}, bf16[64,7168]{1,0:T(8,128)(2,1)}, u32[]{:S(2)}, u32[]{:S(2)}) collective-permute-start(bf16[64,7168]{1,0:T(8,128)(2,1)} %pad_maximum_fusion.2), channel_id=1, source_target_pairs={{0,4},{1,3},{2,6},{3,1},{4,0},{5,7},{6,2},{7,5},{8,12},{9,11},{10,... | collective-permute-start | bytes 2752520 | tf_op jit(solution)/shard_map/ppermute | solution.py:634
  323.9 17.7 %collective-permute-start.15 = (bf16[512,2688]{1,0:T(8,128)(2,1)}, bf16[512,2688]{1,0:T(8,128)(2,1)S(1)}, u32[]{:S(2)}, u32[]{:S(2)}) collective-permute-start(bf16[512,2688]{1,0:T(8,128)(2,1)} %fusion.3), channel_id=1, source_target_pairs={{0,1},{1,0},{2,3},{3,2},{4,5},{5,4},{6,7},{7,6},{8,9},{9,8},{10,11... | collective-permute-start | bytes 8257544 | tf_op jit(solution)/shard_map/ppermute | solution.py:545
  326.2 18.2 %collective-permute-start.37 = (bf16[32,4096]{1,0:T(8,128)(2,1)}, bf16[32,4096]{1,0:T(8,128)(2,1)S(1)}, u32[]{:S(2)}, u32[]{:S(2)}) collective-permute-start(bf16[32,4096]{1,0:T(8,128)(2,1)} %get-tuple-element.168), channel_id=1, source_target_pairs={{0,24},{1,25},{2,26},{3,27},{4,28},{5,29},{6,30},{7,31},{8,0},{9,1... | collective-permute-start | bytes 786440 | tf_op jit(solution)/shard_map/ppermute | solution.py:634
  338.0 24.1 %collective-permute-start.36 = (bf16[32,4096]{1,0:T(8,128)(2,1)}, bf16[32,4096]{1,0:T(8,128)(2,1)S(1)}, u32[]{:S(2)}, u32[]{:S(2)}) collective-permute-start(bf16[32,4096]{1,0:T(8,128)(2,1)} %get-tuple-element.169), channel_id=1, source_target_pairs={{0,16},{1,17},{2,18},{3,19},{4,20},{5,21},{6,22},{7,23},{8,24},{9,... | collective-permute-start | bytes 786440 | tf_op jit(solution)/shard_map/ppermute | solution.py:634
  339.1 23.0 %collective-permute-start.35 = (bf16[32,4096]{1,0:T(8,128)(2,1)}, bf16[32,4096]{1,0:T(8,128)(2,1)}, u32[]{:S(2)}, u32[]{:S(2)}) collective-permute-start(bf16[32,4096]{1,0:T(8,128)(2,1)} %get-tuple-element.170), channel_id=1, source_target_pairs={{0,8},{1,9},{2,10},{3,11},{4,12},{5,13},{6,14},{7,15},{8,16},{9,17... | collective-permute-start | bytes 786440 | tf_op jit(solution)/shard_map/ppermute | solution.py:634
  341.9 43.6 %collective-permute-start.16 = (bf16[256,2688]{1,0:T(8,128)(2,1)S(1)}, bf16[256,2688]{1,0:T(8,128)(2,1)S(1)}, u32[]{:S(2)}, u32[]{:S(2)}) collective-permute-start(bf16[256,2688]{1,0:T(8,128)(2,1)S(1)} %add_convert_fusion.3), channel_id=1, source_target_pairs={{0,2},{1,5},{2,0},{3,7},{4,6},{5,1},{6,4},{7,3},{8,10},{9,13},{10,... | collective-permute-start | bytes 4128776 | tf_op jit(solution)/shard_map/ppermute | solution.py:634
  364.5 19.4 %collective-permute-start.39 = (bf16[32,4096]{1,0:T(8,128)(2,1)S(1)}, bf16[32,4096]{1,0:T(8,128)(2,1)S(1)}, u32[]{:S(2)}, u32[]{:S(2)}) collective-permute-start(bf16[32,4096]{1,0:T(8,128)(2,1)S(1)} %get-tuple-element.163), channel_id=1, source_target_pairs={{0,16},{1,17},{2,18},{3,19},{4,20},{5,21},{6,22},{7,23},{8,24},{9,... | collective-permute-start | bytes 786440 | tf_op jit(solution)/shard_map/ppermute | solution.py:634
  365.2 18.8 %collective-permute-start.40 = (bf16[32,4096]{1,0:T(8,128)(2,1)S(1)}, bf16[32,4096]{1,0:T(8,128)(2,1)S(1)}, u32[]{:S(2)}, u32[]{:S(2)}) collective-permute-start(bf16[32,4096]{1,0:T(8,128)(2,1)S(1)} %get-tuple-element.163), channel_id=1, source_target_pairs={{0,24},{1,25},{2,26},{3,27},{4,28},{5,29},{6,30},{7,31},{8,0},{9,1... | collective-permute-start | bytes 786440 | tf_op jit(solution)/shard_map/ppermute | solution.py:634
  369.9 100.2 %collective-permute-start.34 = (bf16[128,7168]{1,0:T(8,128)(2,1)}, bf16[128,7168]{1,0:T(8,128)(2,1)}, u32[]{:S(2)}, u32[]{:S(2)}) collective-permute-start(bf16[128,7168]{1,0:T(8,128)(2,1)} %constant_dynamic-update-slice_fusion.5.refs_0_), channel_id=1, source_target_pairs={{0,2},{1,5},{2,0},{3,7},{4,6},{5,1},{6,4},{7,3},{8,10},{9,13},{10,... | collective-permute-start | bytes 5505032 | tf_op jit(solution)/shard_map/ppermute | solution.py:634
  384.0 51.9 %collective-permute-start.41 = (bf16[128,4096]{1,0:T(8,128)(2,1)S(1)}, bf16[128,4096]{1,0:T(8,128)(2,1)S(1)}, u32[]{:S(2)}, u32[]{:S(2)}) collective-permute-start(bf16[128,4096]{1,0:T(8,128)(2,1)S(1)} %pad_maximum_fusion.1), channel_id=1, source_target_pairs={{0,4},{1,3},{2,6},{3,1},{4,0},{5,7},{6,2},{7,5},{8,12},{9,11},{10,... | collective-permute-start | bytes 3145736 | tf_op jit(solution)/shard_map/ppermute | solution.py:634
  385.9 27.3 %collective-permute-start.17 = (bf16[128,2688]{1,0:T(8,128)(2,1)S(1)}, bf16[128,2688]{1,0:T(8,128)(2,1)S(1)}, u32[]{:S(2)}, u32[]{:S(2)}) collective-permute-start(bf16[128,2688]{1,0:T(8,128)(2,1)S(1)} %add_convert_fusion.6), channel_id=1, source_target_pairs={{0,4},{1,3},{2,6},{3,1},{4,0},{5,7},{6,2},{7,5},{8,12},{9,11},{10,... | collective-permute-start | bytes 2064392 | tf_op jit(solution)/shard_map/ppermute | solution.py:634
  414.4 16.9 %collective-permute-start.19 = (bf16[32,2688]{1,0:T(8,128)(2,1)S(1)}, bf16[32,2688]{1,0:T(8,128)(2,1)S(1)}, u32[]{:S(2)}, u32[]{:S(2)}) collective-permute-start(bf16[32,2688]{1,0:T(8,128)(2,1)S(1)} %get-tuple-element.176), channel_id=1, source_target_pairs={{0,16},{1,17},{2,18},{3,19},{4,20},{5,21},{6,22},{7,23},{8,24},{9,... | collective-permute-start | bytes 516104 | tf_op jit(solution)/shard_map/ppermute | solution.py:634
  437.0 44.7 %collective-permute-start.42 = (bf16[256,4096]{1,0:T(8,128)(2,1)}, bf16[256,4096]{1,0:T(8,128)(2,1)S(1)}, u32[]{:S(2)}, u32[]{:S(2)}) collective-permute-start(bf16[256,4096]{1,0:T(8,128)(2,1)} %constant_dynamic-update-slice_fusion.10.refs_0_), channel_id=1, source_target_pairs={{0,2},{1,5},{2,0},{3,7},{4,6},{5,1},{6,4},{7,3},{8,10},{9,13},{10,... | collective-permute-start | bytes 6291464 | tf_op jit(solution)/shard_map/ppermute | solution.py:634
  446.0 17.6 %collective-permute-start.24 = (bf16[128,2688]{1,0:T(8,128)(2,1)S(1)}, bf16[128,2688]{1,0:T(8,128)(2,1)S(1)}, u32[]{:S(2)}, u32[]{:S(2)}) collective-permute-start(bf16[128,2688]{1,0:T(8,128)(2,1)S(1)} %pad_maximum_fusion.3), channel_id=1, source_target_pairs={{0,4},{1,3},{2,6},{3,1},{4,0},{5,7},{6,2},{7,5},{8,12},{9,11},{10,... | collective-permute-start | bytes 2064392 | tf_op jit(solution)/shard_map/ppermute | solution.py:634
  464.4 30.3 %collective-permute-start.25 = (bf16[256,2688]{1,0:T(8,128)(2,1)}, bf16[256,2688]{1,0:T(8,128)(2,1)S(1)}, u32[]{:S(2)}, u32[]{:S(2)}) collective-permute-start(bf16[256,2688]{1,0:T(8,128)(2,1)} %constant_dynamic-update-slice_fusion.refs_0_), channel_id=1, source_target_pairs={{0,2},{1,5},{2,0},{3,7},{4,6},{5,1},{6,4},{7,3},{8,10},{9,13},{10,... | collective-permute-start | bytes 4128776 | tf_op jit(solution)/shard_map/ppermute | solution.py:634
  (51 other events, 359.4 us)
Sparse Core Ops, SparseCore 0:
  9.6 16.1 all-gather.3
  27.3 14.8 all-gather.5
  43.7 14.8 all-gather.7
  157.2 152.8 all-reduce.8

commit v2 on v1

v2 whole, which is shorter than its diff:
```python
import functools

import jax
import jax.numpy as jnp
from jax import lax
from jax.experimental import pallas as pl
from jax.experimental.pallas import tpu as pltpu
from jax.sharding import PartitionSpec as P

HD = 64
QH = 8
KVH = 2
SH = 24
SP = 64
STATE = 128
BLOCK = 128
INNER = 1536
LANES = 128
KV_AT = QH * HD
X, Y, Z, ZZ = 0, 1, 2, 3
TURNED = -1
WHOLE = {"down": 2, "wide": 1, "outs": 1, "rest": 2}
LINKS = {
    "down": ((X, Z, ZZ, Y), (Y, Z, X, ZZ)),
    "wide": ((X, Y, Z, ZZ), (Y, Z, X, ZZ)),
    "outs": ((Z, Y, X, ZZ), (X, Z, Y, ZZ)),
    "rest": ((X, Y, ZZ, Z), (Y, Z, X, ZZ)),
}
PLAN = (
    "state",
    "down",
    "grads",
    "wide",
    "down",
    "outs",
    "scan",
    "wide",
    "down",
    "attend",
    "sums",
    "outs",
    "wide",
    "down",
    "rest",
    "early",
    "outs",
    "wide",
    "down",
    "rest",
    "outs",
    "wide",
    "late",
    "down",
    "rest",
    "outs",
    "wide",
    "down",
    "rest",
    "outs",
    "wide",
    "rest",
    "outs",
    "wide",
    "rest",
    "outs",
    "rest",
)
AUX_AT = KV_AT + 2 * KVH * HD
EPSILON = 1e-05
NEGATIVE = -1e30
BF = jnp.bfloat16
F32 = jnp.float32
SWAP = [(0, 1), (1, 0)]
VMEM_LIMIT = 30 * 1024 * 1024
LARGE_LIMIT = 50 * 1024 * 1024
LONG = pl.CostEstimate(flops=15_000_000_000, bytes_accessed=1_000_000, transcendentals=0)
COST = pl.CostEstimate(flops=1_000_000, bytes_accessed=1_000_000, transcendentals=0)


def dot(left, right, over=((1,), (0,))):
    return lax.dot_general(left, right, (over, ((), ())), preferred_element_type=F32)


def split2(value):
    high = value.astype(BF)
    return high, (value - high.astype(F32)).astype(BF)


def split3(value):
    high = value.astype(BF)
    rest = value - high.astype(F32)
    middle = rest.astype(BF)
    return high, middle, (rest - middle.astype(F32)).astype(BF)


def dot3(left, right, over=((1,), (0,))):
    left_high, left_low = split2(left)
    right_high, right_low = split2(right)
    return dot(left_high, right_high, over) + (
        dot(left_high, right_low, over) + dot(left_low, right_high, over)
    )


def dot1(left, right, over=((1,), (0,))):
    return dot(left.astype(BF), right.astype(BF), over)


def spread(value, begin=0, end=SH):
    first_half = lax.broadcasted_iota(jnp.int32, (value.shape[0], LANES), 1) < SP
    return jnp.concatenate(
        [
            jnp.where(first_half, value[:, head : head + 1], value[:, head + 1 : head + 2])
            for head in range(begin, end, 2)
        ],
        axis=1,
    )


def gather_heads(*values):
    parts = [part for value in values for part in split2(value)]
    sums = dot(jnp.concatenate(parts), head_ones(), ((1,), (1,)))
    found, row = [], 0
    for value in values:
        rows = value.shape[0]
        found.append(sums[row : row + rows] + sums[row + rows : row + 2 * rows])
        row += 2 * rows
    return found


def head_ones():
    head = lax.broadcasted_iota(jnp.int32, (LANES, INNER), 0)
    column = lax.broadcasted_iota(jnp.int32, (LANES, INNER), 1)
    return ((column >= head * SP) & (column < (head + 1) * SP)).astype(BF)


def lower_ones():
    rows = lax.broadcasted_iota(jnp.int32, (BLOCK, BLOCK), 0)
    columns = lax.broadcasted_iota(jnp.int32, (BLOCK, BLOCK), 1)
    return rows >= columns


def cumulate(value, lower, over):
    high, middle, low = split3(value)
    return dot(lower, high, over) + (dot(lower, middle, over) + dot(lower, low, over))


def decays(aux, dt_bias, rate):
    raw = aux[:, 2 * STATE :] + dt_bias
    step = jnp.maximum(raw, 0.0) + jnp.log1p(jnp.exp(-jnp.abs(raw)))
    log_decay = -step * rate
    cumulated = cumulate(log_decay, lower_ones().astype(BF), ((1,), (0,)))
    return raw, step, log_decay, cumulated


def forward_kernel(
    resets, mixed, gate, aux, dt_bias, decay_log, state_in, ssm_out, gated, states, state
):
    number = pl.program_id(0)

    @pl.when(number == 0)
    def _():
        state[...] = state_in[...]

    @pl.when(resets[number] != 0)
    def _():
        state[...] = jnp.zeros_like(state)

    aux_now = aux[...]
    b_in = aux_now[:, :STATE]
    c_out = aux_now[:, STATE : 2 * STATE]
    _, step, _, cumulated = decays(aux_now, dt_bias[...], jnp.exp(decay_log[...]))
    scaled = mixed[...].astype(F32) * spread(step)
    wide = spread(cumulated)
    tail = jnp.exp(wide[BLOCK - 1 :, :] - wide)
    grown = jnp.exp(wide)
    before = state[...]
    states[...] = before[None].astype(BF)
    state[...] = grown[BLOCK - 1 :, :] * before + dot1(b_in, scaled * tail, ((0,), (0,)))
    outer = grown * dot1(c_out, before)
    both = dot3(c_out, b_in, ((1,), (1,)))
    lower = lower_ones()
    flipped = cumulated.T
    first_half = lax.broadcasted_iota(jnp.int32, (BLOCK, LANES), 1) < SP
    scaled_low = scaled.astype(BF)
    zero = jnp.zeros((BLOCK, LANES), BF)
    for pair in range(SH // 2):
        weights = []
        for head in (2 * pair, 2 * pair + 1):
            spread_now = cumulated[:, head : head + 1] - flipped[head : head + 1, :]
            weights.append((jnp.exp(jnp.where(lower, spread_now, NEGATIVE)) * both).astype(BF))
        columns = slice(pair * LANES, (pair + 1) * LANES)
        low = scaled_low[:, columns]
        low = jnp.concatenate([jnp.where(first_half, low, zero), jnp.where(first_half, zero, low)])
        inner = dot(jnp.concatenate(weights, axis=1), low)
        total = inner + outer[:, columns]
        ssm_out[:, columns] = total
        gate_now = gate[:, columns].astype(F32)
        gated[:, columns] = (total * (gate_now / (1.0 + jnp.exp(-gate_now)))).astype(BF)


def silu_of(gate):
    chance = 1.0 / (1.0 + jnp.exp(-gate))
    return gate * chance, chance


def state_back_kernel(
    resets, d_gated, gate, aux, ssm_out, dt_bias, decay_log, d_state_out, d_gate, d_state
):
    number = pl.num_programs(0) - 1 - pl.program_id(0)

    @pl.when(pl.program_id(0) == 0)
    def _():
        d_state[...] = jnp.zeros_like(d_state)

    aux_now = aux[...]
    _, _, _, cumulated = decays(aux_now, dt_bias[...], jnp.exp(decay_log[...]))
    grown = spread(jnp.exp(cumulated))
    gate_silu, chance = silu_of(gate[...].astype(F32))
    d_gated_now = d_gated[...].astype(F32)
    d_gate[...] = (d_gated_now * ssm_out[...] * (chance + gate_silu * (1.0 - chance))).astype(BF)
    d_grown = d_gated_now * gate_silu * grown
    c_out = aux_now[:, STATE : 2 * STATE]
    d_state[...] = grown[BLOCK - 1 :, :] * d_state[...] + dot1(c_out, d_grown, ((0,), (0,)))

    @pl.when(resets[number] != 0)
    def _():
        d_state[...] = jnp.zeros_like(d_state)

    d_state_out[...] = d_state[...].astype(BF)


def backward_kernel(
    resets,
    d_gated,
    mixed,
    gate,
    aux,
    ssm_out,
    states,
    dt_bias,
    decay_log,
    d_state_in,
    d_mixed,
    d_aux,
    d_heads,
    d_state,
):
    number = pl.num_programs(0) - 1 - pl.program_id(0)

    @pl.when(pl.program_id(0) == 0)
    def _():
        d_state[...] = d_state_in[...].astype(F32)
        d_heads[...] = jnp.zeros_like(d_heads)

    lower = lower_ones()
    aux_now = aux[...]
    b_in = aux_now[:, :STATE]
    c_out = aux_now[:, STATE : 2 * STATE]
    rate = jnp.exp(decay_log[...])
    raw, step, log_decay, cumulated = decays(aux_now, dt_bias[...], rate)
    step_wide = spread(step)
    mixed_now = mixed[...].astype(F32)
    scaled = mixed_now * step_wide
    wide = spread(cumulated)
    tail = jnp.exp(wide[BLOCK - 1 :, :] - wide)
    grown = jnp.exp(wide)
    gate_now = gate[...].astype(F32)
    gate_silu, _ = silu_of(gate_now)
    d_gated_now = d_gated[...].astype(F32)
    ssm_now = ssm_out[...]
    d_out = d_gated_now * gate_silu
    before = states[0].astype(F32)
    d_after = d_state[...]
    d_grown = d_out * grown
    d_c = dot1(d_grown, before, ((1,), (1,)))
    d_before = grown[BLOCK - 1 :, :] * d_after + dot1(c_out, d_grown, ((0,), (0,)))
    tailed = scaled * tail
    d_b = dot1(tailed, d_after, ((1,), (1,)))
    d_tailed = dot1(b_in, d_after)
    ends = jnp.sum(tailed * d_tailed, axis=0, keepdims=True) + grown[BLOCK - 1 :, :] * jnp.sum(
        d_after * before, axis=0, keepdims=True
    )
    both = dot3(c_out, b_in, ((1,), (1,)))
    flipped = cumulated.T
    first_half = lax.broadcasted_iota(jnp.int32, (BLOCK, LANES), 1) < SP
    scaled_low = scaled.astype(BF)
    d_low = d_out.astype(BF)
    zero = jnp.zeros((BLOCK, LANES), BF)
    d_both = jnp.zeros((BLOCK, BLOCK), F32)
    parts = []
    for pair in range(SH // 2):
        columns = slice(pair * LANES, (pair + 1) * LANES)
        falls = []
        for head in (2 * pair, 2 * pair + 1):
            spread_now = cumulated[:, head : head + 1] - flipped[head : head + 1, :]
            falls.append(jnp.exp(jnp.where(lower, spread_now, NEGATIVE)))
        weight = jnp.concatenate([(falls[0] * both).astype(BF), (falls[1] * both).astype(BF)])
        low = d_low[:, columns]
        low = jnp.concatenate([jnp.where(first_half, low, zero), jnp.where(first_half, zero, low)])
        d_weight = dot(low, scaled_low[:, columns], ((1,), (1,)))
        d_both = d_both + falls[0] * d_weight[:BLOCK] + falls[1] * d_weight[BLOCK:]
        parts.append(dot(weight, low, ((0,), (0,))))
    d_inner = jnp.concatenate(parts, axis=1)
    carried = tail * d_tailed
    d_scaled = d_inner + carried
    d_mixed[...] = (d_scaled * step_wide).astype(BF)
    d_step, d_cumulated, d_last = gather_heads(
        d_scaled * mixed_now,
        d_low.astype(F32) * ssm_now - scaled_low.astype(F32) * d_inner - scaled * carried,
        jnp.broadcast_to(ends, (8, INNER)),
    )
    d_decay = cumulate(d_cumulated, lower.astype(BF), ((0,), (0,))) + d_last[:1]
    d_raw = (d_step - d_decay * rate) * (1.0 / (1.0 + jnp.exp(-raw)))
    real = lax.broadcasted_iota(jnp.int32, (BLOCK, LANES), 1) < SH
    d_raw = jnp.where(real, d_raw, 0.0)
    d_c = d_c + dot1(d_both, b_in)
    d_b = d_b + dot1(d_both, c_out, ((0,), (0,)))
    d_aux[...] = jnp.concatenate([d_b, d_c, d_raw], axis=1).astype(BF)
    d_heads[...] += jnp.concatenate(
        [
            jnp.sum(d_raw, axis=0, keepdims=True),
            jnp.sum(jnp.where(real, d_decay * log_decay, 0.0), axis=0, keepdims=True),
            jnp.zeros((6, LANES), F32),
        ]
    )
    d_state[...] = d_before

    @pl.when(resets[number] != 0)
    def _():
        d_state[...] = jnp.zeros_like(d_state)


def scalars():
    return pl.BlockSpec(memory_space=pltpu.SMEM)


def whole(shape):
    return pl.BlockSpec(shape, lambda number: (0,) * len(shape))


def params_of(limit=VMEM_LIMIT):
    return pltpu.CompilerParams(dimension_semantics=("arbitrary",), vmem_limit_bytes=limit)


def run_forward(resets, mixed, aux, dt_bias, decay_log, state_in):
    rows = mixed.shape[0]
    count = rows // BLOCK
    return pl.pallas_call(
        forward_kernel,
        grid=(count,),
        in_specs=[
            scalars(),
            pl.BlockSpec((BLOCK, INNER), lambda number: (number, 0)),
            pl.BlockSpec((BLOCK, INNER), lambda number: (number, 1)),
            pl.BlockSpec((BLOCK, 3 * LANES), lambda number: (number, 0)),
            whole((1, LANES)),
            whole((1, LANES)),
            whole((STATE, INNER)),
        ],
        out_specs=[
            pl.BlockSpec((BLOCK, INNER), lambda number: (number, 0)),
            pl.BlockSpec((BLOCK, INNER), lambda number: (number, 0)),
            pl.BlockSpec((1, STATE, INNER), lambda number: (number, 0, 0)),
        ],
        out_shape=[
            jax.ShapeDtypeStruct((rows, INNER), F32),
            jax.ShapeDtypeStruct((rows, INNER), BF),
            jax.ShapeDtypeStruct((count, STATE, INNER), BF),
        ],
        scratch_shapes=[pltpu.VMEM((STATE, INNER), F32)],
        compiler_params=params_of(),
        cost_estimate=LONG,
        name="ssm_forward",
    )(resets, mixed, mixed, aux, dt_bias, decay_log, state_in)


def run_state_back(resets, d_gated, mixed, aux, ssm_out, dt_bias, decay_log):
    count = mixed.shape[0] // BLOCK
    turned = lambda number: (count - 1 - number, 0)
    return pl.pallas_call(
        state_back_kernel,
        grid=(count,),
        in_specs=[
            scalars(),
            pl.BlockSpec((BLOCK, INNER), turned),
            pl.BlockSpec((BLOCK, INNER), lambda number: (count - 1 - number, 1)),
            pl.BlockSpec((BLOCK, 3 * LANES), turned),
            pl.BlockSpec((BLOCK, INNER), turned),
            whole((1, LANES)),
            whole((1, LANES)),
        ],
        out_specs=[whole((STATE, INNER)), pl.BlockSpec((BLOCK, INNER), turned)],
        out_shape=[
            jax.ShapeDtypeStruct((STATE, INNER), BF),
            jax.ShapeDtypeStruct((mixed.shape[0], INNER), BF),
        ],
        scratch_shapes=[pltpu.VMEM((STATE, INNER), F32)],
        compiler_params=params_of(),
        cost_estimate=COST,
        name="ssm_state_back",
    )(resets, d_gated, mixed, aux, ssm_out, dt_bias, decay_log)


def run_backward(resets, d_gated, mixed, aux, ssm_out, states, dt_bias, decay_log, d_state_in):
    rows = mixed.shape[0]
    count = rows // BLOCK
    turned = lambda number: (count - 1 - number, 0)
    return pl.pallas_call(
        backward_kernel,
        grid=(count,),
        in_specs=[
            scalars(),
            pl.BlockSpec((BLOCK, INNER), turned),
            pl.BlockSpec((BLOCK, INNER), turned),
            pl.BlockSpec((BLOCK, INNER), lambda number: (count - 1 - number, 1)),
            pl.BlockSpec((BLOCK, 3 * LANES), turned),
            pl.BlockSpec((BLOCK, INNER), turned),
            pl.BlockSpec((1, STATE, INNER), lambda number: (count - 1 - number, 0, 0)),
            whole((1, LANES)),
            whole((1, LANES)),
            whole((STATE, INNER)),
        ],
        out_specs=[
            pl.BlockSpec((BLOCK, INNER), turned),
            pl.BlockSpec((BLOCK, 3 * LANES), turned),
            whole((8, LANES)),
        ],
        out_shape=[
            jax.ShapeDtypeStruct((rows, INNER), BF),
            jax.ShapeDtypeStruct((rows, 3 * LANES), BF),
            jax.ShapeDtypeStruct((8, LANES), F32),
        ],
        scratch_shapes=[pltpu.VMEM((STATE, INNER), F32)],
        compiler_params=params_of(),
        cost_estimate=COST,
        name="ssm_backward",
    )(resets, d_gated, mixed, mixed, aux, ssm_out, states, dt_bias, decay_log, d_state_in)


def head_rows(ref, start, group, width):
    return jnp.concatenate(
        [
            ref[start : start + BLOCK, (group * width + head) * HD : (group * width + head + 1) * HD]
            for head in range(width)
        ]
    )


def masked_scores(q_rows, k_rows, bias_row, lower, width):
    raw = dot(q_rows, k_rows, ((1,), (1,))) + bias_row
    edge = raw.shape[1] - BLOCK
    corner = jnp.where(jnp.concatenate([lower] * width), raw[:, edge:], NEGATIVE)
    return jnp.concatenate([raw[:, :edge], corner], axis=1)


def attend_kernel(q_ref, prior_ref, here_ref, bias_ref, out_ref, total_ref):
    width = QH // KVH
    rows = q_ref.shape[0]
    halo = prior_ref.shape[0]
    lower = lower_ones()
    for group in range(KVH):
        key_columns = slice(group * HD, (group + 1) * HD)
        value_columns = slice((KVH + group) * HD, (KVH + group + 1) * HD)
        keys = jnp.concatenate([prior_ref[:, key_columns], here_ref[:, key_columns]])
        values = jnp.concatenate([prior_ref[:, value_columns], here_ref[:, value_columns]])
        for block in range(rows // BLOCK):
            start = block * BLOCK
            reach = halo + start + BLOCK
            q_rows = head_rows(q_ref, start, group, width)
            scores = masked_scores(
                q_rows, keys[:reach], bias_ref[block : block + 1, :reach], lower, width
            )
            top = jnp.max(scores, axis=1, keepdims=True)
            powers = jnp.exp(scores - top)
            total = jnp.sum(powers, axis=1, keepdims=True)
            probs = (powers * (1.0 / total)).astype(BF)
            out = dot(probs, values[:reach])
            log_total = top + jnp.log(total)
            for head in range(width):
                place = group * width + head
                some = slice(head * BLOCK, (head + 1) * BLOCK)
                out_ref[start : start + BLOCK, place * HD : (place + 1) * HD] = out[some].astype(BF)
                total_ref[start : start + BLOCK, place : place + 1] = log_total[some]


def attend_back_kernel(
    q_ref, prior_ref, here_ref, bias_ref, total_ref, d_ref, dq_ref, d_prior_ref, d_here_ref, sums
):
    width = QH // KVH
    rows = q_ref.shape[0]
    halo = prior_ref.shape[0]
    lower = lower_ones()
    sums[...] = jnp.zeros_like(sums)
    for group in range(KVH):
        key_columns = slice(group * HD, (group + 1) * HD)
        value_columns = slice((KVH + group) * HD, (KVH + group + 1) * HD)
        keys = jnp.concatenate([prior_ref[:, key_columns], here_ref[:, key_columns]])
        values = jnp.concatenate([prior_ref[:, value_columns], here_ref[:, value_columns]])
        for block in range(rows // BLOCK):
            start = block * BLOCK
            reach = halo + start + BLOCK
            q_rows = head_rows(q_ref, start, group, width)
            d_rows = head_rows(d_ref, start, group, width)
            scores = masked_scores(
                q_rows, keys[:reach], bias_ref[block : block + 1, :reach], lower, width
            )
            log_total = jnp.concatenate(
                [
                    total_ref[start : start + BLOCK, group * width + head : group * width + head + 1]
                    for head in range(width)
                ]
            )
            probs = jnp.exp(scores - log_total)
            probs_low = probs.astype(BF)
            d_probs = dot(d_rows, values[:reach], ((1,), (1,)))
            weighed = probs * d_probs
            d_scores = (weighed - probs * jnp.sum(weighed, axis=1, keepdims=True)).astype(BF)
            d_queries = dot(d_scores, keys[:reach]) * HD**-0.5
            for head in range(width):
                place = group * width + head
                some = slice(head * BLOCK, (head + 1) * BLOCK)
                dq_ref[start : start + BLOCK, place * HD : (place + 1) * HD] = d_queries[some].astype(BF)
            sums[:reach, key_columns] += dot(d_scores, q_rows, ((0,), (0,)))
            sums[:reach, value_columns] += dot(probs_low, d_rows, ((0,), (0,)))
    d_prior_ref[...] = sums[:halo].astype(BF)
    d_here_ref[...] = sums[halo:]


def run_attend(queries, prior, here, bias):
    rows = queries.shape[0]
    return pl.pallas_call(
        attend_kernel,
        out_shape=[
            jax.ShapeDtypeStruct((rows, QH * HD), BF),
            jax.ShapeDtypeStruct((rows, QH), F32),
        ],
        compiler_params=pltpu.CompilerParams(vmem_limit_bytes=VMEM_LIMIT),
        cost_estimate=LONG,
        name="attend",
    )(queries, prior, here, bias)


def run_attend_back(queries, prior, here, bias, log_total, d_attended):
    rows = queries.shape[0]
    halo = prior.shape[0]
    return pl.pallas_call(
        attend_back_kernel,
        out_shape=[
            jax.ShapeDtypeStruct((rows, QH * HD), BF),
            jax.ShapeDtypeStruct((halo, 2 * KVH * HD), BF),
            jax.ShapeDtypeStruct((rows, 2 * KVH * HD), F32),
        ],
        scratch_shapes=[pltpu.VMEM((halo + rows, 2 * KVH * HD), F32)],
        compiler_params=pltpu.CompilerParams(vmem_limit_bytes=VMEM_LIMIT),
        cost_estimate=COST,
        name="attend_back",
    )(queries, prior, here, bias, log_total, d_attended)


def swap(value):
    return lax.ppermute(value, "shard", SWAP)


def natural(mine, theirs, position, axis):
    return jnp.where(
        position == 0,
        jnp.concatenate([mine, theirs], axis=axis),
        jnp.concatenate([theirs, mine], axis=axis),
    )


def half_of(value, which, axis):
    size = value.shape[axis] // 2
    return lax.dynamic_slice_in_dim(value, which * size, size, axis)


class Stream:
    def __init__(self, terms, whole, *orders):
        self.terms = terms
        self.count = lax.axis_size("rep")
        self.bits = self.count.bit_length() - 1
        self.stack = None
        self.got = None
        self.gone = 0
        if self.count != 1 << self.bits:
            self.stack = lax.psum(self.part(0, terms[0].shape[0]), "rep")
            self.bits = 0
        places = range(self.bits)
        self.orders = [
            [bit for bit in order if bit < self.bits] + [bit for bit in places if bit not in order]
            for order in orders
        ]
        rep, core = lax.axis_index("rep"), lax.axis_index("shard")
        self.cuts = max(0, self.bits - whole)
        self.sides = [
            jnp.where(core == 0, (rep >> first) & 1, (rep >> second) & 1)
            for first, second in zip(*self.orders)
        ][: self.cuts]
        self.steps = [("scatter", step) for step in places[: self.cuts]]
        self.steps += [("exchange", step) for step in places[self.cuts :]]
        self.steps += [("gather", step) for step in reversed(places[: self.cuts])]

    def pairs(self, step):
        return [
            (rep * 2 + core, (rep ^ (1 << self.orders[core][step])) * 2 + core)
            for rep in range(self.count)
            for core in range(2)
        ]

    def part(self, start, size):
        total = lax.dynamic_slice_in_dim(self.terms[0], start, size, 0).astype(F32)
        for term in self.terms[1:]:
            total = total + lax.dynamic_slice_in_dim(term, start, size, 0).astype(F32)
        return total.astype(BF)

    def latest(self):
        if self.got is not None:
            return self.got
        return self.terms[-1] if self.stack is None else self.stack

    def hold(self, token):
        if self.got is not None:
            self.got = after(self.got, token)
        elif self.stack is None:
            self.terms[-1] = after(self.terms[-1], token)

    def prepare(self):
        kind, step = self.steps[0]
        if kind == "gather":
            if self.stack is None:
                self.stack = self.part(0, self.terms[0].shape[0])
            else:
                self.stack = jnp.concatenate([self.stack, self.got])
            self.operand = self.stack
        elif kind == "exchange":
            self.operand = self.part(0, self.terms[0].shape[0])
        else:
            size = self.terms[0].shape[0] // 2
            self.operand = self.part((1 - self.sides[step]) * size, size)

    def go(self):
        kind, step = self.steps.pop(0)
        self.gone += 1
        got = lax.ppermute(self.operand, ("rep", "shard"), self.pairs(step))
        if kind == "gather":
            self.got = got
        elif kind == "exchange":
            self.terms = [self.operand, got]
        else:
            size = self.terms[0].shape[0] // 2
            self.terms = [
                lax.dynamic_slice_in_dim(term, self.sides[step] * size, size, 0)
                for term in self.terms
            ] + [got]

    def own(self):
        block = jnp.zeros((), jnp.int32)
        for side in self.sides:
            block = 2 * block + side
        return block.astype(jnp.int32)

    def finish(self, outputs, started=None, weights=()):
        if self.stack is None:
            self.stack = self.part(0, self.terms[0].shape[0])
        stacks = [self.stack] if self.got is None else [self.stack, self.got]
        blocks = 1 << self.cuts
        far = max(1, blocks // 4)
        quarters = blocks // far
        each = quarters // len(stacks)
        size = stacks[0].shape[0] // each // far
        width = stacks[0].shape[1]
        own = self.own()
        if size % 16:
            flat = jnp.concatenate(stacks).reshape(blocks, size, width)
            flat = jnp.zeros_like(flat).at[jnp.arange(blocks) ^ own].set(flat).reshape(-1, width)
            made = []
            for shape, _, pieces in outputs:
                cuts = [flat[:, begin:end].astype(F32) for _, begin, end in pieces]
                if pieces[0][0] == TURNED:
                    made.append(cuts[0].T)
                    continue
                whole_width = shape.shape[-1]
                if len(shape.shape) == 3:
                    value = jnp.stack(cuts)
                    value = jnp.pad(value, ((0, 0), (0, 0), (whole_width - value.shape[-1], 0)))
                else:
                    value = jnp.concatenate(cuts, axis=1)
                made.append(value)
            products = [
                jnp.sum(
                    value * weight[:, : value.shape[1]].astype(F32),
                    axis=0 if pieces[0][0] == TURNED else 1,
                )
                for value, weight, (_, _, pieces) in zip(made, weights, outputs)
                if weight is not None
            ]
            if started is not None:
                made[-1] = jnp.concatenate([made[-1], started[:, made[-1].shape[1] :]], axis=1)
            if products:
                made.append(jnp.broadcast_to(sum(products), (8, products[0].shape[0])))
            return made
        rows = far * size
        in_specs = [
            pl.BlockSpec((rows, width), lambda step, places: (jnp.minimum(step, each - 1), 0))
        ]
        if len(stacks) == 2:
            in_specs.append(
                pl.BlockSpec((rows, width), lambda step, places: (jnp.maximum(step - each, 0), 0))
            )
        out_specs = []
        scratch = []
        for shape, block, pieces in outputs:
            if pieces[0][0] == TURNED:
                out_specs.append(
                    pl.BlockSpec((shape.shape[0], rows), lambda step, places: (0, places[step]))
                )
                scratch = [pltpu.VMEM((rows, block), F32)]
            elif len(shape.shape) == 3:
                last = shape.shape[2] // block - 1
                out_specs.append(
                    pl.BlockSpec(
                        (shape.shape[0], rows, block),
                        lambda step, places, last=last: (0, places[step], last),
                    )
                )
            else:
                out_specs.append(pl.BlockSpec((rows, block), lambda step, places: (places[step], 0)))
        inputs = list(stacks)
        shapes = [shape for shape, _, _ in outputs]
        for weight, (_, block, pieces) in zip(weights, outputs):
            if weight is None:
                continue
            inputs.append(weight)
            if pieces[0][0] == TURNED:
                in_specs.append(
                    pl.BlockSpec((weight.shape[0], rows), lambda step, places: (0, places[step]))
                )
            else:
                in_specs.append(pl.BlockSpec((rows, block), lambda step, places: (places[step], 0)))
        if weights:
            out_specs.append(pl.BlockSpec((8, rows), lambda step, places: (0, places[step])))
            shapes.append(jax.ShapeDtypeStruct((8, rows * quarters), F32))
        aliases = {}
        if started is not None:
            aliases = {1 + len(inputs): len(outputs) - 1}
            inputs.append(started)
            in_specs.append(pl.BlockSpec(memory_space=pl.ANY))
        places = jnp.concatenate(
            [jnp.arange(quarters, dtype=jnp.int32) ^ (own // far), (own % far).reshape(1)]
        )
        return pl.pallas_call(
            functools.partial(
                finish_kernel,
                len(stacks),
                far,
                [cut for _, _, cut in outputs],
                [weight is not None for weight in weights],
            ),
            grid_spec=pltpu.PrefetchScalarGridSpec(
                num_scalar_prefetch=1,
                grid=(quarters,),
                in_specs=in_specs,
                out_specs=out_specs,
                scratch_shapes=scratch,
            ),
            out_shape=shapes,
            input_output_aliases=aliases,
            compiler_params=params_of(),
            cost_estimate=COST,
            name="unpack",
        )(places, *inputs)


def finish_kernel(count, far, layout, weighed, places, *refs):
    turned = any(pieces[0][0] == TURNED for pieces in layout)
    if turned:
        held, refs = refs[-1], refs[:-1]
    if any(weighed):
        products, refs = refs[-1], refs[:-1]
    outputs = refs[-len(layout) :]
    weights = list(refs[count : count + sum(weighed)])
    steps = pl.num_programs(0)
    within = places[steps]
    size = refs[0].shape[0] // far

    def write(ref):
        width = ref.shape[1]
        for number in range(far):
            row = pl.multiple_of((within ^ number) * size, size)
            piece_rows = slice(number * size, (number + 1) * size)
            for out, pieces in zip(outputs, layout):
                for target, begin, end in pieces:
                    if target == TURNED:
                        continue
                    value = ref[piece_rows, begin:end].astype(F32)
                    if len(out.shape) == 3:
                        out[target, pl.ds(row, size), :] = value
                    else:
                        out[pl.ds(row, size), target : target + end - begin] = value
            if turned:
                held[pl.ds(row, size), :] = ref[piece_rows, width - held.shape[1] :].astype(F32)
        if turned:
            flipped = held[...].T
            for out, pieces in zip(outputs, layout):
                target, begin, end = pieces[0]
                if target == TURNED:
                    first = width - held.shape[1]
                    out[...] = flipped[begin - first : end - first, :]

    if count == 1:
        write(refs[0])
    else:

        @pl.when(pl.program_id(0) < steps // 2)
        def _():
            write(refs[0])

        @pl.when(pl.program_id(0) >= steps // 2)
        def _():
            write(refs[1])

    if any(weighed):
        ones = jnp.ones((8, LANES), BF)
        total = jnp.zeros(products.shape, F32)
        for out, pieces, used in zip(outputs, layout, weighed):
            if not used:
                continue
            product = out[...] * weights.pop(0)[...].astype(F32)
            if pieces[0][0] == TURNED:
                total = total + jnp.sum(product, axis=0, keepdims=True)
                continue
            narrow = product[:, :LANES]
            for column in range(LANES, product.shape[1], LANES):
                narrow = narrow + product[:, column : column + LANES]
            for part in split3(narrow):
                total = total + dot(ones, part, ((1,), (1,)))
        products[...] = total


def after(value, *others):
    return lax.optimization_barrier((value, *others))[0]


def fence(value, *others):
    anywhere = pl.BlockSpec(memory_space=pl.ANY)
    return pl.pallas_call(
        lambda *refs: None,
        in_specs=[anywhere] * (1 + len(others)),
        out_specs=anywhere,
        out_shape=jax.ShapeDtypeStruct(value.shape, value.dtype),
        input_output_aliases={0: 0},
        cost_estimate=COST,
        name="fence",
    )(value, *others)


def columns_of(ref, which, size):
    return ref[:, pl.ds(pl.multiple_of(which * size, size), size)]


def inverse_rms(values):
    return lax.rsqrt(jnp.mean(values * values, axis=-1, keepdims=True) + EPSILON)


def norm_back(values, inverse, gain, grad):
    scaled = grad * gain
    shared = jnp.mean(scaled * values, axis=-1, keepdims=True) * (inverse * inverse)
    return (
        inverse * (scaled - values * shared),
        jnp.sum(grad * (values * inverse), axis=0, keepdims=True),
    )


def project_kernel(
    position,
    resets,
    tokens,
    gains,
    dt_bias,
    decay_log,
    query_mine,
    query_theirs,
    kv_mine,
    kv_theirs,
    aux_mine,
    aux_theirs,
    ssm_mine,
    ssm_theirs,
    normed,
    queries,
    key_vals,
    aux,
    mixed,
    state_out,
    tails,
    carries,
):
    here = position[0]
    half = tokens.shape[1] // 2
    step = pl.program_id(0)
    blocks = tokens.shape[0] // BLOCK

    def product(mine, theirs, over=((1,), (0,))):
        return dot(columns_of(normed, here, half), mine[...], over) + dot(
            columns_of(normed, 1 - here, half), theirs[...], over
        )

    @pl.when(pl.program_id(0) == 0)
    def _():
        hidden = tokens[...].astype(F32)
        normed[...] = (hidden * inverse_rms(hidden) * gains[0:1]).astype(BF)
        queries[...] = product(query_mine, query_theirs).astype(BF) * jnp.asarray(HD**-0.5, BF)
        key_vals[...] = product(kv_mine, kv_theirs).astype(BF)
        found = product(aux_mine, aux_theirs, ((1,), (1,)))
        aux[:, : found.shape[1]] = found
        aux[:, found.shape[1] :] = jnp.zeros_like(aux[:, found.shape[1] :])
        rate = jnp.exp(decay_log[...])
        for block in range(blocks):
            rows = slice(block * BLOCK, (block + 1) * BLOCK)
            _, step_size, _, cumulated = decays(aux[rows, :], dt_bias[...], rate)
            last = cumulated[BLOCK - 1 :, :]
            tails[rows, :] = step_size * jnp.exp(last - cumulated)
            carries[block : block + 1, :] = jnp.exp(last)

    found = product(ssm_mine, ssm_theirs)
    mixed[...] = found.astype(BF)

    for number in range(INNER // CHUNK):

        @pl.when(step == number)
        def _():
            heads = (number * CHUNK // SP, (number + 1) * CHUNK // SP)
            scaled = (found * spread(tails[...], *heads)).astype(BF)
            carried = spread(carries[...], *heads)
            state = jnp.zeros((STATE, CHUNK), F32)
            for block in range(blocks):
                rows = slice(block * BLOCK, (block + 1) * BLOCK)
                b_in = aux[rows, :STATE].astype(BF)
                state = jnp.where(resets[block] != 0, 0.0, carried[block : block + 1, :] * state)
                state = state + dot(b_in, scaled[rows, :], ((0,), (0,)))
            state_out[...] = state


CHUNK = 512


def run_project(position, resets, tokens, gains, dt_bias, decay_log, query, kv, aux, ssm):
    rows, width = tokens.shape
    half = width // 2
    inner = ssm[0].shape[1]
    aux_width = 3 * LANES
    fixed = lambda shape: pl.BlockSpec(shape, lambda step, place, resets: (0,) * len(shape))
    sliding = pl.BlockSpec((half, CHUNK), lambda step, place, resets: (0, step))
    weights = [fixed(item.shape) for item in (*query, *kv, *aux)]
    return pl.pallas_call(
        project_kernel,
        grid_spec=pltpu.PrefetchScalarGridSpec(
            num_scalar_prefetch=2,
            grid=(inner // CHUNK,),
            in_specs=[
                *[fixed(item.shape) for item in (tokens, gains, dt_bias, decay_log)],
                *weights,
                sliding,
                sliding,
            ],
            out_specs=[
                fixed((rows, width)),
                fixed((rows, KV_AT)),
                fixed((rows, AUX_AT - KV_AT)),
                fixed((rows, aux_width)),
                pl.BlockSpec((rows, CHUNK), lambda step, place, resets: (0, step)),
                pl.BlockSpec(
                    (STATE, CHUNK),
                    lambda step, place, resets: (0, jnp.minimum(step, INNER // CHUNK - 1)),
                ),
            ],
            scratch_shapes=[pltpu.VMEM((rows, LANES), F32), pltpu.VMEM((8, LANES), F32)],
        ),
        out_shape=[
            jax.ShapeDtypeStruct((rows, width), BF),
            jax.ShapeDtypeStruct((rows, KV_AT), BF),
            jax.ShapeDtypeStruct((rows, AUX_AT - KV_AT), BF),
            jax.ShapeDtypeStruct((rows, aux_width), F32),
            jax.ShapeDtypeStruct((rows, inner), BF),
            jax.ShapeDtypeStruct((STATE, INNER), F32),
        ],
        compiler_params=params_of(LARGE_LIMIT),
        cost_estimate=LONG,
        name="project",
    )(position, resets, tokens, gains, dt_bias, decay_log, *query, *kv, *aux, *ssm)


def middle_kernel(
    position,
    tokens,
    attended,
    gated,
    cotangent,
    gains,
    attn_mine,
    attn_theirs,
    ssm_mine,
    ssm_theirs,
    gate_mine,
    gate_theirs,
    up_mine,
    up_theirs,
    down_mine,
    down_theirs,
    output,
    d_middle,
    d_attn_branch,
    d_ssm_branch,
    d_attended,
    d_gated,
    gain_grads,
    grad_down_theirs,
    grad_down_mine,
    grad_wide_theirs,
    grad_wide_mine,
    attn_branch,
    ssm_branch,
    middle,
    normed,
    flipped,
    out_sum,
    d_normed,
):
    here = position[0]
    step = pl.program_id(0)
    count = pl.num_programs(0)
    width = tokens.shape[1]
    half = width // 2
    attn_half = attended.shape[1] // 2
    ssm_half = gated.shape[1] // 2
    flat = ((1,), (1,))

    def place(which, size):
        return pl.ds(pl.multiple_of(which * size, size), size)

    @pl.when(step == 0)
    def _():
        attn = dot(columns_of(attended, here, attn_half), attn_mine[...]) + dot(
            columns_of(attended, 1 - here, attn_half), attn_theirs[...]
        )
        attn_branch[...] = attn
        ssm = dot(columns_of(gated, here, ssm_half), ssm_mine[...]) + dot(
            columns_of(gated, 1 - here, ssm_half), ssm_theirs[...]
        )
        ssm_branch[...] = ssm
        joined = tokens[...].astype(F32) + 0.5 * (
            attn * inverse_rms(attn) * gains[1:2] + ssm * inverse_rms(ssm) * gains[2:3]
        )
        middle[...] = joined
        out_sum[...] = joined
        scaled = joined * inverse_rms(joined) * gains[3:4]
        normed[...] = scaled.astype(BF)
        flipped[...] = scaled.T.astype(BF)
        d_normed[...] = jnp.zeros_like(d_normed)

    first = step < count // 2
    mine = columns_of(normed, here, half)
    theirs = columns_of(normed, 1 - here, half)
    gate_val = dot(mine, gate_mine[...]) + dot(theirs, gate_theirs[...])
    up_val = dot(mine, up_mine[...]) + dot(theirs, up_theirs[...])
    gate_silu, chance = silu_of(gate_val)
    activated = (gate_silu * up_val).astype(BF)
    down = jnp.where(first, down_theirs[...], down_mine[...])
    d_activated = dot(cotangent[...], down, flat)
    out_sum[...] += dot(activated, down)
    d_up = (d_activated * gate_silu).astype(BF)
    d_gate = (d_activated * up_val * (chance + gate_silu * (1.0 - chance))).astype(BF)
    d_normed[:, place(here, half)] += dot(d_gate, gate_mine[...], flat) + dot(d_up, up_mine[...], flat)
    d_normed[:, place(1 - here, half)] += dot(d_gate, gate_theirs[...], flat) + dot(
        d_up, up_theirs[...], flat
    )
    grad_down = dot(activated, cotangent[...], ((0,), (0,))).astype(BF)

    @pl.when(first)
    def _():
        grad_down_theirs[...] = grad_down

    @pl.when(jnp.logical_not(first))
    def _():
        grad_down_mine[...] = grad_down

    for which, ref in ((here, grad_wide_mine), (1 - here, grad_wide_theirs)):
        turned = flipped[place(which, half), :]
        ref[:, :CHUNK] = dot(turned, d_gate).astype(BF)
        ref[:, CHUNK:] = dot(turned, d_up).astype(BF)

    @pl.when(step == count - 1)
    def _():
        output[...] = out_sum[...].astype(BF)
        joined = middle[...]
        d_joined, d_gain_ff = norm_back(joined, inverse_rms(joined), gains[3:4], d_normed[...])
        d_joined = cotangent[...].astype(F32) + d_joined
        d_middle[...] = d_joined
        attn = attn_branch[...]
        d_attn, d_gain_attn = norm_back(attn, inverse_rms(attn), gains[1:2], 0.5 * d_joined)
        d_attn_low = d_attn.astype(BF)
        d_attn_branch[...] = d_attn_low
        ssm = ssm_branch[...]
        d_ssm, d_gain_ssm = norm_back(ssm, inverse_rms(ssm), gains[2:3], 0.5 * d_joined)
        d_ssm_low = d_ssm.astype(BF)
        d_ssm_branch[...] = d_ssm_low
        gain_grads[...] = jnp.concatenate(
            [d_gain_attn, d_gain_ssm, d_gain_ff, jnp.zeros((5, width), F32)]
        )
        for which, attn_weight, ssm_weight in (
            (here, attn_mine, ssm_mine),
            (1 - here, attn_theirs, ssm_theirs),
        ):
            d_attended[:, place(which, attn_half)] = dot(d_attn_low, attn_weight[...], flat).astype(BF)
            d_gated[:, place(which, ssm_half)] = dot(d_ssm_low, ssm_weight[...], flat).astype(BF)


def run_middle(position, tokens, attended, gated, cotangent, gains, attn, ssm, gate, up, down):
    rows, width = tokens.shape
    half = width // 2
    hidden = gate[0].shape[1]
    count = hidden // CHUNK
    fixed = lambda shape: pl.BlockSpec(shape, lambda step, place: (0,) * len(shape))

    def chunk(step, place):
        first = step < count // 2
        return jnp.where(first, 1 - place[0], place[0]) * (count // 2) + step % (count // 2)

    sliding = pl.BlockSpec((half, CHUNK), lambda step, place: (0, chunk(step, place)))
    early = lambda step, place: (jnp.minimum(step, count // 2 - 1), 0)
    late = lambda step, place: (jnp.maximum(step - count // 2, 0), 0)
    wide = pl.BlockSpec((half, 2 * CHUNK), lambda step, place: (0, chunk(step, place)))
    low = lambda shape: jax.ShapeDtypeStruct(shape, BF)
    full = lambda shape: jax.ShapeDtypeStruct(shape, F32)
    return pl.pallas_call(
        middle_kernel,
        grid_spec=pltpu.PrefetchScalarGridSpec(
            num_scalar_prefetch=1,
            grid=(count,),
            in_specs=[
                *[fixed(item.shape) for item in (tokens, attended, gated, cotangent, gains)],
                *[fixed(item.shape) for item in (*attn, *ssm)],
                *[sliding] * 4,
                pl.BlockSpec((CHUNK, width), late),
                pl.BlockSpec((CHUNK, width), early),
            ],
            out_specs=[
                *[fixed((rows, width))] * 4,
                fixed(attended.shape),
                fixed(gated.shape),
                fixed((8, width)),
                pl.BlockSpec((CHUNK, width), early),
                pl.BlockSpec((CHUNK, width), late),
                wide,
                wide,
            ],
            scratch_shapes=[
                *[pltpu.VMEM((rows, width), F32)] * 3,
                pltpu.VMEM((rows, width), BF),
                pltpu.VMEM((width, rows), BF),
                *[pltpu.VMEM((rows, width), F32)] * 2,
            ],
        ),
        out_shape=[
            low((rows, width)),
            full((rows, width)),
            low((rows, width)),
            low((rows, width)),
            low(attended.shape),
            low(gated.shape),
            full((8, width)),
            low((hidden // 2, width)),
            low((hidden // 2, width)),
            low((half, 2 * hidden)),
            low((half, 2 * hidden)),
        ],
        compiler_params=params_of(LARGE_LIMIT),
        cost_estimate=LONG,
        name="middle",
    )(position, tokens, attended, gated, cotangent, gains, *attn, *ssm, *gate, *up, *down)


def outs_grads_kernel(
    position, attended, gated, normed, d_attn, d_ssm, d_gate, theirs, mine
):
    here = position[0]
    step = pl.program_id(0)
    which = jnp.where(step == 0, 1 - here, here)
    rows = theirs.shape[0]
    down = ((0,), (0,))

    def write(ref):
        at = 0
        for left, right in ((attended, d_attn), (gated, d_ssm), (normed, d_gate)):
            half = left.shape[1] // 2
            for begin in range(0, half, rows):
                turned = left[:, pl.ds(pl.multiple_of(which * half + begin, rows), rows)]
                ref[:, at : at + right.shape[1]] = dot(turned, right[...], down).astype(BF)
                at += right.shape[1]

    @pl.when(step == 0)
    def _():
        write(theirs)

    @pl.when(step == 1)
    def _():
        write(mine)


def run_outs_grads(position, attended, gated, normed, d_attn, d_ssm, d_gate):
    inputs = (attended, gated, normed, d_attn, d_ssm, d_gate)
    rows = attended.shape[1] // 2
    width = sum(
        left.shape[1] // 2 // rows * right.shape[1] for left, right in zip(inputs[:3], inputs[3:])
    )
    fixed = lambda shape: pl.BlockSpec(shape, lambda step, place: (0, 0))
    return pl.pallas_call(
        outs_grads_kernel,
        grid_spec=pltpu.PrefetchScalarGridSpec(
            num_scalar_prefetch=1,
            grid=(2,),
            in_specs=[fixed(item.shape) for item in inputs],
            out_specs=[fixed((rows, width))] * 2,
        ),
        out_shape=[jax.ShapeDtypeStruct((rows, width), BF)] * 2,
        compiler_params=params_of(),
        cost_estimate=COST,
        name="outs_grads",
    )(position, *inputs)


def early_back_kernel(
    position,
    d_query,
    d_kv,
    d_gate,
    query_mine,
    query_theirs,
    kv_mine,
    kv_theirs,
    ssm_mine,
    ssm_theirs,
    d_normed,
):
    here = position[0]
    half = d_normed.shape[1] // 2
    flat = ((1,), (1,))
    for which, query, kv, ssm in (
        (here, query_mine, kv_mine, ssm_mine),
        (1 - here, query_theirs, kv_theirs, ssm_theirs),
    ):
        d_normed[:, pl.ds(pl.multiple_of(which * half, half), half)] = (
            dot(d_query[...], query[...], flat)
            + dot(d_kv[...], kv[...], flat)
            + dot(d_gate[...], ssm[...], flat)
        )


def run_early_back(position, d_query, d_kv, d_gate, query, kv, ssm):
    rows = d_query.shape[0]
    half = query[0].shape[0]
    fixed = lambda shape: pl.BlockSpec(shape, lambda step, place: (0, 0))
    return pl.pallas_call(
        early_back_kernel,
        grid_spec=pltpu.PrefetchScalarGridSpec(
            num_scalar_prefetch=1,
            grid=(1,),
            in_specs=[
                *[fixed(item.shape) for item in (d_query, d_kv, d_gate, *query, *kv)],
                *[pl.BlockSpec((half, INNER), lambda step, place: (0, 1))] * 2,
            ],
            out_specs=fixed((rows, 2 * half)),
        ),
        out_shape=jax.ShapeDtypeStruct((rows, 2 * half), F32),
        compiler_params=params_of(),
        cost_estimate=COST,
        name="early_back",
    )(position, d_query, d_kv, d_gate, *query, *kv, *ssm)


def rest_grads_kernel(
    position, normed, d_query, d_kv, d_mixed, d_aux, gain_grads, d_heads, theirs, mine
):
    here = position[0]
    step = pl.program_id(0)
    half = normed.shape[1] // 2
    which = jnp.where(step == 0, 1 - here, here)
    turned = normed[:, pl.ds(pl.multiple_of(which * half, half), half)]

    def write(ref):
        at = 0
        for right in (d_query, d_kv, d_mixed):
            ref[:, at : at + right.shape[1]] = dot(turned, right[...], ((0,), (0,))).astype(BF)
            at += right.shape[1]
        gains = gain_grads[0:3, pl.ds(pl.multiple_of(which * half, half), half)]
        heads = jnp.concatenate([d_heads[0:1, :], d_heads[1:2, :]], axis=1)
        heads = jnp.concatenate([heads, jnp.zeros((1, half - heads.shape[1]), F32)], axis=1)
        before = 2 * STATE + SH
        columns = jnp.concatenate(
            [
                jnp.zeros((before, half), F32),
                gains,
                heads,
                jnp.zeros((d_aux.shape[1] - before - 4, half), F32),
            ]
        ).T
        ref[:, at:] = (dot(turned, d_aux[...], ((0,), (0,))) + columns).astype(BF)

    @pl.when(step == 0)
    def _():
        write(theirs)

    @pl.when(step == 1)
    def _():
        write(mine)


def run_rest_grads(position, *inputs):
    half = inputs[0].shape[1] // 2
    total = sum(item.shape[1] for item in inputs[1:5])
    fixed = lambda shape: pl.BlockSpec(shape, lambda step, place: (0, 0))
    return pl.pallas_call(
        rest_grads_kernel,
        grid_spec=pltpu.PrefetchScalarGridSpec(
            num_scalar_prefetch=1,
            grid=(2,),
            in_specs=[fixed(item.shape) for item in inputs],
            out_specs=[fixed((half, total))] * 2,
        ),
        out_shape=[jax.ShapeDtypeStruct((half, total), BF)] * 2,
        compiler_params=params_of(),
        cost_estimate=COST,
        name="rest_grads",
    )(position, *inputs)


def late_back_kernel(
    position,
    tokens,
    gains,
    d_middle,
    d_normed,
    d_mixed,
    d_aux,
    aux_mine,
    aux_theirs,
    ssm_mine,
    ssm_theirs,
    grad_tokens,
    total,
):
    here = position[0]
    half = tokens.shape[1] // 2
    for which, aux, ssm in ((here, aux_mine, ssm_mine), (1 - here, aux_theirs, ssm_theirs)):
        columns = pl.ds(pl.multiple_of(which * half, half), half)
        total[:, columns] = (
            d_normed[:, columns]
            + dot(d_mixed[...], ssm[...], ((1,), (1,)))
            + dot(d_aux[:, : aux.shape[0]], aux[...])
        )
    hidden = tokens[...].astype(F32)
    d_hidden, _ = norm_back(hidden, inverse_rms(hidden), gains[0:1], total[...])
    grad_tokens[...] = d_middle[...] + d_hidden


def run_late_back(position, tokens, gains, d_middle, d_normed, d_mixed, d_aux, aux, ssm):
    rows, width = tokens.shape
    half = width // 2
    fixed = lambda shape: pl.BlockSpec(shape, lambda step, place: (0, 0))
    inputs = (tokens, gains, d_middle, d_normed, d_mixed, d_aux, *aux)
    return pl.pallas_call(
        late_back_kernel,
        grid_spec=pltpu.PrefetchScalarGridSpec(
            num_scalar_prefetch=1,
            grid=(1,),
            in_specs=[
                *[fixed(item.shape) for item in inputs],
                *[pl.BlockSpec((half, INNER), lambda step, place: (0, 0))] * 2,
            ],
            out_specs=fixed((rows, width)),
            scratch_shapes=[pltpu.VMEM((rows, width), F32)],
        ),
        out_shape=jax.ShapeDtypeStruct((rows, width), F32),
        compiler_params=params_of(),
        cost_estimate=COST,
        name="late_back",
    )(position, *inputs, *ssm)


def local(
    tokens,
    cotangent,
    doc_blocks,
    gain_in,
    w_query,
    w_kv,
    w_attn_out,
    gain_attn,
    w_ssm_in,
    w_ssm_aux,
    dt_bias,
    decay_log,
    w_ssm_out,
    gain_ssm,
    gain_ff,
    w_gate,
    w_up,
    w_down,
):
    rows, width = tokens.shape
    half = width // 2
    position = lax.axis_index("shard")
    here = position.astype(jnp.int32).reshape(1)
    blocks_here = rows // BLOCK
    docs = doc_blocks[0]
    here_docs = lax.dynamic_slice_in_dim(docs, position * blocks_here, blocks_here, 0)
    prior_docs = jnp.where(position > 0, docs[:blocks_here], -1)
    earlier = jnp.concatenate([prior_docs[-1:], here_docs[:-1]])
    resets = (here_docs != earlier).astype(jnp.int32)
    key_docs = jnp.repeat(jnp.concatenate([prior_docs, here_docs]), BLOCK)
    bias = jnp.where(here_docs[:, None] == key_docs[None, :], 0.0, NEGATIVE)
    lane_pad = LANES - SH
    dt_row = jnp.pad(dt_bias, (0, lane_pad))[None]
    decay_row = jnp.pad(decay_log, (0, lane_pad))[None]

    gains = jnp.stack([gain_in, gain_attn, gain_ssm, gain_ff])
    gains_theirs = swap(gains)
    ssm_in = (w_ssm_in, swap(w_ssm_in))
    query = (w_query, swap(w_query))
    kv = (w_kv, swap(w_kv))
    aux_in = (w_ssm_aux.T, swap(w_ssm_aux.T))
    attn_out = (w_attn_out, swap(w_attn_out))
    ssm_back = (w_ssm_out, swap(w_ssm_out))
    gate = (w_gate, swap(w_gate))
    up = (w_up, swap(w_up))
    down = (w_down, swap(w_down))
    gains_all = jnp.pad(natural(gains, gains_theirs, position, 1).astype(F32), ((0, 4), (0, 0)))

    normed, scaled_queries, key_vals, aux, mixed, state_end = run_project(
        here, resets, tokens, gains_all, dt_row, decay_row, query, kv, aux_in, ssm_in
    )
    key_prior = lax.ppermute(key_vals, "shard", [(0, 1)])
    state_prior = lax.ppermute(state_end, "shard", [(0, 1)])
    attended, log_total = run_attend(scaled_queries, key_prior, key_vals, bias)
    ssm_out, gated, states = run_forward(resets, mixed, aux, dt_row, decay_row, state_prior)

    (
        output,
        d_middle,
        d_attn_low,
        d_ssm_low,
        d_attended,
        d_gated,
        gain_grads,
        down_theirs,
        down_mine,
        wide_theirs,
        wide_mine,
    ) = run_middle(
        here, tokens, attended, gated, cotangent, gains_all, attn_out, ssm_back, gate, up, down
    )
    sums = {
        "down": Stream([down_mine, swap(down_theirs)], WHOLE["down"], *LINKS["down"]),
        "wide": Stream([wide_mine, swap(wide_theirs)], WHOLE["wide"], *LINKS["wide"]),
    }
    token = wide_theirs
    made = {}
    outs_rows = w_attn_out.shape[0]
    full = lambda *shape: jax.ShapeDtypeStruct(shape, F32)
    ssm_pieces = w_ssm_out.shape[0] // outs_rows
    gate_at = width * (1 + ssm_pieces)
    aux_at = AUX_AT + INNER
    spare = aux_at + 2 * STATE + SH
    wide_pieces = [
        [
            (column, 2 * column + offset, 2 * column + offset + CHUNK)
            for column in range(0, w_gate.shape[1], CHUNK)
        ]
        for offset in (0, CHUNK)
    ]
    layouts = {
        "down": [(full(*w_down.shape), width, [(0, 0, width)])],
        "wide": [(full(half, w_gate.shape[1]), w_gate.shape[1], pieces) for pieces in wide_pieces],
        "outs": [
            (full(outs_rows, width), width, [(0, 0, width)]),
            (
                full(ssm_pieces, outs_rows, width),
                width,
                [(piece, width * (1 + piece), width * (2 + piece)) for piece in range(ssm_pieces)],
            ),
            (
                full(half // outs_rows, outs_rows, 2 * INNER),
                INNER,
                [
                    (piece, gate_at + INNER * piece, gate_at + INNER * (piece + 1))
                    for piece in range(half // outs_rows)
                ],
            ),
        ],
        "rest": [
            (full(half, KV_AT), KV_AT, [(0, 0, KV_AT)]),
            (full(half, AUX_AT - KV_AT), AUX_AT - KV_AT, [(0, KV_AT, AUX_AT)]),
            (full(spare - aux_at, half), 3 * LANES, [(TURNED, aux_at, spare)]),
            (full(8, half), 3 * LANES, [(TURNED, spare, spare + 8)]),
            (full(half, 2 * INNER), INNER, [(0, AUX_AT, aux_at)]),
        ],
    }
    def closed(value, number):
        if number + 1 == len(PLAN) or PLAN[number + 1] not in layouts:
            return value
        names = []
        for name in PLAN[number + 1 :]:
            if name not in layouts:
                break
            names.append(name)
        waits = [
            stream.latest()
            for name, stream in sums.items()
            if stream.steps
            and (name in names or stream.gone > 1 or (stream.gone == 1 and name == "down"))
        ]
        return fence(value, *waits)

    d_kv = None

    def key_grads(made_before):
        if made_before is not None:
            return made_before
        return (d_here + after(d_prior_got, token).astype(F32)).astype(BF)

    def go_on(name):
        nonlocal token
        stream = sums[name]
        stream.hold(token)
        if stream.steps:
            stream.prepare()
            token = stream.operand
            stream.go()
        elif name not in made:
            started = made["outs"][2].reshape(half, 2 * INNER) if name == "rest" else None
            weights = (w_query, w_kv, w_ssm_aux.T, None, w_ssm_in) if name == "rest" else ()
            made[name] = stream.finish(layouts[name], started, weights)
            token = made[name][0]

    for number, name in enumerate(PLAN):
        if name in layouts:
            go_on(name)
        elif name == "state":
            d_state_start, d_mixed_gate = run_state_back(
                resets, after(d_gated, token), mixed, aux, ssm_out, dt_row, decay_row
            )
            token = closed(d_state_start, number)
            d_state_end = lax.ppermute(token, "shard", [(1, 0)])
        elif name == "grads":
            outs_theirs, outs_mine = run_outs_grads(
                here, after(attended, token), gated, normed, d_attn_low, d_ssm_low, d_mixed_gate
            )
            token = closed(outs_theirs, number)
            sums["outs"] = Stream([outs_mine, swap(token)], WHOLE["outs"], *LINKS["outs"])
        elif name == "attend":
            d_query, d_prior, d_here = run_attend_back(
                scaled_queries, key_prior, key_vals, bias, log_total, after(d_attended, token)
            )
            token = closed(d_prior, number)
            d_prior_got = lax.ppermute(token, "shard", [(1, 0)])
        elif name == "scan":
            d_mixed, d_aux, d_heads = run_backward(
                resets,
                after(d_gated, token),
                mixed,
                aux,
                ssm_out,
                states,
                dt_row,
                decay_row,
                d_state_end,
            )
            token = d_heads = closed(d_heads, number)
        elif name == "sums":
            d_kv = key_grads(d_kv)
            rest_theirs, rest_mine = run_rest_grads(
                here, normed, d_query, d_kv, d_mixed, d_aux, gain_grads, d_heads
            )
            token = closed(rest_theirs, number)
            sums["rest"] = Stream([rest_mine, swap(token)], WHOLE["rest"], *LINKS["rest"])
        elif name == "early":
            d_kv = key_grads(d_kv)
            d_normed = run_early_back(
                here, after(d_query, token), d_kv, d_mixed_gate, query, kv, ssm_in
            )
            token = d_normed
        elif name == "late":
            grad_tokens = run_late_back(
                here,
                tokens,
                gains_all,
                d_middle,
                d_normed,
                d_mixed,
                after(d_aux, token),
                aux_in,
                ssm_in,
            )
            token = grad_tokens

    for name in layouts:
        while name not in made:
            go_on(name)
    (grad_down,) = made["down"]
    grad_gate, grad_up = made["wide"]
    grad_attn_out, grad_ssm_out, _ = made["outs"]
    grad_query, grad_kv, grad_aux, extras, grad_ssm_in, products = made["rest"]
    gate_products = jnp.sum(
        w_ssm_in[:, INNER:].astype(F32) * made["outs"][2].reshape(half, 2 * INNER)[:, INNER:], axis=1
    )
    grad_gain_in = (products[0] + gate_products) / gain_in.astype(F32)
    return (
        output,
        grad_tokens,
        grad_gain_in,
        grad_query,
        grad_kv,
        grad_attn_out,
        extras[0],
        grad_ssm_in,
        grad_aux.T,
        extras[3, :SH],
        extras[3, LANES : LANES + SH],
        grad_ssm_out.reshape(w_ssm_out.shape),
        extras[1],
        extras[2],
        grad_gate,
        grad_up,
        grad_down,
    )


def solution(mesh):
    halves = P("shard", None)
    half = P("shard")
    tokens = P(("rep", "shard"), None)
    return jax.shard_map(
        local,
        mesh=mesh,
        in_specs=(
            tokens,
            tokens,
            P("rep", None),
            half,
            halves,
            halves,
            halves,
            half,
            halves,
            halves,
            P(),
            P(),
            halves,
            half,
            half,
            halves,
            halves,
            halves,
        ),
        out_specs=(
            tokens,
            tokens,
            half,
            halves,
            halves,
            halves,
            half,
            halves,
            halves,
            P(),
            P(),
            halves,
            half,
            half,
            halves,
            halves,
            halves,
        ),
        check_vma=False,
    )
```

time: 530 us -> 398 us (0.75)
  waiting for transfers between devices: 168 us -> 113 us
  Pallas kernels: 184 us -> 143 us
  matrix products: 17.8 us -> 0 us
  starting transfers between devices: 57.3 us -> 41.9 us
  between operations: 14.6 us -> 1.55 us
  local copies, waits for them, and re-layouts: 36 us -> 45.8 us
    ppermute x32 -> x28, waiting for transfers between devices: 162 us -> 111 us  [the longest x26 109 us: go(): got = lax.ppermute(self.operand, ('rep', 'shard'), self.pairs(step))]
    unnamed x91 -> x156, local copies, waits for them, and re-layouts: 21.2 us -> 40.6 us
    dot_general x8 -> x0, matrix products: 17.8 us -> none  [dot(): lax.dot_general(left, right, (over, ((), ())), preferred_element_type=F32)]
    ppermute x32 -> x28, starting transfers between devices: 51.3 us -> 34 us  [the longest x26 26.9 us: go(): got = lax.ppermute(self.operand, ('rep', 'shard'), self.pairs(step))]
    pallas_call x5 -> x12, Pallas kernels: 55 us -> 38.1 us  [the longest x4 22 us: finish(): pl.pallas_call(functools.partial(finish_kernel, len(stacks), far, [cut fo...]
    convert_element_type x9 -> x20, other arithmetic: 20.5 us -> 35.8 us  [part(): return total.astype(BF)]
    pallas_call x1, Pallas kernels: 26 us -> 16.1 us  [run_backward(): pl.pallas_call(backward_kernel, grid=(count,), in_specs=[scalars(), pl.Bl...]
    concatenate x7 -> x0, local copies, waits for them, and re-layouts: 7.05 us -> none  [the longest x3 4.17 us: prepare(): self.stack = jnp.concatenate([self.stack, *self.got])]
  transfers between devices with their start and end apart: 47 -> 44, of which waited for: 17 -> 16; matrix products, arithmetic and copies ran while one was open for 14% -> 13% of each run, Pallas kernels for 24% -> 25%
where the time goes in v2:
time: 398 us; the launch traced here: 391 us
  Pallas kernels  143 us (36%)
  waiting for transfers between devices  113 us (28%)
  other arithmetic  46.4 us (12%)
  local copies, waits for them, and re-layouts  45.8 us (12%)
  starting transfers between devices  41.9 us (11%)
    ppermute x26, waiting for transfers between devices, go(): got = lax.ppermute(self.operand, ('rep', 'shard'), self.pairs(step))  109 us
    unnamed x156, local copies, waits for them, and re-layouts  40.6 us
    pallas_call x1, Pallas kernels, run_middle(): pl.pallas_call(middle_kernel, grid_spec=pltpu.PrefetchScalarGridSpec(num_...  39.9 us
    convert_element_type x20, other arithmetic, part(): return total.astype(BF)  35.8 us
    ppermute x26, starting transfers between devices, go(): got = lax.ppermute(self.operand, ('rep', 'shard'), self.pairs(step))  26.9 us
    pallas_call x4, Pallas kernels, finish(): pl.pallas_call(functools.partial(finish_kernel, len(stacks), far, [cut fo...  22 us
    pallas_call x1, Pallas kernels, run_backward(): pl.pallas_call(backward_kernel, grid=(count,), in_specs=[scalars(), pl.Bl...  16.1 us
    pallas_call x1, Pallas kernels, run_project(): pl.pallas_call(project_kernel, grid_spec=pltpu.PrefetchScalarGridSpec(num...  14 us
  transfers between devices with their start and end apart: 44, of which 16 were waited for; matrix products, arithmetic and copies ran while one was open for 13% of the time, Pallas kernels for 25%

profile of v2, /device:TPU:1, one launch (start us, length us, event | category | flops | bytes accessed | tf_op | source)
XLA Modules:
  0.0 391.4 jit_solution(4059842233827410191)
XLA Ops:
  13.5 14.0 %project.1 = (bf16[512,1024]{1,0:T(8,128)(2,1)}, bf16[512,512]{1,0:T(8,128)(2,1)S(1)}, bf16[512,256]{1,0:T(8,128)(2,1)S(1)}, f32[512,384]{1,0:T(8,128)S(1)}, bf1...) custom-call(s32[1]{0:T(128)} %bitcast.position, s32[4]{0:T(128)S(1)} %compare_convert_fusion.resets, ...), custom_call_target="tpu_custom_call" | custom-call | flops 15000000512 | bytes 1000000 | tf_op jit(solution)/shard_map/project/pallas_call | solution.py:955
  33.2 7.6 %attend.1 = (bf16[512,512]{1,0:T(8,128)(2,1)S(1)}, f32[512,8]{1,0:T(8,128)S(1)}) custom-call(bf16[512,512]{1,0:T(8,128)(2,1)S(1)} %get-tuple-element.99.q_ref, bf16[512,256]{1,0:T(8,128)(2,1)S(1)} %collective-permute-done.5.prior_ref, bf16[512,256]{1,0:T(8,128)(2,1)S(1)} %get-tuple-element.100.here_ref, f32[4,1024]{1,0:T(4,128)S(1)} %compare_select_fusion.bias_ref), custom_call_target="tpu_custom_call" | custom-call | flops 15000000512 | bytes 1000000 | tf_op jit(solution)/shard_map/attend/pallas_call | solution.py:531
  42.7 8.6 %ssm_forward.1 = (f32[512,1536]{1,0:T(8,128)S(1)}, bf16[512,1536]{1,0:T(8,128)(2,1)S(1)}, bf16[4,128,1536]{2,1,0:T(8,128)(2,1)S(1)}) custom-call(s32[4]{0:T(128)S(1)} %compare_convert_fusion.resets, bf16[512,3072]{1,0:T(8,128)(2,1)S(1)} %copy-done.1, bf16[512,3072]{1,0:T(8,128)(2,1)S(1)} %copy-done.1, f32[512,384]{1,0:T(8,128)S(1)} %get-tuple-element.103.aux, ...), custom_call_target="tpu_custom_call" | custom-call | flops 15000000512 | bytes 1000000 | tf_op jit(solution)/shard_map/ssm_forward/pallas_call | solution.py:348
  54.2 39.9 %middle.1 = (bf16[512,1024]{1,0:T(8,128)(2,1)}, f32[512,1024]{1,0:T(8,128)}, bf16[512,1024]{1,0:T(8,128)(2,1)S(1)}, bf16[512,1024]{1,0:T(8,128)(2,1)}, bf16[512,...) custom-call(s32[1]{0:T(128)} %bitcast.position, ...), custom_call_target="tpu_custom_call" | custom-call | flops 15000000512 | bytes 1000000 | tf_op jit(solution)/shard_map/middle/pallas_call | solution.py:1135
  102.1 5.1 %ssm_state_back.1 = (bf16[128,1536]{1,0:T(8,128)(2,1)S(1)}, bf16[512,1536]{1,0:T(8,128)(2,1)S(1)}) custom-call(s32[4]{0:T(128)S(1)} %compare_convert_fusion.resets, bf16[512,1536]{1,0:T(8,128)(2,1)S(1)} %copy-done.10, bf16[512,3072]{1,0:T(8,128)(2,1)S(1)} %copy-done.1, f32[512,384]{1,0:T(8,128)S(1)} %copy-done.20, f32[512,1536]{1,0:T(8,128)S(1)} %copy-done.3, ...), custom_call_target="tpu_custom_call" | custom-call | flops 1000000 | bytes 1000000 | tf_op jit(solution)/shard_map/ssm_state_back/pallas_call | solution.py:380
  111.2 2.7 collective-permute-start.13
  117.8 4.3 %outs_grads.1 = (bf16[256,7168]{1,0:T(8,128)(2,1)S(1)}, bf16[256,7168]{1,0:T(8,128)(2,1)S(1)}) custom-call(s32[1]{0:T(128)} %bitcast.position, bf16[512,512]{1,0:T(8,128)(2,1)S(1)} %copy-done.52, bf16[512,1536]{1,0:T(8,128)(2,1)S(1)} %copy-done.32, bf16[512,1024]{1,0:T(8,128)(2,1)S(1)} %copy-done.15, bf16[512,1024]{1,0:T(8,128)(2,1)S(1)} %copy-done.45, ...), custom_call_target="tpu_custom_call" | custom-call | flops 1000000 | bytes 1000000 | tf_op jit(solution)/shard_map/outs_grads/pallas_call | solution.py:1217
  127.2 4.3 %add_convert_fusion = bf16[256,4096]{1,0:T(8,128)(2,1)} fusion(bf16[512,4096]{1,0:T(8,128)(2,1)} %collective-permute-done.14.refs_2_, s32[]{:T(128)S(6)} %select_n.193, bf16[512,4096]{1,0:T(8,128)(2,1)} %get-tuple-element.118), kind=kLoop, calls=%fused_computation | loop fusion | flops 4194304 | bytes 6291460 | tf_op jit(solution)/shard_map/convert_element_type | solution.py:614
  139.3 3.7 add_convert_fusion.1
  151.2 16.1 %ssm_backward.1 = (bf16[512,1536]{1,0:T(8,128)(2,1)S(1)}, bf16[512,384]{1,0:T(8,128)(2,1)S(1)}, f32[8,128]{1,0:T(8,128)S(1)}) custom-call(s32[4]{0:T(128)S(1)} %copy-done.73, bf16[512,1536]{1,0:T(8,128)(2,1)S(1)} %copy-done.11, bf16[512,3072]{1,0:T(8,128)(2,1)S(1)} %copy-done.1, bf16[512,3072]{1,0:T(8,128)(2,1)S(1)} %copy-done.1, f32[512,384]{1,0:T(8,128)S(1)} %copy-done.21, ...), custom_call_target="tpu_custom_call" | custom-call | flops 1000000 | bytes 1000000 | tf_op jit(solution)/shard_map/ssm_backward/pallas_call | solution.py:408
  169.9 3.5 add_convert_fusion.3
  177.1 13.6 %attend_back.1 = (bf16[512,512]{1,0:T(8,128)(2,1)S(1)}, bf16[512,256]{1,0:T(8,128)(2,1)S(1)}, f32[512,256]{1,0:T(8,128)S(1)}) custom-call(bf16[512,512]{1,0:T(8,128)(2,1)S(1)} %copy-done.48, bf16[512,256]{1,0:T(8,128)(2,1)S(1)} %copy-done.59, bf16[512,256]{1,0:T(8,128)(2,1)S(1)} %copy-done.57, f32[4,1024]{1,0:T(4,128)S(1)} %compare_select_fusion.bias_ref, ...), custom_call_target="tpu_custom_call" | custom-call | flops 1000000 | bytes 1000000 | tf_op jit(solution)/shard_map/attend_back/pallas_call | solution.py:546
  190.8 5.0 %collective-permute-start.19 = (bf16[512,256]{1,0:T(8,128)(2,1)S(1)}, bf16[512,256]{1,0:T(8,128)(2,1)S(1)}, u32[]{:S(2)}, u32[]{:S(2)}) collective-permute-start(bf16[512,256]{1,0:T(8,128)(2,1)S(1)} %get-tuple-element.137), channel_id=1, source_target_pairs={{1,0},{3,2},{5,4},{7,6},{9,8},{11,10},{13,12},{15,14},{17,16},{19,... | collective-permute-start | bytes 786440 | tf_op jit(solution)/shard_map/ppermute | solution.py:1565
  197.0 3.7 rest_grads.1
  207.7 2.6 collective-permute-start.25
  217.5 3.7 early_back.1.d_normed
  221.2 11.5 %collective-permute-done.25 = bf16[64,7168]{1,0:T(8,128)(2,1)S(1)} collective-permute-done((bf16[64,7168]{1,0:T(8,128)(2,1)S(1)}, bf16[64,7168]{1,0:T(8,128)(2,1)S(1)}, u32[]{:S(2)}, u32[]{:S(2)}) %collective-permute-start.25) | collective-permute-done | bytes 917536 | tf_op jit(solution)/shard_map/ppermute | solution.py:644
  243.0 2.6 collective-permute-start.30
  250.6 11.5 %collective-permute-done.26 = bf16[64,4096]{1,0:T(8,128)(2,1)S(1)} collective-permute-done((bf16[64,4096]{1,0:T(8,128)(2,1)S(1)}, bf16[64,4096]{1,0:T(8,128)(2,1)S(1)}, u32[]{:S(2)}, u32[]{:S(2)}) %collective-permute-start.26) | collective-permute-done | bytes 524320 | tf_op jit(solution)/shard_map/ppermute | solution.py:644
  264.5 4.4 %late_back.1 = f32[512,1024]{1,0:T(8,128)} custom-call(s32[1]{0:T(128)} %bitcast.position, bf16[512,1024]{1,0:T(8,128)(2,1)S(1)} %copy-done.40, f32[8,1024]{1,0:T(8,128)S(1)} %copy-done.63, f32[512,1024]{1,0:T(8,128)S(1)} %copy-done.30, f32[512,1024]{1,0:T(8,128)S(1)} %early_back.1.d_normed, bf16[512,1536]{1,0:T(8,128)(2,1)S(1)} %copy-done.14, ...), custom_call_target="tpu_custom_call" | custom-call | flops 1000000 | bytes 1000000 | tf_op jit(solution)/shard_map/late_back/pallas_call | solution.py:1371
  270.2 17.2 %collective-permute-done.30 = bf16[128,2688]{1,0:T(8,128)(2,1)S(1)} collective-permute-done((bf16[128,2688]{1,0:T(8,128)(2,1)S(1)}, bf16[128,2688]{1,0:T(8,128)(2,1)S(1)}, u32[]{:S(2)}, u32[]{:S(2)}) %collective-permute-start.30) | collective-permute-done | bytes 688160 | tf_op jit(solution)/shard_map/ppermute | solution.py:644
  293.7 3.0 unpack.4
  296.8 3.0 collective-permute-done.32
  300.9 3.8 collective-permute-done.38
  304.8 17.7 %collective-permute-done.37 = bf16[128,4096]{1,0:T(8,128)(2,1)S(1)} collective-permute-done((bf16[128,4096]{1,0:T(8,128)(2,1)S(1)}, bf16[128,4096]{1,0:T(8,128)(2,1)S(1)}, u32[]{:S(2)}, u32[]{:S(2)}) %collective-permute-start.37) | collective-permute-done | bytes 1048608 | tf_op jit(solution)/shard_map/ppermute | solution.py:644
  325.1 10.7 %collective-permute-done.41 = bf16[64,7168]{1,0:T(8,128)(2,1)S(1)} collective-permute-done((bf16[64,7168]{1,0:T(8,128)(2,1)S(1)}, bf16[64,7168]{1,0:T(8,128)(2,1)S(1)}, u32[]{:S(2)}, u32[]{:S(2)}) %collective-permute-start.41) | collective-permute-done | bytes 917536 | tf_op jit(solution)/shard_map/ppermute | solution.py:644
  337.3 19.6 %collective-permute-done.40.refs_1_ = bf16[256,4096]{1,0:T(8,128)(2,1)} collective-permute-done((bf16[256,4096]{1,0:T(8,128)(2,1)}, bf16[256,4096]{1,0:T(8,128)(2,1)}, u32[]{:S(2)}, u32[]{:S(2)}) %collective-permute-start.40) | collective-permute-done | bytes 2097184 | tf_op jit(solution)/shard_map/ppermute | solution.py:644
  356.8 6.9 %unpack.5 = (f32[512,2048]{1,0:T(8,128)}, f32[512,2048]{1,0:T(8,128)}) custom-call(s32[5]{0:T(128)S(1)} %get-tuple-element.189.places, bf16[256,4096]{1,0:T(8,128)(2,1)} %pad_maximum_fusion.refs_0_, bf16[256,4096]{1,0:T(8,128)(2,1)} %collective-permute-done.40.refs_1_), custom_call_target="tpu_custom_call" | custom-call | flops 1000000 | bytes 1000000 | tf_op jit(solution)/shard_map/unpack/pallas_call | solution.py:751
  366.5 3.5 collective-permute-done.43.refs_1_
  370.0 6.3 %unpack.6 = (f32[256,1024]{1,0:T(8,128)}, f32[3,256,1024]{2,1,0:T(8,128)}, f32[2,256,3072]{2,1,0:T(8,128)}) custom-call(s32[5]{0:T(128)S(1)} %pad_add_fusion.4.places, bf16[128,7168]{1,0:T(8,128)(2,1)} %pad_maximum_fusion.1.refs_0_, bf16[128,7168]{1,0:T(8,128)(2,1)} %collective-permute-done.43.refs_1_), custom_call_target="tpu_custom_call" | custom-call | flops 1000000 | bytes 1000000 | tf_op jit(solution)/shard_map/unpack/pallas_call | solution.py:751
  378.6 5.2 %collective-permute-done.42.refs_1_ = bf16[256,2688]{1,0:T(8,128)(2,1)} collective-permute-done((bf16[256,2688]{1,0:T(8,128)(2,1)}, bf16[256,2688]{1,0:T(8,128)(2,1)}, u32[]{:S(2)}, u32[]{:S(2)}) %collective-permute-start.42) | collective-permute-done | bytes 1376288 | tf_op jit(solution)/shard_map/ppermute | solution.py:644
  383.7 5.8 %unpack.7 = (f32[512,512]{1,0:T(8,128)}, f32[512,256]{1,0:T(8,128)}, f32[280,512]{1,0:T(8,128)}, f32[8,512]{1,0:T(8,128)S(1)}, f32[512,3072]{1,0:T(8,128)}, /*index=5*/f32[8,512]{1,0:T(8,128)S(1)}) custom-call(s32[5]{0:T(128)S(1)} %get-tuple-element.188.places, bf16[256,2688]{1,0:T(8,128)(2,1)} %pad_maximum_fusion.2.refs_0_, ...), custom_call_target="tpu_custom_call", output_to_operand_aliasing={{4}: (7, {})} | custom-call | flops 1000000 | bytes 1000000 | tf_op jit(solution)/shard_map/unpack/pallas_call | solution.py:751
  (285 shorter events, 118.8 us)
Async XLA Ops:
  7.5 46.7 %collective-permute-start.10 = (bf16[512,2048]{1,0:T(8,128)(2,1)}, bf16[512,2048]{1,0:T(8,128)(2,1)}, u32[]{:S(2)}, u32[]{:S(2)}) collective-permute-start(bf16[512,2048]{1,0:T(8,128)(2,1)} %up_mine.1), channel_id=1, source_target_pairs={{0,1},{1,0},{2,3},{3,2},{4,5},{5,4},{6,7},{7,6},{8,9},{9,8},{10,11... | collective-permute-start | bytes 6291464 | tf_op jit(solution)/shard_map/ppermute | solution.py:561
  8.3 46.0 %collective-permute-start.11 = (bf16[1024,1024]{1,0:T(8,128)(2,1)}, bf16[1024,1024]{1,0:T(8,128)(2,1)}, u32[]{:S(2)}, u32[]{:S(2)}) collective-permute-start(bf16[1024,1024]{1,0:T(8,128)(2,1)} %down_mine.1), channel_id=1, source_target_pairs={{0,1},{1,0},{2,3},{3,2},{4,5},{5,4},{6,7},{7,6},{8,9},{9,8},{10,11... | collective-permute-start | bytes 6291464 | tf_op jit(solution)/shard_map/ppermute | solution.py:561
  8.4 45.8 %collective-permute-start.9 = (bf16[512,2048]{1,0:T(8,128)(2,1)}, bf16[512,2048]{1,0:T(8,128)(2,1)}, u32[]{:S(2)}, u32[]{:S(2)}) collective-permute-start(bf16[512,2048]{1,0:T(8,128)(2,1)} %gate_mine.1), channel_id=1, source_target_pairs={{0,1},{1,0},{2,3},{3,2},{4,5},{5,4},{6,7},{7,6},{8,9},{9,8},{10,11... | collective-permute-start | bytes 6291464 | tf_op jit(solution)/shard_map/ppermute | solution.py:561
  8.8 45.4 %collective-permute-start.8 = (bf16[768,1024]{1,0:T(8,128)(2,1)}, bf16[768,1024]{1,0:T(8,128)(2,1)}, u32[]{:S(2)}, u32[]{:S(2)}) collective-permute-start(bf16[768,1024]{1,0:T(8,128)(2,1)} %ssm_mine.5), channel_id=1, source_target_pairs={{0,1},{1,0},{2,3},{3,2},{4,5},{5,4},{6,7},{7,6},{8,9},{9,8},{10,11... | collective-permute-start | bytes 4718600 | tf_op jit(solution)/shard_map/ppermute | solution.py:561
  41.5 12.7 %collective-permute-start.7 = (bf16[256,1024]{1,0:T(8,128)(2,1)S(1)}, bf16[256,1024]{1,0:T(8,128)(2,1)S(1)}, u32[]{:S(2)}, u32[]{:S(2)}) collective-permute-start(bf16[256,1024]{1,0:T(8,128)(2,1)S(1)} %copy-done.74), channel_id=1, source_target_pairs={{0,1},{1,0},{2,3},{3,2},{4,5},{5,4},{6,7},{7,6},{8,9},{9,8},{10,11... | collective-permute-start | bytes 1572872 | tf_op jit(solution)/shard_map/ppermute | solution.py:561
  97.2 29.3 %collective-permute-start.14 = (bf16[512,4096]{1,0:T(8,128)(2,1)}, bf16[512,4096]{1,0:T(8,128)(2,1)}, u32[]{:S(2)}, u32[]{:S(2)}) collective-permute-start(bf16[512,4096]{1,0:T(8,128)(2,1)} %get-tuple-element.113), channel_id=1, source_target_pairs={{0,1},{1,0},{2,3},{3,2},{4,5},{5,4},{6,7},{7,6},{8,9},{9,8},{10,11... | collective-permute-start | bytes 12582920 | tf_op jit(solution)/shard_map/ppermute | solution.py:561
  111.2 15.3 %collective-permute-start.13 = (bf16[512,1024]{1,0:T(8,128)(2,1)S(1)}, bf16[512,1024]{1,0:T(8,128)(2,1)}, u32[]{:S(2)}, u32[]{:S(2)}) collective-permute-start(bf16[512,1024]{1,0:T(8,128)(2,1)S(1)} %add_convert_fusion.4), channel_id=1, source_target_pairs={{0,2},{1,5},{2,0},{3,7},{4,6},{5,1},{6,4},{7,3},{8,10},{9,13},{10,... | collective-permute-start | bytes 3145736 | tf_op jit(solution)/shard_map/ppermute | solution.py:644
  126.5 12.8 %collective-permute-start.17 = (bf16[256,7168]{1,0:T(8,128)(2,1)}, bf16[256,7168]{1,0:T(8,128)(2,1)}, u32[]{:S(2)}, u32[]{:S(2)}) collective-permute-start(bf16[256,7168]{1,0:T(8,128)(2,1)} %fence.5), channel_id=1, source_target_pairs={{0,1},{1,0},{2,3},{3,2},{4,5},{5,4},{6,7},{7,6},{8,9},{9,8},{10,11... | collective-permute-start | bytes 11010056 | tf_op jit(solution)/shard_map/ppermute | solution.py:561
  131.5 38.4 %collective-permute-start.16 = (bf16[256,4096]{1,0:T(8,128)(2,1)}, bf16[256,4096]{1,0:T(8,128)(2,1)}, u32[]{:S(2)}, u32[]{:S(2)}) collective-permute-start(bf16[256,4096]{1,0:T(8,128)(2,1)} %add_convert_fusion), channel_id=1, source_target_pairs={{0,2},{1,5},{2,0},{3,7},{4,6},{5,1},{6,4},{7,3},{8,10},{9,13},{10,... | collective-permute-start | bytes 6291464 | tf_op jit(solution)/shard_map/ppermute | solution.py:644
  138.0 31.9 %collective-permute-start.15 = (bf16[256,1024]{1,0:T(8,128)(2,1)}, bf16[256,1024]{1,0:T(8,128)(2,1)}, u32[]{:S(2)}, u32[]{:S(2)}) collective-permute-start(bf16[256,1024]{1,0:T(8,128)(2,1)} %add_convert_fusion.16), channel_id=1, source_target_pairs={{0,8},{1,9},{2,10},{3,11},{4,12},{5,13},{6,14},{7,15},{8,0},{9,1},... | collective-permute-start | bytes 1572872 | tf_op jit(solution)/shard_map/ppermute | solution.py:644
  143.0 61.6 %collective-permute-start.22 = (bf16[128,7168]{1,0:T(8,128)(2,1)}, bf16[128,7168]{1,0:T(8,128)(2,1)}, u32[]{:S(2)}, u32[]{:S(2)}) collective-permute-start(bf16[128,7168]{1,0:T(8,128)(2,1)} %add_convert_fusion.1), channel_id=1, source_target_pairs={{0,8},{1,3},{2,10},{3,1},{4,12},{5,7},{6,14},{7,5},{8,0},{9,11},{1... | collective-permute-start | bytes 5505032 | tf_op jit(solution)/shard_map/ppermute | solution.py:644
  173.5 31.1 %collective-permute-start.21 = (bf16[128,4096]{1,0:T(8,128)(2,1)}, bf16[128,4096]{1,0:T(8,128)(2,1)}, u32[]{:S(2)}, u32[]{:S(2)}) collective-permute-start(bf16[128,4096]{1,0:T(8,128)(2,1)} %add_convert_fusion.3), channel_id=1, source_target_pairs={{0,4},{1,9},{2,6},{3,11},{4,0},{5,13},{6,2},{7,15},{8,12},{9,1},{1... | collective-permute-start | bytes 3145736 | tf_op jit(solution)/shard_map/ppermute | solution.py:644
  176.0 27.9 %collective-permute-start.20 = (bf16[256,1024]{1,0:T(8,128)(2,1)S(1)}, bf16[256,1024]{1,0:T(8,128)(2,1)S(1)}, u32[]{:S(2)}, u32[]{:S(2)}) collective-permute-start(bf16[256,1024]{1,0:T(8,128)(2,1)S(1)} %add_convert_fusion.15), channel_id=1, source_target_pairs={{0,16},{1,3},{2,18},{3,1},{4,20},{5,7},{6,22},{7,5},{8,24},{9,11},... | collective-permute-start | bytes 1572872 | tf_op jit(solution)/shard_map/ppermute | solution.py:644
  207.7 25.0 %collective-permute-start.25 = (bf16[64,7168]{1,0:T(8,128)(2,1)S(1)}, bf16[64,7168]{1,0:T(8,128)(2,1)S(1)}, u32[]{:S(2)}, u32[]{:S(2)}) collective-permute-start(bf16[64,7168]{1,0:T(8,128)(2,1)S(1)} %add_convert_fusion.5), channel_id=1, source_target_pairs={{0,4},{1,9},{2,6},{3,11},{4,0},{5,13},{6,2},{7,15},{8,12},{9,1},{1... | collective-permute-start | bytes 2752520 | tf_op jit(solution)/shard_map/ppermute | solution.py:644
  212.5 22.1 %collective-permute-start.24 = (bf16[64,4096]{1,0:T(8,128)(2,1)S(1)}, bf16[64,4096]{1,0:T(8,128)(2,1)S(1)}, u32[]{:S(2)}, u32[]{:S(2)}) collective-permute-start(bf16[64,4096]{1,0:T(8,128)(2,1)S(1)} %add_convert_fusion.14), channel_id=1, source_target_pairs={{0,8},{1,3},{2,10},{3,1},{4,12},{5,7},{6,14},{7,5},{8,0},{9,11},{1... | collective-permute-start | bytes 1572872 | tf_op jit(solution)/shard_map/ppermute | solution.py:644
  214.9 22.0 %collective-permute-start.29 = (bf16[256,1024]{1,0:T(8,128)(2,1)S(1)}, bf16[256,1024]{1,0:T(8,128)(2,1)S(1)}, u32[]{:S(2)}, u32[]{:S(2)}) collective-permute-start(bf16[256,1024]{1,0:T(8,128)(2,1)S(1)} %add_convert_fusion.13), channel_id=1, source_target_pairs={{0,4},{1,17},{2,6},{3,19},{4,0},{5,21},{6,2},{7,23},{8,12},{9,25},... | collective-permute-start | bytes 1572872 | tf_op jit(solution)/shard_map/ppermute | solution.py:644
  216.8 24.5 %collective-permute-start.28 = (bf16[256,2688]{1,0:T(8,128)(2,1)S(1)}, bf16[256,2688]{1,0:T(8,128)(2,1)S(1)}, u32[]{:S(2)}, u32[]{:S(2)}) collective-permute-start(bf16[256,2688]{1,0:T(8,128)(2,1)S(1)} %add_convert_fusion.2), channel_id=1, source_target_pairs={{0,2},{1,5},{2,0},{3,7},{4,6},{5,1},{6,4},{7,3},{8,10},{9,13},{10,... | collective-permute-start | bytes 4128776 | tf_op jit(solution)/shard_map/ppermute | solution.py:644
  234.5 13.5 %collective-permute-start.27 = (bf16[32,7168]{1,0:T(8,128)(2,1)S(1)}, bf16[32,7168]{1,0:T(8,128)(2,1)S(1)}, u32[]{:S(2)}, u32[]{:S(2)}) collective-permute-start(bf16[32,7168]{1,0:T(8,128)(2,1)S(1)} %add_convert_fusion.19), channel_id=1, source_target_pairs={{0,2},{1,5},{2,0},{3,7},{4,6},{5,1},{6,4},{7,3},{8,10},{9,13},{10,... | collective-permute-start | bytes 1376264 | tf_op jit(solution)/shard_map/ppermute | solution.py:644
  236.7 25.4 %collective-permute-start.26 = (bf16[64,4096]{1,0:T(8,128)(2,1)S(1)}, bf16[64,4096]{1,0:T(8,128)(2,1)S(1)}, u32[]{:S(2)}, u32[]{:S(2)}) collective-permute-start(bf16[64,4096]{1,0:T(8,128)(2,1)S(1)} %add_convert_fusion.12), channel_id=1, source_target_pairs={{0,16},{1,17},{2,18},{3,19},{4,20},{5,21},{6,22},{7,23},{8,24},{9,... | collective-permute-start | bytes 1572872 | tf_op jit(solution)/shard_map/ppermute | solution.py:644
  237.0 31.8 %collective-permute-start.31 = (bf16[256,1024]{1,0:T(8,128)(2,1)S(1)}, bf16[256,1024]{1,0:T(8,128)(2,1)S(1)}, u32[]{:S(2)}, u32[]{:S(2)}) collective-permute-start(bf16[256,1024]{1,0:T(8,128)(2,1)S(1)} %add_convert_fusion.11), channel_id=1, source_target_pairs={{0,8},{1,9},{2,10},{3,11},{4,12},{5,13},{6,14},{7,15},{8,0},{9,1},... | collective-permute-start | bytes 1572872 | tf_op jit(solution)/shard_map/ppermute | solution.py:644
  243.0 44.4 %collective-permute-start.30 = (bf16[128,2688]{1,0:T(8,128)(2,1)S(1)}, bf16[128,2688]{1,0:T(8,128)(2,1)S(1)}, u32[]{:S(2)}, u32[]{:S(2)}) collective-permute-start(bf16[128,2688]{1,0:T(8,128)(2,1)S(1)} %add_convert_fusion.9), channel_id=1, source_target_pairs={{0,4},{1,9},{2,6},{3,11},{4,0},{5,13},{6,2},{7,15},{8,12},{9,1},{1... | collective-permute-start | bytes 2064392 | tf_op jit(solution)/shard_map/ppermute | solution.py:644
  249.9 41.3 %collective-permute-start.35 = (bf16[32,7168]{1,0:T(8,128)(2,1)S(1)}, bf16[32,7168]{1,0:T(8,128)(2,1)S(1)}, u32[]{:S(2)}, u32[]{:S(2)}) collective-permute-start(bf16[32,7168]{1,0:T(8,128)(2,1)S(1)} %add_convert_fusion.18), channel_id=1, source_target_pairs={{0,16},{1,17},{2,18},{3,19},{4,20},{5,21},{6,22},{7,23},{8,24},{9,... | collective-permute-start | bytes 1376264 | tf_op jit(solution)/shard_map/ppermute | solution.py:644
  262.3 31.3 %collective-permute-start.34 = (bf16[64,4096]{1,0:T(8,128)(2,1)S(1)}, bf16[64,4096]{1,0:T(8,128)(2,1)S(1)}, u32[]{:S(2)}, u32[]{:S(2)}) collective-permute-start(bf16[64,4096]{1,0:T(8,128)(2,1)S(1)} %add_convert_fusion.10), channel_id=1, source_target_pairs={{0,8},{1,3},{2,10},{3,1},{4,12},{5,7},{6,14},{7,5},{8,0},{9,11},{1... | collective-permute-start | bytes 1572872 | tf_op jit(solution)/shard_map/ppermute | solution.py:644
  268.9 24.8 %collective-permute-start.33 = (bf16[512,1024]{1,0:T(8,128)(2,1)S(1)}, bf16[512,1024]{1,0:T(8,128)(2,1)S(1)}, u32[]{:S(2)}, u32[]{:S(2)}) collective-permute-start(bf16[512,1024]{1,0:T(8,128)(2,1)S(1)} %pad_maximum_fusion.3.refs_0_), channel_id=1, source_target_pairs={{0,2},{1,5},{2,0},{3,7},{4,6},{5,1},{6,4},{7,3},{8,10},{9,13},{10,... | collective-permute-start | bytes 3145736 | tf_op jit(solution)/shard_map/ppermute | solution.py:644
  291.3 13.4 %collective-permute-start.38 = (bf16[32,7168]{1,0:T(8,128)(2,1)S(1)}, bf16[32,7168]{1,0:T(8,128)(2,1)S(1)}, u32[]{:S(2)}, u32[]{:S(2)}) collective-permute-start(bf16[32,7168]{1,0:T(8,128)(2,1)S(1)} %add_convert_fusion.17), channel_id=1, source_target_pairs={{0,2},{1,5},{2,0},{3,7},{4,6},{5,1},{6,4},{7,3},{8,10},{9,13},{10,... | collective-permute-start | bytes 1376264 | tf_op jit(solution)/shard_map/ppermute | solution.py:644
  293.7 28.9 %collective-permute-start.37 = (bf16[128,4096]{1,0:T(8,128)(2,1)S(1)}, bf16[128,4096]{1,0:T(8,128)(2,1)S(1)}, u32[]{:S(2)}, u32[]{:S(2)}) collective-permute-start(bf16[128,4096]{1,0:T(8,128)(2,1)S(1)} %pad_maximum_fusion.4), channel_id=1, source_target_pairs={{0,4},{1,9},{2,6},{3,11},{4,0},{5,13},{6,2},{7,15},{8,12},{9,1},{1... | collective-permute-start | bytes 3145736 | tf_op jit(solution)/shard_map/ppermute | solution.py:644
  299.9 24.1 %collective-permute-start.36 = (bf16[128,2688]{1,0:T(8,128)(2,1)S(1)}, bf16[128,2688]{1,0:T(8,128)(2,1)S(1)}, u32[]{:S(2)}, u32[]{:S(2)}) collective-permute-start(bf16[128,2688]{1,0:T(8,128)(2,1)S(1)} %add_convert_fusion.7), channel_id=1, source_target_pairs={{0,8},{1,17},{2,10},{3,19},{4,12},{5,21},{6,14},{7,23},{8,0},{9,25... | collective-permute-start | bytes 2064392 | tf_op jit(solution)/shard_map/ppermute | solution.py:644
  304.8 31.0 %collective-permute-start.41 = (bf16[64,7168]{1,0:T(8,128)(2,1)S(1)}, bf16[64,7168]{1,0:T(8,128)(2,1)S(1)}, u32[]{:S(2)}, u32[]{:S(2)}) collective-permute-start(bf16[64,7168]{1,0:T(8,128)(2,1)S(1)} %pad_maximum_fusion.5), channel_id=1, source_target_pairs={{0,4},{1,9},{2,6},{3,11},{4,0},{5,13},{6,2},{7,15},{8,12},{9,1},{1... | collective-permute-start | bytes 2752520 | tf_op jit(solution)/shard_map/ppermute | solution.py:644
  324.1 32.8 %collective-permute-start.40 = (bf16[256,4096]{1,0:T(8,128)(2,1)}, bf16[256,4096]{1,0:T(8,128)(2,1)}, u32[]{:S(2)}, u32[]{:S(2)}) collective-permute-start(bf16[256,4096]{1,0:T(8,128)(2,1)} %pad_maximum_fusion.refs_0_), channel_id=1, source_target_pairs={{0,2},{1,5},{2,0},{3,7},{4,6},{5,1},{6,4},{7,3},{8,10},{9,13},{10,... | collective-permute-start | bytes 6291464 | tf_op jit(solution)/shard_map/ppermute | solution.py:644
  325.1 38.7 %collective-permute-start.39 = (bf16[128,2688]{1,0:T(8,128)(2,1)}, bf16[128,2688]{1,0:T(8,128)(2,1)}, u32[]{:S(2)}, u32[]{:S(2)}) collective-permute-start(bf16[128,2688]{1,0:T(8,128)(2,1)} %add_convert_fusion.6), channel_id=1, source_target_pairs={{0,4},{1,9},{2,6},{3,11},{4,0},{5,13},{6,2},{7,15},{8,12},{9,1},{1... | collective-permute-start | bytes 2064392 | tf_op jit(solution)/shard_map/ppermute | solution.py:644
  337.2 32.8 %collective-permute-start.43 = (bf16[128,7168]{1,0:T(8,128)(2,1)}, bf16[128,7168]{1,0:T(8,128)(2,1)}, u32[]{:S(2)}, u32[]{:S(2)}) collective-permute-start(bf16[128,7168]{1,0:T(8,128)(2,1)} %pad_maximum_fusion.1.refs_0_), channel_id=1, source_target_pairs={{0,8},{1,3},{2,10},{3,1},{4,12},{5,7},{6,14},{7,5},{8,0},{9,11},{1... | collective-permute-start | bytes 5505032 | tf_op jit(solution)/shard_map/ppermute | solution.py:644
  366.2 17.5 %collective-permute-start.42 = (bf16[256,2688]{1,0:T(8,128)(2,1)}, bf16[256,2688]{1,0:T(8,128)(2,1)}, u32[]{:S(2)}, u32[]{:S(2)}) collective-permute-start(bf16[256,2688]{1,0:T(8,128)(2,1)} %pad_maximum_fusion.2.refs_0_), channel_id=1, source_target_pairs={{0,2},{1,5},{2,0},{3,7},{4,6},{5,1},{6,4},{7,3},{8,10},{9,13},{10,... | collective-permute-start | bytes 4128776 | tf_op jit(solution)/shard_map/ppermute | solution.py:644
  (90 other events, 904.0 us)

commit v3 on v2

--- a/solution.py
+++ b/solution.py
@@ -21,46 +21,46 @@
 TURNED = -1
 WHOLE = {"down": 2, "wide": 1, "outs": 1, "rest": 2}
 LINKS = {
-    "down": ((X, Z, ZZ, Y), (Y, Z, X, ZZ)),
-    "wide": ((X, Y, Z, ZZ), (Y, Z, X, ZZ)),
-    "outs": ((Z, Y, X, ZZ), (X, Z, Y, ZZ)),
-    "rest": ((X, Y, ZZ, Z), (Y, Z, X, ZZ)),
+    "down": ((Z, Y, ZZ, X), (Z, X, Y, ZZ)),
+    "wide": ((X, Y, ZZ, Z), (Y, X, Z, ZZ)),
+    "outs": ((Z, Y, X, ZZ), (Y, X, Z, ZZ)),
+    "rest": ((X, Z, Y, ZZ), (Y, X, Z, ZZ)),
 }
 PLAN = (
     "state",
+    "wide",
     "down",
     "grads",
+    "scan",
     "wide",
     "down",
     "outs",
-    "scan",
+    "attend",
     "wide",
+    "sums",
+    "early",
     "down",
-    "attend",
-    "sums",
-    "outs",
-    "wide",
-    "down",
-    "rest",
-    "early",
-    "outs",
-    "wide",
-    "down",
-    "rest",
-    "outs",
-    "wide",
-    "late",
-    "down",
-    "rest",
-    "outs",
-    "wide",
-    "down",
-    "rest",
     "outs",
     "wide",
     "rest",
+    "down",
     "outs",
     "wide",
+    "rest",
+    "down",
+    "outs",
+    "wide",
+    "rest",
+    "down",
+    "outs",
+    "wide",
+    "rest",
+    "down",
+    "outs",
+    "late",
+    "wide",
+    "rest",
+    "outs",
     "rest",
     "outs",
     "rest",
@@ -73,6 +73,7 @@
 SWAP = [(0, 1), (1, 0)]
 VMEM_LIMIT = 30 * 1024 * 1024
 LARGE_LIMIT = 50 * 1024 * 1024
+WHOLE_LIMIT = 60 * 1024 * 1024
 LONG = pl.CostEstimate(flops=15_000_000_000, bytes_accessed=1_000_000, transcendentals=0)
 COST = pl.CostEstimate(flops=1_000_000, bytes_accessed=1_000_000, transcendentals=0)
 
@@ -395,7 +396,7 @@
             jax.ShapeDtypeStruct((mixed.shape[0], INNER), BF),
         ],
         scratch_shapes=[pltpu.VMEM((STATE, INNER), F32)],
-        compiler_params=params_of(),
+        compiler_params=params_of(WHOLE_LIMIT),
         cost_estimate=COST,
         name="ssm_state_back",
     )(resets, d_gated, mixed, aux, ssm_out, dt_bias, decay_log)
@@ -659,7 +660,7 @@
             block = 2 * block + side
         return block.astype(jnp.int32)
 
-    def finish(self, outputs, started=None, weights=()):
+    def finish(self, outputs, started=None, weights=(), part=None, before=()):
         if self.stack is None:
             self.stack = self.part(0, self.terms[0].shape[0])
         stacks = [self.stack] if self.got is None else [self.stack, self.got]
@@ -670,6 +671,12 @@
         size = stacks[0].shape[0] // each // far
         width = stacks[0].shape[1]
         own = self.own()
+        numbers = jnp.arange(quarters, dtype=jnp.int32)
+        if part is not None:
+            if size % 16:
+                return None
+            stacks = stacks[part : part + 1]
+            numbers = numbers[each * part : each * (part + 1)]
         if size % 16:
             flat = jnp.concatenate(stacks).reshape(blocks, size, width)
             flat = jnp.zeros_like(flat).at[jnp.arange(blocks) ^ own].set(flat).reshape(-1, width)
@@ -679,12 +686,7 @@
                 if pieces[0][0] == TURNED:
                     made.append(cuts[0].T)
                     continue
-                whole_width = shape.shape[-1]
-                if len(shape.shape) == 3:
-                    value = jnp.stack(cuts)
-                    value = jnp.pad(value, ((0, 0), (0, 0), (whole_width - value.shape[-1], 0)))
-                else:
-                    value = jnp.concatenate(cuts, axis=1)
+                value = jnp.stack(cuts) if len(shape.shape) == 3 else jnp.concatenate(cuts, axis=1)
                 made.append(value)
             products = [
                 jnp.sum(
@@ -694,8 +696,13 @@
                 for value, weight, (_, _, pieces) in zip(made, weights, outputs)
                 if weight is not None
             ]
-            if started is not None:
-                made[-1] = jnp.concatenate([made[-1], started[:, made[-1].shape[1] :]], axis=1)
+            spare = outputs[-1][0].shape[-1] - made[-1].shape[-1]
+            if spare:
+                left = made[-1].ndim == 3
+                other = jnp.zeros(made[-1].shape[:-1] + (spare,), F32)
+                if started is not None:
+                    other = started[..., :spare] if left else started[..., -spare:]
+                made[-1] = jnp.concatenate([other, made[-1]] if left else [made[-1], other], axis=-1)
             if products:
                 made.append(jnp.broadcast_to(sum(products), (8, products[0].shape[0])))
             return made
@@ -741,13 +748,14 @@
             out_specs.append(pl.BlockSpec((8, rows), lambda step, places: (0, places[step])))
             shapes.append(jax.ShapeDtypeStruct((8, rows * quarters), F32))
         aliases = {}
-        if started is not None:
+        if part != 1 and started is not None:
+            before = [started]
             aliases = {1 + len(inputs): len(outputs) - 1}
-            inputs.append(started)
-            in_specs.append(pl.BlockSpec(memory_space=pl.ANY))
-        places = jnp.concatenate(
-            [jnp.arange(quarters, dtype=jnp.int32) ^ (own // far), (own % far).reshape(1)]
-        )
+        elif part == 1:
+            aliases = {1 + len(inputs) + number: number for number in range(len(shapes))}
+        inputs += before
+        in_specs += [pl.BlockSpec(memory_space=pl.ANY)] * len(before)
+        places = jnp.concatenate([numbers ^ (own // far), (own % far).reshape(1)])
         return pl.pallas_call(
             functools.partial(
                 finish_kernel,
@@ -758,7 +766,7 @@
             ),
             grid_spec=pltpu.PrefetchScalarGridSpec(
                 num_scalar_prefetch=1,
-                grid=(quarters,),
+                grid=numbers.shape,
                 in_specs=in_specs,
                 out_specs=out_specs,
                 scratch_shapes=scratch,
@@ -871,9 +879,8 @@
     )
 
 
-def project_kernel(
+def project_small_kernel(
     position,
-    resets,
     tokens,
     gains,
     dt_bias,
@@ -884,45 +891,82 @@
     kv_theirs,
     aux_mine,
     aux_theirs,
-    ssm_mine,
-    ssm_theirs,
     normed,
     queries,
     key_vals,
     aux,
-    mixed,
-    state_out,
     tails,
     carries,
 ):
     here = position[0]
     half = tokens.shape[1] // 2
-    step = pl.program_id(0)
-    blocks = tokens.shape[0] // BLOCK
+    hidden = tokens[...].astype(F32)
+    normed[...] = (hidden * inverse_rms(hidden) * gains[0:1]).astype(BF)
 
     def product(mine, theirs, over=((1,), (0,))):
         return dot(columns_of(normed, here, half), mine[...], over) + dot(
             columns_of(normed, 1 - here, half), theirs[...], over
         )
 
-    @pl.when(pl.program_id(0) == 0)
-    def _():
-        hidden = tokens[...].astype(F32)
-        normed[...] = (hidden * inverse_rms(hidden) * gains[0:1]).astype(BF)
-        queries[...] = product(query_mine, query_theirs).astype(BF) * jnp.asarray(HD**-0.5, BF)
-        key_vals[...] = product(kv_mine, kv_theirs).astype(BF)
-        found = product(aux_mine, aux_theirs, ((1,), (1,)))
-        aux[:, : found.shape[1]] = found
-        aux[:, found.shape[1] :] = jnp.zeros_like(aux[:, found.shape[1] :])
-        rate = jnp.exp(decay_log[...])
-        for block in range(blocks):
-            rows = slice(block * BLOCK, (block + 1) * BLOCK)
-            _, step_size, _, cumulated = decays(aux[rows, :], dt_bias[...], rate)
-            last = cumulated[BLOCK - 1 :, :]
-            tails[rows, :] = step_size * jnp.exp(last - cumulated)
-            carries[block : block + 1, :] = jnp.exp(last)
-
-    found = product(ssm_mine, ssm_theirs)
+    key_vals[...] = product(kv_mine, kv_theirs).astype(BF)
+    queries[...] = product(query_mine, query_theirs).astype(BF) * jnp.asarray(HD**-0.5, BF)
+    found = product(aux_mine, aux_theirs, ((1,), (1,)))
+    aux[:, : found.shape[1]] = found
+    aux[:, found.shape[1] :] = jnp.zeros_like(aux[:, found.shape[1] :])
+    rate = jnp.exp(decay_log[...])
+    for block in range(tokens.shape[0] // BLOCK):
+        rows = slice(block * BLOCK, (block + 1) * BLOCK)
+        _, step_size, _, cumulated = decays(aux[rows, :], dt_bias[...], rate)
+        last = cumulated[BLOCK - 1 :, :]
+        tails[rows, :] = step_size * jnp.exp(last - cumulated)
+        carries[block : block + 1, :] = jnp.exp(last)
+
+
+def run_project_small(position, tokens, gains, dt_bias, decay_log, query, kv, aux):
+    rows, width = tokens.shape
+    fixed = lambda shape: pl.BlockSpec(shape, lambda step, place: (0, 0))
+    inputs = (tokens, gains, dt_bias, decay_log, *query, *kv, *aux)
+    shapes = [
+        jax.ShapeDtypeStruct((rows, width), BF),
+        jax.ShapeDtypeStruct((rows, KV_AT), BF),
+        jax.ShapeDtypeStruct((rows, AUX_AT - KV_AT), BF),
+        jax.ShapeDtypeStruct((rows, 3 * LANES), F32),
+        jax.ShapeDtypeStruct((rows, LANES), F32),
+        jax.ShapeDtypeStruct((8, LANES), F32),
+    ]
+    return pl.pallas_call(
+        project_small_kernel,
+        grid_spec=pltpu.PrefetchScalarGridSpec(
+            num_scalar_prefetch=1,
+            grid=(1,),
+            in_specs=[fixed(item.shape) for item in inputs],
+            out_specs=[fixed(shape.shape) for shape in shapes],
+        ),
+        out_shape=shapes,
+        compiler_params=params_of(WHOLE_LIMIT),
+        cost_estimate=LONG,
+        name="project_small",
+    )(position, *inputs)
+
+
+def project_kernel(
+    position,
+    resets,
+    normed,
+    aux,
+    tails,
+    carries,
+    ssm_mine,
+    ssm_theirs,
+    mixed,
+    state_out,
+):
+    here = position[0]
+    half = normed.shape[1] // 2
+    step = pl.program_id(0)
+    found = dot(columns_of(normed, here, half), ssm_mine[...]) + dot(
+        columns_of(normed, 1 - here, half), ssm_theirs[...]
+    )
     mixed[...] = found.astype(BF)
 
     for number in range(INNER // CHUNK):
@@ -933,7 +977,7 @@
             scaled = (found * spread(tails[...], *heads)).astype(BF)
             carried = spread(carries[...], *heads)
             state = jnp.zeros((STATE, CHUNK), F32)
-            for block in range(blocks):
+            for block in range(normed.shape[0] // BLOCK):
                 rows = slice(block * BLOCK, (block + 1) * BLOCK)
                 b_in = aux[rows, :STATE].astype(BF)
                 state = jnp.where(resets[block] != 0, 0.0, carried[block : block + 1, :] * state)
@@ -944,50 +988,38 @@
 CHUNK = 512
 
 
-def run_project(position, resets, tokens, gains, dt_bias, decay_log, query, kv, aux, ssm):
-    rows, width = tokens.shape
+def run_project(position, resets, normed, aux, tails, carries, ssm):
+    rows, width = normed.shape
     half = width // 2
     inner = ssm[0].shape[1]
-    aux_width = 3 * LANES
-    fixed = lambda shape: pl.BlockSpec(shape, lambda step, place, resets: (0,) * len(shape))
+    fixed = lambda shape: pl.BlockSpec(shape, lambda step, place, resets: (0, 0))
     sliding = pl.BlockSpec((half, CHUNK), lambda step, place, resets: (0, step))
-    weights = [fixed(item.shape) for item in (*query, *kv, *aux)]
     return pl.pallas_call(
         project_kernel,
         grid_spec=pltpu.PrefetchScalarGridSpec(
             num_scalar_prefetch=2,
             grid=(inner // CHUNK,),
             in_specs=[
-                *[fixed(item.shape) for item in (tokens, gains, dt_bias, decay_log)],
-                *weights,
+                *[fixed(item.shape) for item in (normed, aux, tails, carries)],
                 sliding,
                 sliding,
             ],
             out_specs=[
-                fixed((rows, width)),
-                fixed((rows, KV_AT)),
-                fixed((rows, AUX_AT - KV_AT)),
-                fixed((rows, aux_width)),
                 pl.BlockSpec((rows, CHUNK), lambda step, place, resets: (0, step)),
                 pl.BlockSpec(
                     (STATE, CHUNK),
                     lambda step, place, resets: (0, jnp.minimum(step, INNER // CHUNK - 1)),
                 ),
             ],
-            scratch_shapes=[pltpu.VMEM((rows, LANES), F32), pltpu.VMEM((8, LANES), F32)],
         ),
         out_shape=[
-            jax.ShapeDtypeStruct((rows, width), BF),
-            jax.ShapeDtypeStruct((rows, KV_AT), BF),
-            jax.ShapeDtypeStruct((rows, AUX_AT - KV_AT), BF),
-            jax.ShapeDtypeStruct((rows, aux_width), F32),
             jax.ShapeDtypeStruct((rows, inner), BF),
             jax.ShapeDtypeStruct((STATE, INNER), F32),
         ],
-        compiler_params=params_of(LARGE_LIMIT),
+        compiler_params=params_of(WHOLE_LIMIT),
         cost_estimate=LONG,
         name="project",
-    )(position, resets, tokens, gains, dt_bias, decay_log, *query, *kv, *aux, *ssm)
+    )(position, resets, normed, aux, tails, carries, *ssm)
 
 
 def middle_kernel(
@@ -1423,23 +1455,24 @@
     dt_row = jnp.pad(dt_bias, (0, lane_pad))[None]
     decay_row = jnp.pad(decay_log, (0, lane_pad))[None]
 
-    gains = jnp.stack([gain_in, gain_attn, gain_ssm, gain_ff])
-    gains_theirs = swap(gains)
-    ssm_in = (w_ssm_in, swap(w_ssm_in))
+    gain_first = natural(gain_in, swap(gain_in), position, 0).astype(F32)[None]
     query = (w_query, swap(w_query))
     kv = (w_kv, swap(w_kv))
     aux_in = (w_ssm_aux.T, swap(w_ssm_aux.T))
-    attn_out = (w_attn_out, swap(w_attn_out))
-    ssm_back = (w_ssm_out, swap(w_ssm_out))
-    gate = (w_gate, swap(w_gate))
-    up = (w_up, swap(w_up))
-    down = (w_down, swap(w_down))
-    gains_all = jnp.pad(natural(gains, gains_theirs, position, 1).astype(F32), ((0, 4), (0, 0)))
-
-    normed, scaled_queries, key_vals, aux, mixed, state_end = run_project(
-        here, resets, tokens, gains_all, dt_row, decay_row, query, kv, aux_in, ssm_in
+    ssm_in = (w_ssm_in, swap(after(w_ssm_in, kv[1])))
+    attn_out, ssm_back, gate, up, down = (
+        (weight, swap(weight)) for weight in (w_attn_out, w_ssm_out, w_gate, w_up, w_down)
+    )
+    normed, scaled_queries, key_vals, aux, tails, carries = run_project_small(
+        here, tokens, gain_first, dt_row, decay_row, query, kv, aux_in
     )
     key_prior = lax.ppermute(key_vals, "shard", [(0, 1)])
+    later_gains = [
+        natural(gain, swap(gain), position, 0).astype(F32)[None]
+        for gain in (gain_attn, gain_ssm, gain_ff)
+    ]
+    gains_all = jnp.concatenate([gain_first, *later_gains, jnp.zeros((4, width), F32)])
+    mixed, state_end = run_project(here, resets, normed, aux, tails, carries, ssm_in)
     state_prior = lax.ppermute(state_end, "shard", [(0, 1)])
     attended, log_total = run_attend(scaled_queries, key_prior, key_vals, bias)
     ssm_out, gated, states = run_forward(resets, mixed, aux, dt_row, decay_row, state_prior)
@@ -1521,7 +1554,9 @@
         ]
         return fence(value, *waits)
 
-    d_kv = None
+    d_kv = ssm_in_grad = None
+    halves = {}
+    rest_weights = (w_query, w_kv, w_ssm_aux.T, None, w_ssm_in)
 
     def key_grads(made_before):
         if made_before is not None:
@@ -1529,18 +1564,32 @@
         return (d_here + after(d_prior_got, token).astype(F32)).astype(BF)
 
     def go_on(name):
-        nonlocal token
+        nonlocal token, ssm_in_grad
         stream = sums[name]
         stream.hold(token)
+        weights = rest_weights if name == "rest" else ()
+        place = {"outs": 2, "rest": 4}.get(name)
+        shape = layouts[name][place][0].shape if place is not None else None
         if stream.steps:
             stream.prepare()
             token = stream.operand
             stream.go()
+            if name == "rest" and not stream.steps and stream.got is not None:
+                held = None if ssm_in_grad is None else ssm_in_grad.reshape(shape)
+                halves[name] = stream.finish(layouts[name], held, weights, 0)
+                if halves[name] is not None:
+                    halves[name] = list(halves[name])
+                    ssm_in_grad = halves[name][place]
         elif name not in made:
-            started = made["outs"][2].reshape(half, 2 * INNER) if name == "rest" else None
-            weights = (w_query, w_kv, w_ssm_aux.T, None, w_ssm_in) if name == "rest" else ()
-            made[name] = stream.finish(layouts[name], started, weights)
+            held = None if place is None or ssm_in_grad is None else ssm_in_grad.reshape(shape)
+            if halves.get(name) is not None:
+                halves[name][place] = held
+                made[name] = stream.finish(layouts[name], None, weights, 1, halves[name])
+            else:
+                made[name] = stream.finish(layouts[name], held, weights)
             token = made[name][0]
+            if place is not None:
+                ssm_in_grad = made[name][place].reshape(half, 2 * INNER)
 
     for number, name in enumerate(PLAN):
         if name in layouts:
@@ -1593,7 +1642,7 @@
             grad_tokens = run_late_back(
                 here,
                 tokens,
-                gains_all,
+                gain_first,
                 d_middle,
                 d_normed,
                 d_mixed,
@@ -1609,9 +1658,10 @@
     (grad_down,) = made["down"]
     grad_gate, grad_up = made["wide"]
     grad_attn_out, grad_ssm_out, _ = made["outs"]
-    grad_query, grad_kv, grad_aux, extras, grad_ssm_in, products = made["rest"]
+    grad_query, grad_kv, grad_aux, extras, _, products = made["rest"]
+    grad_ssm_in = ssm_in_grad
     gate_products = jnp.sum(
-        w_ssm_in[:, INNER:].astype(F32) * made["outs"][2].reshape(half, 2 * INNER)[:, INNER:], axis=1
+        w_ssm_in[:, INNER:].astype(F32) * grad_ssm_in[:, INNER:], axis=1
     )
     grad_gain_in = (products[0] + gate_products) / gain_in.astype(F32)
     return (

time: 398 us -> 398 us (level)
  Pallas kernels: 143 us -> 152 us
  local copies, waits for them, and re-layouts: 45.8 us -> 39 us
    unnamed x156 -> x152, local copies, waits for them, and re-layouts: 40.6 us -> 33.2 us
    pallas_call x0 -> x1, Pallas kernels: none -> 5.09 us  [run_project_small(): pl.pallas_call(project_small_kernel, grid_spec=pltpu.PrefetchScalarGridSp...]
    ppermute x14 -> x17, waiting for transfers between devices: 0.3 us -> 4.41 us  [swap(): return lax.ppermute(value, 'shard', SWAP)]
    pallas_call x4 -> x5, Pallas kernels: 22 us -> 20.4 us  [finish(): pl.pallas_call(functools.partial(finish_kernel, len(stacks), far, [cut fo...]
  transfers between devices with their start and end apart: 44 -> 47, of which waited for: 16 -> 20; matrix products, arithmetic and copies ran while one was open for 13% -> 9% of each run, Pallas kernels for 25% -> 26%
where the time goes in v3:
time: 398 us; the launch traced here: 391 us
  Pallas kernels  152 us (38%)
  waiting for transfers between devices  112 us (28%)
  other arithmetic  43.4 us (11%)
  starting transfers between devices  42.9 us (11%)
  local copies, waits for them, and re-layouts  39 us (10%)
    ppermute x26, waiting for transfers between devices, go(): got = lax.ppermute(self.operand, ('rep', 'shard'), self.pairs(step))  106 us
    pallas_call x1, Pallas kernels, run_middle(): pl.pallas_call(middle_kernel, grid_spec=pltpu.PrefetchScalarGridSpec(num_...  39.9 us
    convert_element_type x20, other arithmetic, part(): return total.astype(BF)  35 us
    unnamed x152, local copies, waits for them, and re-layouts  33.2 us
    ppermute x26, starting transfers between devices, go(): got = lax.ppermute(self.operand, ('rep', 'shard'), self.pairs(step))  23.3 us
    pallas_call x5, Pallas kernels, finish(): pl.pallas_call(functools.partial(finish_kernel, len(stacks), far, [cut fo...  20.4 us
    pallas_call x1, Pallas kernels, run_backward(): pl.pallas_call(backward_kernel, grid=(count,), in_specs=[scalars(), pl.Bl...  16.2 us
    pallas_call x1, Pallas kernels, run_attend_back(): pl.pallas_call(attend_back_kernel, out_shape=[jax.ShapeDtypeStruct((rows,...  14.7 us
  transfers between devices with their start and end apart: 47, of which 20 were waited for; matrix products, arithmetic and copies ran while one was open for 9% of the time, Pallas kernels for 26%

profile of v3, /device:TPU:1, one launch (start us, length us, event | category | flops | bytes accessed | tf_op | source)
XLA Modules:
  0.0 391.2 jit_solution(598045209814107771)
XLA Ops:
  12.5 5.1 %project_small.1 = (bf16[512,1024]{1,0:T(8,128)(2,1)}, bf16[512,512]{1,0:T(8,128)(2,1)}, bf16[512,256]{1,0:T(8,128)(2,1)}, f32[512,384]{1,0:T(8,128)}, f32[512,128]{1,0:T(8,128)}, /*index=5*/f32[8,128]{1,0:T(8,128)}) custom-call(s32[1]{0:T(128)} %bitcast.position, bf16[512,1024]{1,0:T(8,128)(2,1)} %tokens.5, f32[1,1024]{1,0:T(1,128)} %copy-done.58, ...), custom_call_target="tpu_custom_call" | custom-call | flops 15000000512 | bytes 1000000 | tf_op jit(solution)/shard_map/project_small/pallas_call | solution.py:937
  19.2 11.4 %project.1 = (bf16[512,3072]{1,0:T(8,128)(2,1)}, f32[128,1536]{1,0:T(8,128)}) custom-call(s32[1]{0:T(128)} %bitcast.position, s32[4]{0:T(128)} %compare_convert_fusion.resets, bf16[512,1024]{1,0:T(8,128)(2,1)} %get-tuple-element.111.normed, f32[512,384]{1,0:T(8,128)} %get-tuple-element.112.aux, f32[512,128]{1,0:T(8,128)} %get-tuple-element.113.tails, ...), custom_call_target="tpu_custom_call" | custom-call | flops 15000000512 | bytes 1000000 | tf_op jit(solution)/shard_map/project/pallas_call | solution.py:997
  32.2 8.7 %attend.1 = (bf16[512,512]{1,0:T(8,128)(2,1)S(1)}, f32[512,8]{1,0:T(8,128)S(1)}) custom-call(bf16[512,512]{1,0:T(8,128)(2,1)S(1)} %copy-done.45, bf16[512,256]{1,0:T(8,128)(2,1)} %collective-permute-done.4.prior_ref, bf16[512,256]{1,0:T(8,128)(2,1)S(1)} %copy-done.53, f32[4,1024]{1,0:T(4,128)S(1)} %compare_select_fusion.bias_ref), custom_call_target="tpu_custom_call" | custom-call | flops 15000000512 | bytes 1000000 | tf_op jit(solution)/shard_map/attend/pallas_call | solution.py:532
  43.2 8.7 %ssm_forward.1 = (f32[512,1536]{1,0:T(8,128)S(1)}, bf16[512,1536]{1,0:T(8,128)(2,1)S(1)}, bf16[4,128,1536]{2,1,0:T(8,128)(2,1)S(1)}) custom-call(s32[4]{0:T(128)S(1)} %copy-done.64, bf16[512,3072]{1,0:T(8,128)(2,1)S(1)} %copy-done.1, bf16[512,3072]{1,0:T(8,128)(2,1)S(1)} %copy-done.1, f32[512,384]{1,0:T(8,128)S(1)} %copy-done.22, f32[1,128]{1,0:T(1,128)S(1)} %copy-done.68, ...), custom_call_target="tpu_custom_call" | custom-call | flops 15000000512 | bytes 1000000 | tf_op jit(solution)/shard_map/ssm_forward/pallas_call | solution.py:349
  56.0 39.9 %middle.1 = (bf16[512,1024]{1,0:T(8,128)(2,1)}, f32[512,1024]{1,0:T(8,128)}, bf16[512,1024]{1,0:T(8,128)(2,1)S(1)}, bf16[512,1024]{1,0:T(8,128)(2,1)}, bf16[512,...) custom-call(s32[1]{0:T(128)} %bitcast.position, ...), custom_call_target="tpu_custom_call" | custom-call | flops 15000000512 | bytes 1000000 | tf_op jit(solution)/shard_map/middle/pallas_call | solution.py:1167
  98.8 7.3 %ssm_state_back.1 = (bf16[128,1536]{1,0:T(8,128)(2,1)}, bf16[512,1536]{1,0:T(8,128)(2,1)}) custom-call(s32[4]{0:T(128)} %compare_convert_fusion.resets, bf16[512,1536]{1,0:T(8,128)(2,1)} %get-tuple-element.139.d_gated, bf16[512,3072]{1,0:T(8,128)(2,1)} %get-tuple-element.116.mixed.gate, f32[512,384]{1,0:T(8,128)} %get-tuple-element.112.aux, ...), custom_call_target="tpu_custom_call" | custom-call | flops 1000000 | bytes 1000000 | tf_op jit(solution)/shard_map/ssm_state_back/pallas_call | solution.py:381
  109.7 4.5 %add_convert_fusion = bf16[256,4096]{1,0:T(8,128)(2,1)} fusion(bf16[512,4096]{1,0:T(8,128)(2,1)} %collective-permute-done.16.refs_2_, s32[]{:T(128)S(6)} %select_n.249, bf16[512,4096]{1,0:T(8,128)(2,1)} %get-tuple-element.125), kind=kLoop, calls=%fused_computation | loop fusion | flops 4194304 | bytes 6291460 | tf_op jit(solution)/shard_map/convert_element_type | solution.py:615
  117.0 6.1 %outs_grads.1 = (bf16[256,7168]{1,0:T(8,128)(2,1)}, bf16[256,7168]{1,0:T(8,128)(2,1)S(1)}) custom-call(s32[1]{0:T(128)} %bitcast.position, bf16[512,512]{1,0:T(8,128)(2,1)S(1)} %copy-done.50, bf16[512,1536]{1,0:T(8,128)(2,1)S(1)} %copy-done.35, bf16[512,1024]{1,0:T(8,128)(2,1)S(1)} %copy-done.17, bf16[512,1024]{1,0:T(8,128)(2,1)S(1)} %copy-done.43, ...), custom_call_target="tpu_custom_call" | custom-call | flops 1000000 | bytes 1000000 | tf_op jit(solution)/shard_map/outs_grads/pallas_call | solution.py:1249
  141.0 16.2 %ssm_backward.1 = (bf16[512,1536]{1,0:T(8,128)(2,1)S(1)}, bf16[512,384]{1,0:T(8,128)(2,1)S(1)}, f32[8,128]{1,0:T(8,128)S(1)}) custom-call(s32[4]{0:T(128)S(1)} %copy-done.65, bf16[512,1536]{1,0:T(8,128)(2,1)S(1)} %copy-done.13, bf16[512,3072]{1,0:T(8,128)(2,1)S(1)} %copy-done.2, bf16[512,3072]{1,0:T(8,128)(2,1)S(1)} %copy-done.2, f32[512,384]{1,0:T(8,128)S(1)} %copy-done.23, ...), custom_call_target="tpu_custom_call" | custom-call | flops 1000000 | bytes 1000000 | tf_op jit(solution)/shard_map/ssm_backward/pallas_call | solution.py:409
  159.8 3.7 add_convert_fusion.3
  167.5 3.3 add_convert_fusion.1
  172.1 14.7 %attend_back.1 = (bf16[512,512]{1,0:T(8,128)(2,1)S(1)}, bf16[512,256]{1,0:T(8,128)(2,1)S(1)}, f32[512,256]{1,0:T(8,128)S(1)}) custom-call(bf16[512,512]{1,0:T(8,128)(2,1)S(1)} %copy-done.46, bf16[512,256]{1,0:T(8,128)(2,1)} %collective-permute-done.4.prior_ref, bf16[512,256]{1,0:T(8,128)(2,1)S(1)} %copy-done.54, f32[4,1024]{1,0:T(4,128)S(1)} %compare_select_fusion.bias_ref, ...), custom_call_target="tpu_custom_call" | custom-call | flops 1000000 | bytes 1000000 | tf_op jit(solution)/shard_map/attend_back/pallas_call | solution.py:547
  189.3 8.8 %collective-permute-start.23 = (bf16[512,256]{1,0:T(8,128)(2,1)}, bf16[512,256]{1,0:T(8,128)(2,1)S(1)}, u32[]{:S(2)}, u32[]{:S(2)}) collective-permute-start(bf16[512,256]{1,0:T(8,128)(2,1)} %fence.5), channel_id=1, source_target_pairs={{1,0},{3,2},{5,4},{7,6},{9,8},{11,10},{13,12},{15,14},{17,16},{19,... | collective-permute-start | bytes 786440 | tf_op jit(solution)/shard_map/ppermute | solution.py:1614
  201.1 5.1 %rest_grads.1 = (bf16[512,2688]{1,0:T(8,128)(2,1)}, bf16[512,2688]{1,0:T(8,128)(2,1)S(1)}) custom-call(s32[1]{0:T(128)} %bitcast.position, bf16[512,1024]{1,0:T(8,128)(2,1)S(1)} %copy-done.18, bf16[512,512]{1,0:T(8,128)(2,1)S(1)} %copy-done.32, bf16[512,256]{1,0:T(8,128)(2,1)S(1)} %add_convert_fusion.20.d_kv, bf16[512,1536]{1,0:T(8,128)(2,1)S(1)} %copy-done.9, ...), custom_call_target="tpu_custom_call" | custom-call | flops 1000000 | bytes 1000000 | tf_op jit(solution)/shard_map/rest_grads/pallas_call | solution.py:1354
  215.5 3.9 early_back.1.d_normed
  232.9 6.2 %collective-permute-done.25 = bf16[64,7168]{1,0:T(8,128)(2,1)S(1)} collective-permute-done((bf16[64,7168]{1,0:T(8,128)(2,1)S(1)}, bf16[64,7168]{1,0:T(8,128)(2,1)S(1)}, u32[]{:S(2)}, u32[]{:S(2)}) %collective-permute-start.25) | collective-permute-done | bytes 917536 | tf_op jit(solution)/shard_map/ppermute | solution.py:645
  241.0 14.3 %collective-permute-done.32 = bf16[64,4096]{1,0:T(8,128)(2,1)S(1)} collective-permute-done((bf16[64,4096]{1,0:T(8,128)(2,1)S(1)}, bf16[64,4096]{1,0:T(8,128)(2,1)S(1)}, u32[]{:S(2)}, u32[]{:S(2)}) %collective-permute-start.32) | collective-permute-done | bytes 524320 | tf_op jit(solution)/shard_map/ppermute | solution.py:645
  264.2 6.1 %collective-permute-done.36 = bf16[64,4096]{1,0:T(8,128)(2,1)S(1)} collective-permute-done((bf16[64,4096]{1,0:T(8,128)(2,1)S(1)}, bf16[64,4096]{1,0:T(8,128)(2,1)S(1)}, u32[]{:S(2)}, u32[]{:S(2)}) %collective-permute-start.36) | collective-permute-done | bytes 524320 | tf_op jit(solution)/shard_map/ppermute | solution.py:645
  271.6 3.1 collective-permute-done.35
  276.7 5.2 %collective-permute-done.34 = bf16[256,1024]{1,0:T(8,128)(2,1)S(1)} collective-permute-done((bf16[256,1024]{1,0:T(8,128)(2,1)S(1)}, bf16[256,1024]{1,0:T(8,128)(2,1)S(1)}, u32[]{:S(2)}, u32[]{:S(2)}) %collective-permute-start.34) | collective-permute-done | bytes 524320 | tf_op jit(solution)/shard_map/ppermute | solution.py:645
  283.8 9.4 %collective-permute-done.40 = bf16[128,4096]{1,0:T(8,128)(2,1)S(1)} collective-permute-done((bf16[128,4096]{1,0:T(8,128)(2,1)S(1)}, bf16[128,4096]{1,0:T(8,128)(2,1)S(1)}, u32[]{:S(2)}, u32[]{:S(2)}) %collective-permute-start.40) | collective-permute-done | bytes 1048608 | tf_op jit(solution)/shard_map/ppermute | solution.py:645
  294.4 5.7 %collective-permute-done.39 = bf16[128,2688]{1,0:T(8,128)(2,1)S(1)} collective-permute-done((bf16[128,2688]{1,0:T(8,128)(2,1)S(1)}, bf16[128,2688]{1,0:T(8,128)(2,1)S(1)}, u32[]{:S(2)}, u32[]{:S(2)}) %collective-permute-start.39) | collective-permute-done | bytes 688160 | tf_op jit(solution)/shard_map/ppermute | solution.py:645
  300.4 27.1 %collective-permute-done.38.refs_1_ = bf16[512,1024]{1,0:T(8,128)(2,1)S(1)} collective-permute-done((bf16[512,1024]{1,0:T(8,128)(2,1)S(1)}, bf16[512,1024]{1,0:T(8,128)(2,1)S(1)}, u32[]{:S(2)}, u32[]{:S(2)}) %collective-permute-start.38) | collective-permute-done | bytes 1048608 | tf_op jit(solution)/shard_map/ppermute | solution.py:645
  327.5 3.2 unpack.5
  333.9 4.5 %late_back.1 = f32[512,1024]{1,0:T(8,128)} custom-call(s32[1]{0:T(128)} %bitcast.position, bf16[512,1024]{1,0:T(8,128)(2,1)S(1)} %copy-done.41, f32[1,1024]{1,0:T(1,128)S(1)} %copy-done.59, f32[512,1024]{1,0:T(8,128)S(1)} %copy-done.30, f32[512,1024]{1,0:T(8,128)S(1)} %early_back.1.d_normed, bf16[512,1536]{1,0:T(8,128)(2,1)S(1)} %copy-done.10, ...), custom_call_target="tpu_custom_call" | custom-call | flops 1000000 | bytes 1000000 | tf_op jit(solution)/shard_map/late_back/pallas_call | solution.py:1403
  338.3 4.2 %unpack.6 = (f32[512,2048]{1,0:T(8,128)}, f32[512,2048]{1,0:T(8,128)}) custom-call(s32[5]{0:T(128)S(1)} %get-tuple-element.208.places, bf16[256,4096]{1,0:T(8,128)(2,1)S(1)} %pad_maximum_fusion.refs_0_, bf16[256,4096]{1,0:T(8,128)(2,1)S(1)} %collective-permute-done.42.refs_1_), custom_call_target="tpu_custom_call" | custom-call | flops 1000000 | bytes 1000000 | tf_op jit(solution)/shard_map/unpack/pallas_call | solution.py:759
  347.7 5.1 %collective-permute-done.43 = bf16[128,2688]{1,0:T(8,128)(2,1)S(1)} collective-permute-done((bf16[128,2688]{1,0:T(8,128)(2,1)S(1)}, bf16[128,2688]{1,0:T(8,128)(2,1)S(1)}, u32[]{:S(2)}, u32[]{:S(2)}) %collective-permute-start.43) | collective-permute-done | bytes 688160 | tf_op jit(solution)/shard_map/ppermute | solution.py:645
  357.7 3.4 unpack.7
  361.1 8.0 %collective-permute-done.46.refs_1_ = bf16[128,7168]{1,0:T(8,128)(2,1)} collective-permute-done((bf16[128,7168]{1,0:T(8,128)(2,1)}, bf16[128,7168]{1,0:T(8,128)(2,1)}, u32[]{:S(2)}, u32[]{:S(2)}) %collective-permute-start.46) | collective-permute-done | bytes 1835040 | tf_op jit(solution)/shard_map/ppermute | solution.py:645
  369.1 6.3 %unpack.8 = (f32[256,1024]{1,0:T(8,128)}, f32[3,256,1024]{2,1,0:T(8,128)}, f32[2,256,3072]{2,1,0:T(8,128)}) custom-call(s32[5]{0:T(128)S(1)} %get-tuple-element.209.places, bf16[128,7168]{1,0:T(8,128)(2,1)} %pad_maximum_fusion.1.refs_0_, bf16[128,7168]{1,0:T(8,128)(2,1)} %collective-permute-done.46.refs_1_, ...), custom_call_target="tpu_custom_call", output_to_operand_aliasing={{2}: (3, {})} | custom-call | flops 1000000 | bytes 1000000 | tf_op jit(solution)/shard_map/unpack/pallas_call | solution.py:759
  375.4 8.2 %collective-permute-done.45.refs_0_ = bf16[256,2688]{1,0:T(8,128)(2,1)} collective-permute-done((bf16[256,2688]{1,0:T(8,128)(2,1)}, bf16[256,2688]{1,0:T(8,128)(2,1)}, u32[]{:S(2)}, u32[]{:S(2)}) %collective-permute-start.45) | collective-permute-done | bytes 1376288 | tf_op jit(solution)/shard_map/ppermute | solution.py:645
  383.6 3.4 unpack.9
  (298 shorter events, 119.0 us)
Async XLA Ops:
  2.6 14.9 %collective-permute-start.5 = (bf16[512,3072]{1,0:T(8,128)(2,1)}, bf16[512,3072]{1,0:T(8,128)(2,1)S(1)}, u32[]{:S(2)}, u32[]{:S(2)}) collective-permute-start(bf16[512,3072]{1,0:T(8,128)(2,1)} %refs_4_.3), channel_id=1, source_target_pairs={{0,1},{1,0},{2,3},{3,2},{4,5},{5,4},{6,7},{7,6},{8,9},{9,8},{10,11... | collective-permute-start | bytes 9437192 | tf_op jit(solution)/shard_map/ppermute | solution.py:562
  10.1 45.9 %collective-permute-start.12 = (bf16[512,2048]{1,0:T(8,128)(2,1)}, bf16[512,2048]{1,0:T(8,128)(2,1)}, u32[]{:S(2)}, u32[]{:S(2)}) collective-permute-start(bf16[512,2048]{1,0:T(8,128)(2,1)} %gate_mine.1), channel_id=1, source_target_pairs={{0,1},{1,0},{2,3},{3,2},{4,5},{5,4},{6,7},{7,6},{8,9},{9,8},{10,11... | collective-permute-start | bytes 6291464 | tf_op jit(solution)/shard_map/ppermute | solution.py:562
  10.5 45.5 %collective-permute-start.13 = (bf16[512,2048]{1,0:T(8,128)(2,1)}, bf16[512,2048]{1,0:T(8,128)(2,1)}, u32[]{:S(2)}, u32[]{:S(2)}) collective-permute-start(bf16[512,2048]{1,0:T(8,128)(2,1)} %up_mine.1), channel_id=1, source_target_pairs={{0,1},{1,0},{2,3},{3,2},{4,5},{5,4},{6,7},{7,6},{8,9},{9,8},{10,11... | collective-permute-start | bytes 6291464 | tf_op jit(solution)/shard_map/ppermute | solution.py:562
  11.7 44.3 %collective-permute-start.14 = (bf16[1024,1024]{1,0:T(8,128)(2,1)}, bf16[1024,1024]{1,0:T(8,128)(2,1)}, u32[]{:S(2)}, u32[]{:S(2)}) collective-permute-start(bf16[1024,1024]{1,0:T(8,128)(2,1)} %down_mine.1), channel_id=1, source_target_pairs={{0,1},{1,0},{2,3},{3,2},{4,5},{5,4},{6,7},{7,6},{8,9},{9,8},{10,11... | collective-permute-start | bytes 6291464 | tf_op jit(solution)/shard_map/ppermute | solution.py:562
  11.9 44.1 %collective-permute-start.11 = (bf16[768,1024]{1,0:T(8,128)(2,1)}, bf16[768,1024]{1,0:T(8,128)(2,1)}, u32[]{:S(2)}, u32[]{:S(2)}) collective-permute-start(bf16[768,1024]{1,0:T(8,128)(2,1)} %ssm_mine.5), channel_id=1, source_target_pairs={{0,1},{1,0},{2,3},{3,2},{4,5},{5,4},{6,7},{7,6},{8,9},{9,8},{10,11... | collective-permute-start | bytes 4718600 | tf_op jit(solution)/shard_map/ppermute | solution.py:562
  17.6 13.1 %collective-permute-start.4 = (bf16[512,256]{1,0:T(8,128)(2,1)}, bf16[512,256]{1,0:T(8,128)(2,1)}, u32[]{:S(2)}, u32[]{:S(2)}) collective-permute-start(bf16[512,256]{1,0:T(8,128)(2,1)} %get-tuple-element.109.here_ref), channel_id=1, source_target_pairs={{0,1},{2,3},{4,5},{6,7},{8,9},{10,11},{12,13},{14,15},{16,17},{18,... | collective-permute-start | bytes 786440 | tf_op jit(solution)/shard_map/ppermute | solution.py:1469
  41.6 14.4 %collective-permute-start.10 = (bf16[256,1024]{1,0:T(8,128)(2,1)S(1)}, bf16[256,1024]{1,0:T(8,128)(2,1)S(1)}, u32[]{:S(2)}, u32[]{:S(2)}) collective-permute-start(bf16[256,1024]{1,0:T(8,128)(2,1)S(1)} %copy-done.70), channel_id=1, source_target_pairs={{0,1},{1,0},{2,3},{3,2},{4,5},{5,4},{6,7},{7,6},{8,9},{9,8},{10,11... | collective-permute-start | bytes 1572872 | tf_op jit(solution)/shard_map/ppermute | solution.py:562
  125.0 34.8 %collective-permute-start.17 = (bf16[256,7168]{1,0:T(8,128)(2,1)}, bf16[256,7168]{1,0:T(8,128)(2,1)}, u32[]{:S(2)}, u32[]{:S(2)}) collective-permute-start(bf16[256,7168]{1,0:T(8,128)(2,1)} %get-tuple-element.138), channel_id=1, source_target_pairs={{0,1},{1,0},{2,3},{3,2},{4,5},{5,4},{6,7},{7,6},{8,9},{9,8},{10,11... | collective-permute-start | bytes 11010056 | tf_op jit(solution)/shard_map/ppermute | solution.py:562
  125.3 34.4 %collective-permute-start.19 = (bf16[256,4096]{1,0:T(8,128)(2,1)}, bf16[256,4096]{1,0:T(8,128)(2,1)}, u32[]{:S(2)}, u32[]{:S(2)}) collective-permute-start(bf16[256,4096]{1,0:T(8,128)(2,1)} %add_convert_fusion), channel_id=1, source_target_pairs={{0,2},{1,5},{2,0},{3,7},{4,6},{5,1},{6,4},{7,3},{8,10},{9,13},{10,... | collective-permute-start | bytes 6291464 | tf_op jit(solution)/shard_map/ppermute | solution.py:645
  127.7 32.0 %collective-permute-start.18 = (bf16[512,1024]{1,0:T(8,128)(2,1)}, bf16[512,1024]{1,0:T(8,128)(2,1)}, u32[]{:S(2)}, u32[]{:S(2)}) collective-permute-start(bf16[512,1024]{1,0:T(8,128)(2,1)} %add_convert_fusion.4), channel_id=1, source_target_pairs={{0,8},{1,9},{2,10},{3,11},{4,12},{5,13},{6,14},{7,15},{8,0},{9,1},... | collective-permute-start | bytes 3145736 | tf_op jit(solution)/shard_map/ppermute | solution.py:645
  163.5 24.8 %collective-permute-start.22 = (bf16[128,4096]{1,0:T(8,128)(2,1)}, bf16[128,4096]{1,0:T(8,128)(2,1)S(1)}, u32[]{:S(2)}, u32[]{:S(2)}) collective-permute-start(bf16[128,4096]{1,0:T(8,128)(2,1)} %add_convert_fusion.3), channel_id=1, source_target_pairs={{0,4},{1,3},{2,6},{3,1},{4,0},{5,7},{6,2},{7,5},{8,12},{9,11},{10,... | collective-permute-start | bytes 3145736 | tf_op jit(solution)/shard_map/ppermute | solution.py:645
  167.3 21.0 %collective-permute-start.21 = (bf16[256,1024]{1,0:T(8,128)(2,1)}, bf16[256,1024]{1,0:T(8,128)(2,1)}, u32[]{:S(2)}, u32[]{:S(2)}) collective-permute-start(bf16[256,1024]{1,0:T(8,128)(2,1)} %add_convert_fusion.16), channel_id=1, source_target_pairs={{0,4},{1,3},{2,6},{3,1},{4,0},{5,7},{6,2},{7,5},{8,12},{9,11},{10,... | collective-permute-start | bytes 1572872 | tf_op jit(solution)/shard_map/ppermute | solution.py:645
  170.8 52.1 %collective-permute-start.24 = (bf16[128,7168]{1,0:T(8,128)(2,1)}, bf16[128,7168]{1,0:T(8,128)(2,1)}, u32[]{:S(2)}, u32[]{:S(2)}) collective-permute-start(bf16[128,7168]{1,0:T(8,128)(2,1)} %add_convert_fusion.1), channel_id=1, source_target_pairs={{0,8},{1,5},{2,10},{3,7},{4,12},{5,1},{6,14},{7,3},{8,0},{9,13},{1... | collective-permute-start | bytes 5505032 | tf_op jit(solution)/shard_map/ppermute | solution.py:645
  207.7 22.9 %collective-permute-start.27 = (bf16[512,2688]{1,0:T(8,128)(2,1)}, bf16[512,2688]{1,0:T(8,128)(2,1)}, u32[]{:S(2)}, u32[]{:S(2)}) collective-permute-start(bf16[512,2688]{1,0:T(8,128)(2,1)} %get-tuple-element.154), channel_id=1, source_target_pairs={{0,1},{1,0},{2,3},{3,2},{4,5},{5,4},{6,7},{7,6},{8,9},{9,8},{10,11... | collective-permute-start | bytes 8257544 | tf_op jit(solution)/shard_map/ppermute | solution.py:562
  207.7 18.3 %collective-permute-start.28 = (bf16[64,4096]{1,0:T(8,128)(2,1)}, bf16[64,4096]{1,0:T(8,128)(2,1)S(1)}, u32[]{:S(2)}, u32[]{:S(2)}) collective-permute-start(bf16[64,4096]{1,0:T(8,128)(2,1)} %add_convert_fusion.15), channel_id=1, source_target_pairs={{0,16},{1,9},{2,18},{3,11},{4,20},{5,13},{6,22},{7,15},{8,24},{9,1... | collective-permute-start | bytes 1572872 | tf_op jit(solution)/shard_map/ppermute | solution.py:645
  225.0 14.1 %collective-permute-start.25 = (bf16[64,7168]{1,0:T(8,128)(2,1)S(1)}, bf16[64,7168]{1,0:T(8,128)(2,1)S(1)}, u32[]{:S(2)}, u32[]{:S(2)}) collective-permute-start(bf16[64,7168]{1,0:T(8,128)(2,1)S(1)} %add_convert_fusion.5), channel_id=1, source_target_pairs={{0,4},{1,3},{2,6},{3,1},{4,0},{5,7},{6,2},{7,5},{8,12},{9,11},{10,... | collective-permute-start | bytes 2752520 | tf_op jit(solution)/shard_map/ppermute | solution.py:645
  228.0 27.3 %collective-permute-start.32 = (bf16[64,4096]{1,0:T(8,128)(2,1)S(1)}, bf16[64,4096]{1,0:T(8,128)(2,1)S(1)}, u32[]{:S(2)}, u32[]{:S(2)}) collective-permute-start(bf16[64,4096]{1,0:T(8,128)(2,1)S(1)} %add_convert_fusion.13), channel_id=1, source_target_pairs={{0,8},{1,17},{2,10},{3,19},{4,12},{5,21},{6,14},{7,23},{8,0},{9,25... | collective-permute-start | bytes 1572872 | tf_op jit(solution)/shard_map/ppermute | solution.py:645
  232.3 23.2 %collective-permute-start.31 = (bf16[256,2688]{1,0:T(8,128)(2,1)S(1)}, bf16[256,2688]{1,0:T(8,128)(2,1)S(1)}, u32[]{:S(2)}, u32[]{:S(2)}) collective-permute-start(bf16[256,2688]{1,0:T(8,128)(2,1)S(1)} %add_convert_fusion.2), channel_id=1, source_target_pairs={{0,2},{1,5},{2,0},{3,7},{4,6},{5,1},{6,4},{7,3},{8,10},{9,13},{10,... | collective-permute-start | bytes 4128776 | tf_op jit(solution)/shard_map/ppermute | solution.py:645
  232.8 28.2 %collective-permute-start.30 = (bf16[256,1024]{1,0:T(8,128)(2,1)S(1)}, bf16[256,1024]{1,0:T(8,128)(2,1)S(1)}, u32[]{:S(2)}, u32[]{:S(2)}) collective-permute-start(bf16[256,1024]{1,0:T(8,128)(2,1)S(1)} %add_convert_fusion.12), channel_id=1, source_target_pairs={{0,2},{1,17},{2,0},{3,19},{4,6},{5,21},{6,4},{7,23},{8,10},{9,25},... | collective-permute-start | bytes 1572872 | tf_op jit(solution)/shard_map/ppermute | solution.py:645
  240.7 21.6 %collective-permute-start.29 = (bf16[32,7168]{1,0:T(8,128)(2,1)S(1)}, bf16[32,7168]{1,0:T(8,128)(2,1)S(1)}, u32[]{:S(2)}, u32[]{:S(2)}) collective-permute-start(bf16[32,7168]{1,0:T(8,128)(2,1)S(1)} %add_convert_fusion.19), channel_id=1, source_target_pairs={{0,2},{1,9},{2,0},{3,11},{4,6},{5,13},{6,4},{7,15},{8,10},{9,1},{1... | collective-permute-start | bytes 1376264 | tf_op jit(solution)/shard_map/ppermute | solution.py:645
  255.4 14.8 %collective-permute-start.36 = (bf16[64,4096]{1,0:T(8,128)(2,1)S(1)}, bf16[64,4096]{1,0:T(8,128)(2,1)S(1)}, u32[]{:S(2)}, u32[]{:S(2)}) collective-permute-start(bf16[64,4096]{1,0:T(8,128)(2,1)S(1)} %add_convert_fusion.11), channel_id=1, source_target_pairs={{0,16},{1,9},{2,18},{3,11},{4,20},{5,13},{6,22},{7,15},{8,24},{9,1... | collective-permute-start | bytes 1572872 | tf_op jit(solution)/shard_map/ppermute | solution.py:645
  257.1 17.6 %collective-permute-start.35 = (bf16[128,2688]{1,0:T(8,128)(2,1)S(1)}, bf16[128,2688]{1,0:T(8,128)(2,1)S(1)}, u32[]{:S(2)}, u32[]{:S(2)}) collective-permute-start(bf16[128,2688]{1,0:T(8,128)(2,1)S(1)} %add_convert_fusion.9), channel_id=1, source_target_pairs={{0,8},{1,3},{2,10},{3,1},{4,12},{5,7},{6,14},{7,5},{8,0},{9,11},{1... | collective-permute-start | bytes 2064392 | tf_op jit(solution)/shard_map/ppermute | solution.py:645
  261.2 20.7 %collective-permute-start.34 = (bf16[256,1024]{1,0:T(8,128)(2,1)S(1)}, bf16[256,1024]{1,0:T(8,128)(2,1)S(1)}, u32[]{:S(2)}, u32[]{:S(2)}) collective-permute-start(bf16[256,1024]{1,0:T(8,128)(2,1)S(1)} %add_convert_fusion.10), channel_id=1, source_target_pairs={{0,4},{1,3},{2,6},{3,1},{4,0},{5,7},{6,2},{7,5},{8,12},{9,11},{10,... | collective-permute-start | bytes 1572872 | tf_op jit(solution)/shard_map/ppermute | solution.py:645
  264.1 19.6 %collective-permute-start.33 = (bf16[32,7168]{1,0:T(8,128)(2,1)S(1)}, bf16[32,7168]{1,0:T(8,128)(2,1)S(1)}, u32[]{:S(2)}, u32[]{:S(2)}) collective-permute-start(bf16[32,7168]{1,0:T(8,128)(2,1)S(1)} %add_convert_fusion.18), channel_id=1, source_target_pairs={{0,16},{1,17},{2,18},{3,19},{4,20},{5,21},{6,22},{7,23},{8,24},{9,... | collective-permute-start | bytes 1376264 | tf_op jit(solution)/shard_map/ppermute | solution.py:645
  270.3 22.9 %collective-permute-start.40 = (bf16[128,4096]{1,0:T(8,128)(2,1)S(1)}, bf16[128,4096]{1,0:T(8,128)(2,1)S(1)}, u32[]{:S(2)}, u32[]{:S(2)}) collective-permute-start(bf16[128,4096]{1,0:T(8,128)(2,1)S(1)} %pad_maximum_fusion.3), channel_id=1, source_target_pairs={{0,4},{1,3},{2,6},{3,1},{4,0},{5,7},{6,2},{7,5},{8,12},{9,11},{10,... | collective-permute-start | bytes 3145736 | tf_op jit(solution)/shard_map/ppermute | solution.py:645
  276.3 23.8 %collective-permute-start.39 = (bf16[128,2688]{1,0:T(8,128)(2,1)S(1)}, bf16[128,2688]{1,0:T(8,128)(2,1)S(1)}, u32[]{:S(2)}, u32[]{:S(2)}) collective-permute-start(bf16[128,2688]{1,0:T(8,128)(2,1)S(1)} %add_convert_fusion.8), channel_id=1, source_target_pairs={{0,4},{1,9},{2,6},{3,11},{4,0},{5,13},{6,2},{7,15},{8,12},{9,1},{1... | collective-permute-start | bytes 2064392 | tf_op jit(solution)/shard_map/ppermute | solution.py:645
  282.0 45.5 %collective-permute-start.38 = (bf16[512,1024]{1,0:T(8,128)(2,1)S(1)}, bf16[512,1024]{1,0:T(8,128)(2,1)S(1)}, u32[]{:S(2)}, u32[]{:S(2)}) collective-permute-start(bf16[512,1024]{1,0:T(8,128)(2,1)S(1)} %pad_maximum_fusion.4.refs_0_), channel_id=1, source_target_pairs={{0,8},{1,9},{2,10},{3,11},{4,12},{5,13},{6,14},{7,15},{8,0},{9,1},... | collective-permute-start | bytes 3145736 | tf_op jit(solution)/shard_map/ppermute | solution.py:645
  293.4 45.0 %collective-permute-start.42 = (bf16[256,4096]{1,0:T(8,128)(2,1)S(1)}, bf16[256,4096]{1,0:T(8,128)(2,1)S(1)}, u32[]{:S(2)}, u32[]{:S(2)}) collective-permute-start(bf16[256,4096]{1,0:T(8,128)(2,1)S(1)} %pad_maximum_fusion.refs_0_), channel_id=1, source_target_pairs={{0,2},{1,5},{2,0},{3,7},{4,6},{5,1},{6,4},{7,3},{8,10},{9,13},{10,... | collective-permute-start | bytes 6291464 | tf_op jit(solution)/shard_map/ppermute | solution.py:645
  294.4 38.0 %collective-permute-start.37 = (bf16[32,7168]{1,0:T(8,128)(2,1)S(1)}, bf16[32,7168]{1,0:T(8,128)(2,1)S(1)}, u32[]{:S(2)}, u32[]{:S(2)}) collective-permute-start(bf16[32,7168]{1,0:T(8,128)(2,1)S(1)} %add_convert_fusion.17), channel_id=1, source_target_pairs={{0,2},{1,9},{2,0},{3,11},{4,6},{5,13},{6,4},{7,15},{8,10},{9,1},{1... | collective-permute-start | bytes 1376264 | tf_op jit(solution)/shard_map/ppermute | solution.py:645
  300.4 42.1 %collective-permute-start.41 = (bf16[128,2688]{1,0:T(8,128)(2,1)S(1)}, bf16[128,2688]{1,0:T(8,128)(2,1)S(1)}, u32[]{:S(2)}, u32[]{:S(2)}) collective-permute-start(bf16[128,2688]{1,0:T(8,128)(2,1)S(1)} %add_convert_fusion.7), channel_id=1, source_target_pairs={{0,16},{1,17},{2,18},{3,19},{4,20},{5,21},{6,22},{7,23},{8,24},{9,... | collective-permute-start | bytes 2064392 | tf_op jit(solution)/shard_map/ppermute | solution.py:645
  346.4 22.7 %collective-permute-start.46 = (bf16[128,7168]{1,0:T(8,128)(2,1)}, bf16[128,7168]{1,0:T(8,128)(2,1)}, u32[]{:S(2)}, u32[]{:S(2)}) collective-permute-start(bf16[128,7168]{1,0:T(8,128)(2,1)} %pad_maximum_fusion.1.refs_0_), channel_id=1, source_target_pairs={{0,8},{1,5},{2,10},{3,7},{4,12},{5,1},{6,14},{7,3},{8,0},{9,13},{1... | collective-permute-start | bytes 5505032 | tf_op jit(solution)/shard_map/ppermute | solution.py:645
  354.0 29.5 %collective-permute-start.45 = (bf16[256,2688]{1,0:T(8,128)(2,1)}, bf16[256,2688]{1,0:T(8,128)(2,1)}, u32[]{:S(2)}, u32[]{:S(2)}) collective-permute-start(bf16[256,2688]{1,0:T(8,128)(2,1)} %pad_maximum_fusion.2.refs_0_), channel_id=1, source_target_pairs={{0,2},{1,5},{2,0},{3,7},{4,6},{5,1},{6,4},{7,3},{8,10},{9,13},{10,... | collective-permute-start | bytes 4128776 | tf_op jit(solution)/shard_map/ppermute | solution.py:645
  (91 other events, 625.1 us)

commit v4 on v3

--- a/solution.py
+++ b/solution.py
@@ -30,12 +30,12 @@
     "state",
     "wide",
     "down",
+    "scan",
     "grads",
-    "scan",
     "wide",
     "down",
+    "attend",
     "outs",
-    "attend",
     "wide",
     "sums",
     "early",

time: 398 us -> 390 us (0.980)
  starting transfers between devices: 42.9 us -> 34.2 us
    ppermute x1, starting transfers between devices: 8.79 us -> 1.91 us  [local(): d_prior_got = lax.ppermute(token, 'shard', [(1, 0)])]
    unnamed x152 -> x142, local copies, waits for them, and re-layouts: 33.2 us -> 35.7 us
  transfers between devices with their start and end apart: 47 -> 47, of which waited for: 20 -> 19; matrix products, arithmetic and copies ran while one was open for 9% -> 9% of each run, Pallas kernels for 26% -> 28%
where the time goes in v4:
time: 390 us; the launch traced here: 384 us
  Pallas kernels  150 us (38%)
  waiting for transfers between devices  114 us (29%)
  other arithmetic  42.7 us (11%)
  local copies, waits for them, and re-layouts  41.4 us (11%)
  starting transfers between devices  34.2 us (9%)
    ppermute x26, waiting for transfers between devices, go(): got = lax.ppermute(self.operand, ('rep', 'shard'), self.pairs(step))  108 us
    pallas_call x1, Pallas kernels, run_middle(): pl.pallas_call(middle_kernel, grid_spec=pltpu.PrefetchScalarGridSpec(num_...  39.9 us
    unnamed x142, local copies, waits for them, and re-layouts  35.7 us
    convert_element_type x20, other arithmetic, part(): return total.astype(BF)  34.2 us
    ppermute x26, starting transfers between devices, go(): got = lax.ppermute(self.operand, ('rep', 'shard'), self.pairs(step))  21.5 us
    pallas_call x5, Pallas kernels, finish(): pl.pallas_call(functools.partial(finish_kernel, len(stacks), far, [cut fo...  20.4 us
    pallas_call x1, Pallas kernels, run_backward(): pl.pallas_call(backward_kernel, grid=(count,), in_specs=[scalars(), pl.Bl...  15.8 us
    pallas_call x1, Pallas kernels, run_attend_back(): pl.pallas_call(attend_back_kernel, out_shape=[jax.ShapeDtypeStruct((rows,...  14.7 us
  transfers between devices with their start and end apart: 47, of which 19 were waited for; matrix products, arithmetic and copies ran while one was open for 9% of the time, Pallas kernels for 28%

profile of v4, /device:TPU:1, one launch (start us, length us, event | category | flops | bytes accessed | tf_op | source)
XLA Modules:
  0.0 383.9 jit_solution(4797732191665580286)
XLA Ops:
  12.4 5.1 %project_small.1 = (bf16[512,1024]{1,0:T(8,128)(2,1)}, bf16[512,512]{1,0:T(8,128)(2,1)}, bf16[512,256]{1,0:T(8,128)(2,1)}, f32[512,384]{1,0:T(8,128)}, f32[512,128]{1,0:T(8,128)}, /*index=5*/f32[8,128]{1,0:T(8,128)}) custom-call(s32[1]{0:T(128)} %bitcast.position, bf16[512,1024]{1,0:T(8,128)(2,1)} %tokens.5, f32[1,1024]{1,0:T(1,128)} %copy-done.58, ...), custom_call_target="tpu_custom_call" | custom-call | flops 15000000512 | bytes 1000000 | tf_op jit(solution)/shard_map/project_small/pallas_call | solution.py:937
  19.2 11.4 %project.1 = (bf16[512,3072]{1,0:T(8,128)(2,1)}, f32[128,1536]{1,0:T(8,128)}) custom-call(s32[1]{0:T(128)} %bitcast.position, s32[4]{0:T(128)} %compare_convert_fusion.resets, bf16[512,1024]{1,0:T(8,128)(2,1)} %get-tuple-element.111.normed, f32[512,384]{1,0:T(8,128)} %get-tuple-element.112.aux, f32[512,128]{1,0:T(8,128)} %get-tuple-element.113.tails, ...), custom_call_target="tpu_custom_call" | custom-call | flops 15000000512 | bytes 1000000 | tf_op jit(solution)/shard_map/project/pallas_call | solution.py:997
  32.2 8.7 %attend.1 = (bf16[512,512]{1,0:T(8,128)(2,1)S(1)}, f32[512,8]{1,0:T(8,128)S(1)}) custom-call(bf16[512,512]{1,0:T(8,128)(2,1)S(1)} %copy-done.45, bf16[512,256]{1,0:T(8,128)(2,1)} %collective-permute-done.4.prior_ref, bf16[512,256]{1,0:T(8,128)(2,1)S(1)} %copy-done.53, f32[4,1024]{1,0:T(4,128)S(1)} %compare_select_fusion.bias_ref), custom_call_target="tpu_custom_call" | custom-call | flops 15000000512 | bytes 1000000 | tf_op jit(solution)/shard_map/attend/pallas_call | solution.py:532
  43.3 8.7 %ssm_forward.1 = (f32[512,1536]{1,0:T(8,128)S(1)}, bf16[512,1536]{1,0:T(8,128)(2,1)S(1)}, bf16[4,128,1536]{2,1,0:T(8,128)(2,1)S(1)}) custom-call(s32[4]{0:T(128)S(1)} %copy-done.60, bf16[512,3072]{1,0:T(8,128)(2,1)S(1)} %copy-done.1, bf16[512,3072]{1,0:T(8,128)(2,1)S(1)} %copy-done.1, f32[512,384]{1,0:T(8,128)S(1)} %copy-done.22, f32[1,128]{1,0:T(1,128)S(1)} %copy-done.64, ...), custom_call_target="tpu_custom_call" | custom-call | flops 15000000512 | bytes 1000000 | tf_op jit(solution)/shard_map/ssm_forward/pallas_call | solution.py:349
  56.0 39.9 %middle.1 = (bf16[512,1024]{1,0:T(8,128)(2,1)}, f32[512,1024]{1,0:T(8,128)}, bf16[512,1024]{1,0:T(8,128)(2,1)S(1)}, bf16[512,1024]{1,0:T(8,128)(2,1)}, bf16[512,...) custom-call(s32[1]{0:T(128)} %bitcast.position, ...), custom_call_target="tpu_custom_call" | custom-call | flops 15000000512 | bytes 1000000 | tf_op jit(solution)/shard_map/middle/pallas_call | solution.py:1167
  98.2 7.3 %ssm_state_back.1 = (bf16[128,1536]{1,0:T(8,128)(2,1)}, bf16[512,1536]{1,0:T(8,128)(2,1)}) custom-call(s32[4]{0:T(128)} %compare_convert_fusion.resets, bf16[512,1536]{1,0:T(8,128)(2,1)} %get-tuple-element.133.d_gated, bf16[512,3072]{1,0:T(8,128)(2,1)} %get-tuple-element.116.mixed.gate, f32[512,384]{1,0:T(8,128)} %get-tuple-element.112.aux, ...), custom_call_target="tpu_custom_call" | custom-call | flops 1000000 | bytes 1000000 | tf_op jit(solution)/shard_map/ssm_state_back/pallas_call | solution.py:381
  108.2 4.4 %add_convert_fusion = bf16[256,4096]{1,0:T(8,128)(2,1)} fusion(bf16[512,4096]{1,0:T(8,128)(2,1)} %collective-permute-done.16.refs_2_, s32[]{:T(128)S(6)} %select_n.253, bf16[512,4096]{1,0:T(8,128)(2,1)} %get-tuple-element.125), kind=kLoop, calls=%fused_computation | loop fusion | flops 4194304 | bytes 6291460 | tf_op jit(solution)/shard_map/convert_element_type | solution.py:615
  128.2 15.8 %ssm_backward.1 = (bf16[512,1536]{1,0:T(8,128)(2,1)S(1)}, bf16[512,384]{1,0:T(8,128)(2,1)S(1)}, f32[8,128]{1,0:T(8,128)S(1)}) custom-call(s32[4]{0:T(128)S(1)} %copy-done.61, bf16[512,1536]{1,0:T(8,128)(2,1)S(1)} %copy-done.13, bf16[512,3072]{1,0:T(8,128)(2,1)S(1)} %copy-done.2, bf16[512,3072]{1,0:T(8,128)(2,1)S(1)} %copy-done.2, f32[512,384]{1,0:T(8,128)S(1)} %copy-done.23, ...), custom_call_target="tpu_custom_call" | custom-call | flops 1000000 | bytes 1000000 | tf_op jit(solution)/shard_map/ssm_backward/pallas_call | solution.py:409
  146.0 4.7 %outs_grads.1 = (bf16[256,7168]{1,0:T(8,128)(2,1)S(1)}, bf16[256,7168]{1,0:T(8,128)(2,1)S(1)}) custom-call(s32[1]{0:T(128)} %bitcast.position, bf16[512,512]{1,0:T(8,128)(2,1)S(1)} %copy-done.50, bf16[512,1536]{1,0:T(8,128)(2,1)S(1)} %copy-done.35, bf16[512,1024]{1,0:T(8,128)(2,1)S(1)} %copy-done.17, bf16[512,1024]{1,0:T(8,128)(2,1)S(1)} %copy-done.43, ...), custom_call_target="tpu_custom_call" | custom-call | flops 1000000 | bytes 1000000 | tf_op jit(solution)/shard_map/outs_grads/pallas_call | solution.py:1249
  154.8 3.5 add_convert_fusion.3
  162.3 14.7 %attend_back.1 = (bf16[512,512]{1,0:T(8,128)(2,1)S(1)}, bf16[512,256]{1,0:T(8,128)(2,1)S(1)}, f32[512,256]{1,0:T(8,128)S(1)}) custom-call(bf16[512,512]{1,0:T(8,128)(2,1)S(1)} %copy-done.46, bf16[512,256]{1,0:T(8,128)(2,1)} %collective-permute-done.4.prior_ref, bf16[512,256]{1,0:T(8,128)(2,1)S(1)} %copy-done.53, f32[4,1024]{1,0:T(4,128)S(1)} %compare_select_fusion.bias_ref, ...), custom_call_target="tpu_custom_call" | custom-call | flops 1000000 | bytes 1000000 | tf_op jit(solution)/shard_map/attend_back/pallas_call | solution.py:547
  179.5 3.9 %add_convert_fusion.1 = bf16[128,7168]{1,0:T(8,128)(2,1)} fusion(bf16[256,7168]{1,0:T(8,128)(2,1)} %collective-permute-done.22.refs_3_, s32[]{:T(128)S(6)} %select_n.265, bf16[256,7168]{1,0:T(8,128)(2,1)} %copy-done.20), kind=kLoop, calls=%fused_computation.1 | loop fusion | flops 3670016 | bytes 5505028 | tf_op jit(solution)/shard_map/convert_element_type | solution.py:615
  194.1 5.0 %rest_grads.1 = (bf16[512,2688]{1,0:T(8,128)(2,1)}, bf16[512,2688]{1,0:T(8,128)(2,1)S(1)}) custom-call(s32[1]{0:T(128)} %bitcast.position, bf16[512,1024]{1,0:T(8,128)(2,1)S(1)} %copy-done.18, bf16[512,512]{1,0:T(8,128)(2,1)S(1)} %copy-done.32, bf16[512,256]{1,0:T(8,128)(2,1)S(1)} %add_convert_fusion.20.d_kv, bf16[512,1536]{1,0:T(8,128)(2,1)S(1)} %copy-done.9, ...), custom_call_target="tpu_custom_call" | custom-call | flops 1000000 | bytes 1000000 | tf_op jit(solution)/shard_map/rest_grads/pallas_call | solution.py:1354
  208.2 3.9 %early_back.1.d_normed = f32[512,1024]{1,0:T(8,128)S(1)} custom-call(s32[1]{0:T(128)} %bitcast.position, bf16[512,512]{1,0:T(8,128)(2,1)S(1)} %copy-done.33, bf16[512,256]{1,0:T(8,128)(2,1)S(1)} %add_convert_fusion.20.d_kv, bf16[512,1536]{1,0:T(8,128)(2,1)S(1)} %copy-done.12, bf16[512,512]{1,0:T(8,128)(2,1)S(1)} %copy-done.14, ...), custom_call_target="tpu_custom_call" | custom-call | flops 1000000 | bytes 1000000 | tf_op jit(solution)/shard_map/early_back/pallas_call | solution.py:1295
  225.8 5.8 %collective-permute-done.25 = bf16[64,7168]{1,0:T(8,128)(2,1)S(1)} collective-permute-done((bf16[64,7168]{1,0:T(8,128)(2,1)S(1)}, bf16[64,7168]{1,0:T(8,128)(2,1)S(1)}, u32[]{:S(2)}, u32[]{:S(2)}) %collective-permute-start.25) | collective-permute-done | bytes 917536 | tf_op jit(solution)/shard_map/ppermute | solution.py:645
  233.4 14.7 %collective-permute-done.32 = bf16[64,4096]{1,0:T(8,128)(2,1)S(1)} collective-permute-done((bf16[64,4096]{1,0:T(8,128)(2,1)S(1)}, bf16[64,4096]{1,0:T(8,128)(2,1)S(1)}, u32[]{:S(2)}, u32[]{:S(2)}) %collective-permute-start.32) | collective-permute-done | bytes 524320 | tf_op jit(solution)/shard_map/ppermute | solution.py:645
  250.5 3.4 collective-permute-done.30
  256.5 6.5 %collective-permute-done.36 = bf16[64,4096]{1,0:T(8,128)(2,1)S(1)} collective-permute-done((bf16[64,4096]{1,0:T(8,128)(2,1)S(1)}, bf16[64,4096]{1,0:T(8,128)(2,1)S(1)}, u32[]{:S(2)}, u32[]{:S(2)}) %collective-permute-start.36) | collective-permute-done | bytes 524320 | tf_op jit(solution)/shard_map/ppermute | solution.py:645
  263.8 3.7 collective-permute-done.35
  269.7 5.2 %collective-permute-done.34 = bf16[256,1024]{1,0:T(8,128)(2,1)S(1)} collective-permute-done((bf16[256,1024]{1,0:T(8,128)(2,1)S(1)}, bf16[256,1024]{1,0:T(8,128)(2,1)S(1)}, u32[]{:S(2)}, u32[]{:S(2)}) %collective-permute-start.34) | collective-permute-done | bytes 524320 | tf_op jit(solution)/shard_map/ppermute | solution.py:645
  276.8 9.3 %collective-permute-done.40 = bf16[128,4096]{1,0:T(8,128)(2,1)S(1)} collective-permute-done((bf16[128,4096]{1,0:T(8,128)(2,1)S(1)}, bf16[128,4096]{1,0:T(8,128)(2,1)S(1)}, u32[]{:S(2)}, u32[]{:S(2)}) %collective-permute-start.40) | collective-permute-done | bytes 1048608 | tf_op jit(solution)/shard_map/ppermute | solution.py:645
  287.8 5.3 %collective-permute-done.39 = bf16[128,2688]{1,0:T(8,128)(2,1)S(1)} collective-permute-done((bf16[128,2688]{1,0:T(8,128)(2,1)S(1)}, bf16[128,2688]{1,0:T(8,128)(2,1)S(1)}, u32[]{:S(2)}, u32[]{:S(2)}) %collective-permute-start.39) | collective-permute-done | bytes 688160 | tf_op jit(solution)/shard_map/ppermute | solution.py:645
  293.4 26.8 %collective-permute-done.38.refs_1_ = bf16[512,1024]{1,0:T(8,128)(2,1)S(1)} collective-permute-done((bf16[512,1024]{1,0:T(8,128)(2,1)S(1)}, bf16[512,1024]{1,0:T(8,128)(2,1)S(1)}, u32[]{:S(2)}, u32[]{:S(2)}) %collective-permute-start.38) | collective-permute-done | bytes 1048608 | tf_op jit(solution)/shard_map/ppermute | solution.py:645
  320.2 3.2 unpack.5
  326.2 4.4 %late_back.1 = f32[512,1024]{1,0:T(8,128)} custom-call(s32[1]{0:T(128)} %bitcast.position, bf16[512,1024]{1,0:T(8,128)(2,1)S(1)} %copy-done.41, f32[1,1024]{1,0:T(1,128)S(1)} %copy-done.59, f32[512,1024]{1,0:T(8,128)S(1)} %copy-done.30, f32[512,1024]{1,0:T(8,128)S(1)} %early_back.1.d_normed, bf16[512,1536]{1,0:T(8,128)(2,1)S(1)} %copy-done.10, ...), custom_call_target="tpu_custom_call" | custom-call | flops 1000000 | bytes 1000000 | tf_op jit(solution)/shard_map/late_back/pallas_call | solution.py:1403
  330.6 4.2 %unpack.6 = (f32[512,2048]{1,0:T(8,128)}, f32[512,2048]{1,0:T(8,128)}) custom-call(s32[5]{0:T(128)S(1)} %get-tuple-element.208.places, bf16[256,4096]{1,0:T(8,128)(2,1)S(1)} %pad_maximum_fusion.refs_0_, bf16[256,4096]{1,0:T(8,128)(2,1)S(1)} %collective-permute-done.42.refs_1_), custom_call_target="tpu_custom_call" | custom-call | flops 1000000 | bytes 1000000 | tf_op jit(solution)/shard_map/unpack/pallas_call | solution.py:759
  340.4 4.8 %collective-permute-done.43 = bf16[128,2688]{1,0:T(8,128)(2,1)S(1)} collective-permute-done((bf16[128,2688]{1,0:T(8,128)(2,1)S(1)}, bf16[128,2688]{1,0:T(8,128)(2,1)S(1)}, u32[]{:S(2)}, u32[]{:S(2)}) %collective-permute-start.43) | collective-permute-done | bytes 688160 | tf_op jit(solution)/shard_map/ppermute | solution.py:645
  349.8 3.4 unpack.7
  353.2 8.7 %collective-permute-done.46.refs_1_ = bf16[128,7168]{1,0:T(8,128)(2,1)} collective-permute-done((bf16[128,7168]{1,0:T(8,128)(2,1)}, bf16[128,7168]{1,0:T(8,128)(2,1)}, u32[]{:S(2)}, u32[]{:S(2)}) %collective-permute-start.46) | collective-permute-done | bytes 1835040 | tf_op jit(solution)/shard_map/ppermute | solution.py:645
  361.8 6.3 %unpack.8 = (f32[256,1024]{1,0:T(8,128)}, f32[3,256,1024]{2,1,0:T(8,128)}, f32[2,256,3072]{2,1,0:T(8,128)}) custom-call(s32[5]{0:T(128)S(1)} %get-tuple-element.209.places, bf16[128,7168]{1,0:T(8,128)(2,1)} %pad_maximum_fusion.1.refs_0_, bf16[128,7168]{1,0:T(8,128)(2,1)} %collective-permute-done.46.refs_1_, ...), custom_call_target="tpu_custom_call", output_to_operand_aliasing={{2}: (3, {})} | custom-call | flops 1000000 | bytes 1000000 | tf_op jit(solution)/shard_map/unpack/pallas_call | solution.py:759
  368.1 8.2 %collective-permute-done.45.refs_0_ = bf16[256,2688]{1,0:T(8,128)(2,1)} collective-permute-done((bf16[256,2688]{1,0:T(8,128)(2,1)}, bf16[256,2688]{1,0:T(8,128)(2,1)}, u32[]{:S(2)}, u32[]{:S(2)}) %collective-permute-start.45) | collective-permute-done | bytes 1376288 | tf_op jit(solution)/shard_map/ppermute | solution.py:645
  376.3 3.4 unpack.9
  (288 shorter events, 118.1 us)
Async XLA Ops:
  2.6 14.9 %collective-permute-start.5 = (bf16[512,3072]{1,0:T(8,128)(2,1)}, bf16[512,3072]{1,0:T(8,128)(2,1)S(1)}, u32[]{:S(2)}, u32[]{:S(2)}) collective-permute-start(bf16[512,3072]{1,0:T(8,128)(2,1)} %refs_4_.3), channel_id=1, source_target_pairs={{0,1},{1,0},{2,3},{3,2},{4,5},{5,4},{6,7},{7,6},{8,9},{9,8},{10,11... | collective-permute-start | bytes 9437192 | tf_op jit(solution)/shard_map/ppermute | solution.py:562
  10.1 45.9 %collective-permute-start.11 = (bf16[768,1024]{1,0:T(8,128)(2,1)}, bf16[768,1024]{1,0:T(8,128)(2,1)}, u32[]{:S(2)}, u32[]{:S(2)}) collective-permute-start(bf16[768,1024]{1,0:T(8,128)(2,1)} %ssm_mine.5), channel_id=1, source_target_pairs={{0,1},{1,0},{2,3},{3,2},{4,5},{5,4},{6,7},{7,6},{8,9},{9,8},{10,11... | collective-permute-start | bytes 4718600 | tf_op jit(solution)/shard_map/ppermute | solution.py:562
  10.5 45.5 %collective-permute-start.12 = (bf16[512,2048]{1,0:T(8,128)(2,1)}, bf16[512,2048]{1,0:T(8,128)(2,1)}, u32[]{:S(2)}, u32[]{:S(2)}) collective-permute-start(bf16[512,2048]{1,0:T(8,128)(2,1)} %gate_mine.1), channel_id=1, source_target_pairs={{0,1},{1,0},{2,3},{3,2},{4,5},{5,4},{6,7},{7,6},{8,9},{9,8},{10,11... | collective-permute-start | bytes 6291464 | tf_op jit(solution)/shard_map/ppermute | solution.py:562
  11.7 44.2 %collective-permute-start.13 = (bf16[512,2048]{1,0:T(8,128)(2,1)}, bf16[512,2048]{1,0:T(8,128)(2,1)}, u32[]{:S(2)}, u32[]{:S(2)}) collective-permute-start(bf16[512,2048]{1,0:T(8,128)(2,1)} %up_mine.1), channel_id=1, source_target_pairs={{0,1},{1,0},{2,3},{3,2},{4,5},{5,4},{6,7},{7,6},{8,9},{9,8},{10,11... | collective-permute-start | bytes 6291464 | tf_op jit(solution)/shard_map/ppermute | solution.py:562
  11.9 44.1 %collective-permute-start.14 = (bf16[1024,1024]{1,0:T(8,128)(2,1)}, bf16[1024,1024]{1,0:T(8,128)(2,1)}, u32[]{:S(2)}, u32[]{:S(2)}) collective-permute-start(bf16[1024,1024]{1,0:T(8,128)(2,1)} %down_mine.1), channel_id=1, source_target_pairs={{0,1},{1,0},{2,3},{3,2},{4,5},{5,4},{6,7},{7,6},{8,9},{9,8},{10,11... | collective-permute-start | bytes 6291464 | tf_op jit(solution)/shard_map/ppermute | solution.py:562
  17.5 13.1 %collective-permute-start.4 = (bf16[512,256]{1,0:T(8,128)(2,1)}, bf16[512,256]{1,0:T(8,128)(2,1)}, u32[]{:S(2)}, u32[]{:S(2)}) collective-permute-start(bf16[512,256]{1,0:T(8,128)(2,1)} %get-tuple-element.109.here_ref), channel_id=1, source_target_pairs={{0,1},{2,3},{4,5},{6,7},{8,9},{10,11},{12,13},{14,15},{16,17},{18,... | collective-permute-start | bytes 786440 | tf_op jit(solution)/shard_map/ppermute | solution.py:1469
  41.6 14.3 %collective-permute-start.10 = (bf16[256,1024]{1,0:T(8,128)(2,1)S(1)}, bf16[256,1024]{1,0:T(8,128)(2,1)S(1)}, u32[]{:S(2)}, u32[]{:S(2)}) collective-permute-start(bf16[256,1024]{1,0:T(8,128)(2,1)S(1)} %copy-done.66), channel_id=1, source_target_pairs={{0,1},{1,0},{2,3},{3,2},{4,5},{5,4},{6,7},{7,6},{8,9},{9,8},{10,11... | collective-permute-start | bytes 1572872 | tf_op jit(solution)/shard_map/ppermute | solution.py:562
  112.6 41.8 %collective-permute-start.18 = (bf16[256,4096]{1,0:T(8,128)(2,1)}, bf16[256,4096]{1,0:T(8,128)(2,1)}, u32[]{:S(2)}, u32[]{:S(2)}) collective-permute-start(bf16[256,4096]{1,0:T(8,128)(2,1)} %add_convert_fusion), channel_id=1, source_target_pairs={{0,2},{1,5},{2,0},{3,7},{4,6},{5,1},{6,4},{7,3},{8,10},{9,13},{10,... | collective-permute-start | bytes 6291464 | tf_op jit(solution)/shard_map/ppermute | solution.py:645
  116.9 37.5 %collective-permute-start.17 = (bf16[512,1024]{1,0:T(8,128)(2,1)S(1)}, bf16[512,1024]{1,0:T(8,128)(2,1)}, u32[]{:S(2)}, u32[]{:S(2)}) collective-permute-start(bf16[512,1024]{1,0:T(8,128)(2,1)S(1)} %add_convert_fusion.4), channel_id=1, source_target_pairs={{0,8},{1,9},{2,10},{3,11},{4,12},{5,13},{6,14},{7,15},{8,0},{9,1},... | collective-permute-start | bytes 3145736 | tf_op jit(solution)/shard_map/ppermute | solution.py:645
  154.4 24.1 %collective-permute-start.22 = (bf16[256,7168]{1,0:T(8,128)(2,1)}, bf16[256,7168]{1,0:T(8,128)(2,1)}, u32[]{:S(2)}, u32[]{:S(2)}) collective-permute-start(bf16[256,7168]{1,0:T(8,128)(2,1)} %fence.4), channel_id=1, source_target_pairs={{0,1},{1,0},{2,3},{3,2},{4,5},{5,4},{6,7},{7,6},{8,9},{9,8},{10,11... | collective-permute-start | bytes 11010056 | tf_op jit(solution)/shard_map/ppermute | solution.py:562
  158.3 20.2 %collective-permute-start.21 = (bf16[128,4096]{1,0:T(8,128)(2,1)}, bf16[128,4096]{1,0:T(8,128)(2,1)S(1)}, u32[]{:S(2)}, u32[]{:S(2)}) collective-permute-start(bf16[128,4096]{1,0:T(8,128)(2,1)} %add_convert_fusion.3), channel_id=1, source_target_pairs={{0,4},{1,3},{2,6},{3,1},{4,0},{5,7},{6,2},{7,5},{8,12},{9,11},{10,... | collective-permute-start | bytes 3145736 | tf_op jit(solution)/shard_map/ppermute | solution.py:645
  161.4 17.1 %collective-permute-start.20 = (bf16[256,1024]{1,0:T(8,128)(2,1)}, bf16[256,1024]{1,0:T(8,128)(2,1)}, u32[]{:S(2)}, u32[]{:S(2)}) collective-permute-start(bf16[256,1024]{1,0:T(8,128)(2,1)} %add_convert_fusion.16), channel_id=1, source_target_pairs={{0,4},{1,3},{2,6},{3,1},{4,0},{5,7},{6,2},{7,5},{8,12},{9,11},{10,... | collective-permute-start | bytes 1572872 | tf_op jit(solution)/shard_map/ppermute | solution.py:645
  183.4 32.1 %collective-permute-start.24 = (bf16[128,7168]{1,0:T(8,128)(2,1)}, bf16[128,7168]{1,0:T(8,128)(2,1)}, u32[]{:S(2)}, u32[]{:S(2)}) collective-permute-start(bf16[128,7168]{1,0:T(8,128)(2,1)} %add_convert_fusion.1), channel_id=1, source_target_pairs={{0,8},{1,5},{2,10},{3,7},{4,12},{5,1},{6,14},{7,3},{8,0},{9,13},{1... | collective-permute-start | bytes 5505032 | tf_op jit(solution)/shard_map/ppermute | solution.py:645
  200.7 22.0 %collective-permute-start.27 = (bf16[512,2688]{1,0:T(8,128)(2,1)}, bf16[512,2688]{1,0:T(8,128)(2,1)}, u32[]{:S(2)}, u32[]{:S(2)}) collective-permute-start(bf16[512,2688]{1,0:T(8,128)(2,1)} %get-tuple-element.154), channel_id=1, source_target_pairs={{0,1},{1,0},{2,3},{3,2},{4,5},{5,4},{6,7},{7,6},{8,9},{9,8},{10,11... | collective-permute-start | bytes 8257544 | tf_op jit(solution)/shard_map/ppermute | solution.py:562
  200.7 17.5 %collective-permute-start.28 = (bf16[64,4096]{1,0:T(8,128)(2,1)}, bf16[64,4096]{1,0:T(8,128)(2,1)S(1)}, u32[]{:S(2)}, u32[]{:S(2)}) collective-permute-start(bf16[64,4096]{1,0:T(8,128)(2,1)} %add_convert_fusion.15), channel_id=1, source_target_pairs={{0,16},{1,9},{2,18},{3,11},{4,20},{5,13},{6,22},{7,15},{8,24},{9,1... | collective-permute-start | bytes 1572872 | tf_op jit(solution)/shard_map/ppermute | solution.py:645
  217.5 14.2 %collective-permute-start.25 = (bf16[64,7168]{1,0:T(8,128)(2,1)S(1)}, bf16[64,7168]{1,0:T(8,128)(2,1)S(1)}, u32[]{:S(2)}, u32[]{:S(2)}) collective-permute-start(bf16[64,7168]{1,0:T(8,128)(2,1)S(1)} %add_convert_fusion.5), channel_id=1, source_target_pairs={{0,4},{1,3},{2,6},{3,1},{4,0},{5,7},{6,2},{7,5},{8,12},{9,11},{10,... | collective-permute-start | bytes 2752520 | tf_op jit(solution)/shard_map/ppermute | solution.py:645
  220.3 27.9 %collective-permute-start.32 = (bf16[64,4096]{1,0:T(8,128)(2,1)S(1)}, bf16[64,4096]{1,0:T(8,128)(2,1)S(1)}, u32[]{:S(2)}, u32[]{:S(2)}) collective-permute-start(bf16[64,4096]{1,0:T(8,128)(2,1)S(1)} %add_convert_fusion.13), channel_id=1, source_target_pairs={{0,8},{1,17},{2,10},{3,19},{4,12},{5,21},{6,14},{7,23},{8,0},{9,25... | collective-permute-start | bytes 1572872 | tf_op jit(solution)/shard_map/ppermute | solution.py:645
  224.3 24.0 %collective-permute-start.31 = (bf16[256,2688]{1,0:T(8,128)(2,1)S(1)}, bf16[256,2688]{1,0:T(8,128)(2,1)S(1)}, u32[]{:S(2)}, u32[]{:S(2)}) collective-permute-start(bf16[256,2688]{1,0:T(8,128)(2,1)S(1)} %add_convert_fusion.2), channel_id=1, source_target_pairs={{0,2},{1,5},{2,0},{3,7},{4,6},{5,1},{6,4},{7,3},{8,10},{9,13},{10,... | collective-permute-start | bytes 4128776 | tf_op jit(solution)/shard_map/ppermute | solution.py:645
  224.8 29.1 %collective-permute-start.30 = (bf16[256,1024]{1,0:T(8,128)(2,1)S(1)}, bf16[256,1024]{1,0:T(8,128)(2,1)S(1)}, u32[]{:S(2)}, u32[]{:S(2)}) collective-permute-start(bf16[256,1024]{1,0:T(8,128)(2,1)S(1)} %add_convert_fusion.12), channel_id=1, source_target_pairs={{0,2},{1,17},{2,0},{3,19},{4,6},{5,21},{6,4},{7,23},{8,10},{9,25},... | collective-permute-start | bytes 1572872 | tf_op jit(solution)/shard_map/ppermute | solution.py:645
  233.3 21.3 %collective-permute-start.29 = (bf16[32,7168]{1,0:T(8,128)(2,1)S(1)}, bf16[32,7168]{1,0:T(8,128)(2,1)S(1)}, u32[]{:S(2)}, u32[]{:S(2)}) collective-permute-start(bf16[32,7168]{1,0:T(8,128)(2,1)S(1)} %add_convert_fusion.19), channel_id=1, source_target_pairs={{0,2},{1,9},{2,0},{3,11},{4,6},{5,13},{6,4},{7,15},{8,10},{9,1},{1... | collective-permute-start | bytes 1376264 | tf_op jit(solution)/shard_map/ppermute | solution.py:645
  248.3 14.7 %collective-permute-start.36 = (bf16[64,4096]{1,0:T(8,128)(2,1)S(1)}, bf16[64,4096]{1,0:T(8,128)(2,1)S(1)}, u32[]{:S(2)}, u32[]{:S(2)}) collective-permute-start(bf16[64,4096]{1,0:T(8,128)(2,1)S(1)} %add_convert_fusion.11), channel_id=1, source_target_pairs={{0,16},{1,9},{2,18},{3,11},{4,20},{5,13},{6,22},{7,15},{8,24},{9,1... | collective-permute-start | bytes 1572872 | tf_op jit(solution)/shard_map/ppermute | solution.py:645
  249.9 17.6 %collective-permute-start.35 = (bf16[128,2688]{1,0:T(8,128)(2,1)S(1)}, bf16[128,2688]{1,0:T(8,128)(2,1)S(1)}, u32[]{:S(2)}, u32[]{:S(2)}) collective-permute-start(bf16[128,2688]{1,0:T(8,128)(2,1)S(1)} %add_convert_fusion.9), channel_id=1, source_target_pairs={{0,8},{1,3},{2,10},{3,1},{4,12},{5,7},{6,14},{7,5},{8,0},{9,11},{1... | collective-permute-start | bytes 2064392 | tf_op jit(solution)/shard_map/ppermute | solution.py:645
  254.1 20.9 %collective-permute-start.34 = (bf16[256,1024]{1,0:T(8,128)(2,1)S(1)}, bf16[256,1024]{1,0:T(8,128)(2,1)S(1)}, u32[]{:S(2)}, u32[]{:S(2)}) collective-permute-start(bf16[256,1024]{1,0:T(8,128)(2,1)S(1)} %add_convert_fusion.10), channel_id=1, source_target_pairs={{0,4},{1,3},{2,6},{3,1},{4,0},{5,7},{6,2},{7,5},{8,12},{9,11},{10,... | collective-permute-start | bytes 1572872 | tf_op jit(solution)/shard_map/ppermute | solution.py:645
  256.4 20.4 %collective-permute-start.33 = (bf16[32,7168]{1,0:T(8,128)(2,1)S(1)}, bf16[32,7168]{1,0:T(8,128)(2,1)S(1)}, u32[]{:S(2)}, u32[]{:S(2)}) collective-permute-start(bf16[32,7168]{1,0:T(8,128)(2,1)S(1)} %add_convert_fusion.18), channel_id=1, source_target_pairs={{0,16},{1,17},{2,18},{3,19},{4,20},{5,21},{6,22},{7,23},{8,24},{9,... | collective-permute-start | bytes 1376264 | tf_op jit(solution)/shard_map/ppermute | solution.py:645
  263.0 23.2 %collective-permute-start.40 = (bf16[128,4096]{1,0:T(8,128)(2,1)S(1)}, bf16[128,4096]{1,0:T(8,128)(2,1)S(1)}, u32[]{:S(2)}, u32[]{:S(2)}) collective-permute-start(bf16[128,4096]{1,0:T(8,128)(2,1)S(1)} %pad_maximum_fusion.3), channel_id=1, source_target_pairs={{0,4},{1,3},{2,6},{3,1},{4,0},{5,7},{6,2},{7,5},{8,12},{9,11},{10,... | collective-permute-start | bytes 3145736 | tf_op jit(solution)/shard_map/ppermute | solution.py:645
  269.1 24.0 %collective-permute-start.39 = (bf16[128,2688]{1,0:T(8,128)(2,1)S(1)}, bf16[128,2688]{1,0:T(8,128)(2,1)S(1)}, u32[]{:S(2)}, u32[]{:S(2)}) collective-permute-start(bf16[128,2688]{1,0:T(8,128)(2,1)S(1)} %add_convert_fusion.8), channel_id=1, source_target_pairs={{0,4},{1,9},{2,6},{3,11},{4,0},{5,13},{6,2},{7,15},{8,12},{9,1},{1... | collective-permute-start | bytes 2064392 | tf_op jit(solution)/shard_map/ppermute | solution.py:645
  275.0 45.2 %collective-permute-start.38 = (bf16[512,1024]{1,0:T(8,128)(2,1)S(1)}, bf16[512,1024]{1,0:T(8,128)(2,1)S(1)}, u32[]{:S(2)}, u32[]{:S(2)}) collective-permute-start(bf16[512,1024]{1,0:T(8,128)(2,1)S(1)} %pad_maximum_fusion.4.refs_0_), channel_id=1, source_target_pairs={{0,8},{1,9},{2,10},{3,11},{4,12},{5,13},{6,14},{7,15},{8,0},{9,1},... | collective-permute-start | bytes 3145736 | tf_op jit(solution)/shard_map/ppermute | solution.py:645
  286.4 44.2 %collective-permute-start.42 = (bf16[256,4096]{1,0:T(8,128)(2,1)S(1)}, bf16[256,4096]{1,0:T(8,128)(2,1)S(1)}, u32[]{:S(2)}, u32[]{:S(2)}) collective-permute-start(bf16[256,4096]{1,0:T(8,128)(2,1)S(1)} %pad_maximum_fusion.refs_0_), channel_id=1, source_target_pairs={{0,2},{1,5},{2,0},{3,7},{4,6},{5,1},{6,4},{7,3},{8,10},{9,13},{10,... | collective-permute-start | bytes 6291464 | tf_op jit(solution)/shard_map/ppermute | solution.py:645
  287.8 37.3 %collective-permute-start.37 = (bf16[32,7168]{1,0:T(8,128)(2,1)S(1)}, bf16[32,7168]{1,0:T(8,128)(2,1)S(1)}, u32[]{:S(2)}, u32[]{:S(2)}) collective-permute-start(bf16[32,7168]{1,0:T(8,128)(2,1)S(1)} %add_convert_fusion.17), channel_id=1, source_target_pairs={{0,2},{1,9},{2,0},{3,11},{4,6},{5,13},{6,4},{7,15},{8,10},{9,1},{1... | collective-permute-start | bytes 1376264 | tf_op jit(solution)/shard_map/ppermute | solution.py:645
  293.3 41.4 %collective-permute-start.41 = (bf16[128,2688]{1,0:T(8,128)(2,1)S(1)}, bf16[128,2688]{1,0:T(8,128)(2,1)S(1)}, u32[]{:S(2)}, u32[]{:S(2)}) collective-permute-start(bf16[128,2688]{1,0:T(8,128)(2,1)S(1)} %add_convert_fusion.7), channel_id=1, source_target_pairs={{0,16},{1,17},{2,18},{3,19},{4,20},{5,21},{6,22},{7,23},{8,24},{9,... | collective-permute-start | bytes 2064392 | tf_op jit(solution)/shard_map/ppermute | solution.py:645
  339.1 22.7 %collective-permute-start.46 = (bf16[128,7168]{1,0:T(8,128)(2,1)}, bf16[128,7168]{1,0:T(8,128)(2,1)}, u32[]{:S(2)}, u32[]{:S(2)}) collective-permute-start(bf16[128,7168]{1,0:T(8,128)(2,1)} %pad_maximum_fusion.1.refs_0_), channel_id=1, source_target_pairs={{0,8},{1,5},{2,10},{3,7},{4,12},{5,1},{6,14},{7,3},{8,0},{9,13},{1... | collective-permute-start | bytes 5505032 | tf_op jit(solution)/shard_map/ppermute | solution.py:645
  346.4 29.9 %collective-permute-start.45 = (bf16[256,2688]{1,0:T(8,128)(2,1)}, bf16[256,2688]{1,0:T(8,128)(2,1)}, u32[]{:S(2)}, u32[]{:S(2)}) collective-permute-start(bf16[256,2688]{1,0:T(8,128)(2,1)} %pad_maximum_fusion.2.refs_0_), channel_id=1, source_target_pairs={{0,2},{1,5},{2,0},{3,7},{4,6},{5,1},{6,4},{7,3},{8,10},{9,13},{10,... | collective-permute-start | bytes 4128776 | tf_op jit(solution)/shard_map/ppermute | solution.py:645
  (86 other events, 641.5 us)

commit v5 on v4

--- a/solution.py
+++ b/solution.py
@@ -30,11 +30,11 @@
     "state",
     "wide",
     "down",
-    "scan",
+    "attend",
     "grads",
     "wide",
     "down",
-    "attend",
+    "scan",
     "outs",
     "wide",
     "sums",

time: 390 us -> 391 us (level)
    unnamed x142 -> x140, local copies, waits for them, and re-layouts: 35.7 us -> 36.1 us
  transfers between devices with their start and end apart: 47 -> 47, of which waited for: 19 -> 19; matrix products, arithmetic and copies ran while one was open for 9% -> 10% of each run, Pallas kernels for 28% -> 28%
where the time goes in v5:
time: 391 us; the launch traced here: 385 us
  Pallas kernels  150 us (38%)
  waiting for transfers between devices  112 us (29%)
  other arithmetic  43.3 us (11%)
  local copies, waits for them, and re-layouts  41.9 us (11%)
  starting transfers between devices  36.2 us (9%)
    ppermute x26, waiting for transfers between devices, go(): got = lax.ppermute(self.operand, ('rep', 'shard'), self.pairs(step))  106 us
    pallas_call x1, Pallas kernels, run_middle(): pl.pallas_call(middle_kernel, grid_spec=pltpu.PrefetchScalarGridSpec(num_...  39.9 us
    unnamed x140, local copies, waits for them, and re-layouts  36.1 us
    convert_element_type x20, other arithmetic, part(): return total.astype(BF)  34.8 us
    ppermute x26, starting transfers between devices, go(): got = lax.ppermute(self.operand, ('rep', 'shard'), self.pairs(step))  23.5 us
    pallas_call x5, Pallas kernels, finish(): pl.pallas_call(functools.partial(finish_kernel, len(stacks), far, [cut fo...  20.3 us
    pallas_call x1, Pallas kernels, run_backward(): pl.pallas_call(backward_kernel, grid=(count,), in_specs=[scalars(), pl.Bl...  15.7 us
    pallas_call x1, Pallas kernels, run_attend_back(): pl.pallas_call(attend_back_kernel, out_shape=[jax.ShapeDtypeStruct((rows,...  14.8 us
  transfers between devices with their start and end apart: 47, of which 19 were waited for; matrix products, arithmetic and copies ran while one was open for 10% of the time, Pallas kernels for 28%

profile of v5, /device:TPU:1, one launch (start us, length us, event | category | flops | bytes accessed | tf_op | source)
XLA Modules:
  0.0 384.6 jit_solution(2920200428678918155)
XLA Ops:
  12.4 5.1 %project_small.1 = (bf16[512,1024]{1,0:T(8,128)(2,1)}, bf16[512,512]{1,0:T(8,128)(2,1)}, bf16[512,256]{1,0:T(8,128)(2,1)}, f32[512,384]{1,0:T(8,128)}, f32[512,128]{1,0:T(8,128)}, /*index=5*/f32[8,128]{1,0:T(8,128)}) custom-call(s32[1]{0:T(128)} %bitcast.position, bf16[512,1024]{1,0:T(8,128)(2,1)} %tokens.5, f32[1,1024]{1,0:T(1,128)} %copy-done.54, ...), custom_call_target="tpu_custom_call" | custom-call | flops 15000000512 | bytes 1000000 | tf_op jit(solution)/shard_map/project_small/pallas_call | solution.py:937
  19.2 11.4 %project.1 = (bf16[512,3072]{1,0:T(8,128)(2,1)}, f32[128,1536]{1,0:T(8,128)}) custom-call(s32[1]{0:T(128)} %bitcast.position, s32[4]{0:T(128)} %compare_convert_fusion.resets, bf16[512,1024]{1,0:T(8,128)(2,1)} %get-tuple-element.111.normed, f32[512,384]{1,0:T(8,128)} %get-tuple-element.112.aux, f32[512,128]{1,0:T(8,128)} %get-tuple-element.113.tails, ...), custom_call_target="tpu_custom_call" | custom-call | flops 15000000512 | bytes 1000000 | tf_op jit(solution)/shard_map/project/pallas_call | solution.py:997
  32.3 8.7 %attend.1 = (bf16[512,512]{1,0:T(8,128)(2,1)S(1)}, f32[512,8]{1,0:T(8,128)S(1)}) custom-call(bf16[512,512]{1,0:T(8,128)(2,1)S(1)} %copy-done.43, bf16[512,256]{1,0:T(8,128)(2,1)} %collective-permute-done.4.prior_ref, bf16[512,256]{1,0:T(8,128)(2,1)S(1)} %copy-done.51, f32[4,1024]{1,0:T(4,128)S(1)} %compare_select_fusion.bias_ref), custom_call_target="tpu_custom_call" | custom-call | flops 15000000512 | bytes 1000000 | tf_op jit(solution)/shard_map/attend/pallas_call | solution.py:532
  43.4 8.6 %ssm_forward.1 = (f32[512,1536]{1,0:T(8,128)S(1)}, bf16[512,1536]{1,0:T(8,128)(2,1)S(1)}, bf16[4,128,1536]{2,1,0:T(8,128)(2,1)S(1)}) custom-call(s32[4]{0:T(128)S(1)} %copy-done.60, bf16[512,3072]{1,0:T(8,128)(2,1)S(1)} %copy-done.1, bf16[512,3072]{1,0:T(8,128)(2,1)S(1)} %copy-done.1, f32[512,384]{1,0:T(8,128)S(1)} %copy-done.22, f32[1,128]{1,0:T(1,128)S(1)} %copy-done.64, ...), custom_call_target="tpu_custom_call" | custom-call | flops 15000000512 | bytes 1000000 | tf_op jit(solution)/shard_map/ssm_forward/pallas_call | solution.py:349
  56.1 39.9 %middle.1 = (bf16[512,1024]{1,0:T(8,128)(2,1)}, f32[512,1024]{1,0:T(8,128)}, bf16[512,1024]{1,0:T(8,128)(2,1)S(1)}, bf16[512,1024]{1,0:T(8,128)(2,1)}, bf16[512,...) custom-call(s32[1]{0:T(128)} %bitcast.position, ...), custom_call_target="tpu_custom_call" | custom-call | flops 15000000512 | bytes 1000000 | tf_op jit(solution)/shard_map/middle/pallas_call | solution.py:1167
  97.1 7.4 %ssm_state_back.1 = (bf16[128,1536]{1,0:T(8,128)(2,1)}, bf16[512,1536]{1,0:T(8,128)(2,1)}) custom-call(s32[4]{0:T(128)} %compare_convert_fusion.resets, bf16[512,1536]{1,0:T(8,128)(2,1)} %get-tuple-element.145.d_gated, bf16[512,3072]{1,0:T(8,128)(2,1)} %get-tuple-element.116.mixed.gate, f32[512,384]{1,0:T(8,128)} %get-tuple-element.112.aux, ...), custom_call_target="tpu_custom_call" | custom-call | flops 1000000 | bytes 1000000 | tf_op jit(solution)/shard_map/ssm_state_back/pallas_call | solution.py:381
  107.1 4.4 %add_convert_fusion = bf16[256,4096]{1,0:T(8,128)(2,1)} fusion(bf16[512,4096]{1,0:T(8,128)(2,1)} %collective-permute-done.16.refs_2_, s32[]{:T(128)S(6)} %select_n.249, bf16[512,4096]{1,0:T(8,128)(2,1)} %get-tuple-element.125), kind=kLoop, calls=%fused_computation | loop fusion | flops 4194304 | bytes 6291460 | tf_op jit(solution)/shard_map/convert_element_type | solution.py:615
  117.4 14.8 %attend_back.1 = (bf16[512,512]{1,0:T(8,128)(2,1)S(1)}, bf16[512,256]{1,0:T(8,128)(2,1)S(1)}, f32[512,256]{1,0:T(8,128)S(1)}) custom-call(bf16[512,512]{1,0:T(8,128)(2,1)S(1)} %copy-done.44, bf16[512,256]{1,0:T(8,128)(2,1)} %collective-permute-done.4.prior_ref, bf16[512,256]{1,0:T(8,128)(2,1)S(1)} %copy-done.51, f32[4,1024]{1,0:T(4,128)S(1)} %compare_select_fusion.bias_ref, ...), custom_call_target="tpu_custom_call" | custom-call | flops 1000000 | bytes 1000000 | tf_op jit(solution)/shard_map/attend_back/pallas_call | solution.py:547
  135.6 4.3 %outs_grads.1 = (bf16[256,7168]{1,0:T(8,128)(2,1)S(1)}, bf16[256,7168]{1,0:T(8,128)(2,1)S(1)}) custom-call(s32[1]{0:T(128)} %bitcast.position, bf16[512,512]{1,0:T(8,128)(2,1)S(1)} %copy-done.48, bf16[512,1536]{1,0:T(8,128)(2,1)S(1)} %copy-done.35, bf16[512,1024]{1,0:T(8,128)(2,1)S(1)} %copy-done.17, bf16[512,1024]{1,0:T(8,128)(2,1)S(1)} %get-tuple-element.138.d_attn, ...), custom_call_target="tpu_custom_call" | custom-call | flops 1000000 | bytes 1000000 | tf_op jit(solution)/shard_map/outs_grads/pallas_call | solution.py:1249
  144.2 3.7 add_convert_fusion.3
  161.8 15.7 %ssm_backward.1 = (bf16[512,1536]{1,0:T(8,128)(2,1)S(1)}, bf16[512,384]{1,0:T(8,128)(2,1)S(1)}, f32[8,128]{1,0:T(8,128)S(1)}) custom-call(s32[4]{0:T(128)S(1)} %copy-done.61, bf16[512,1536]{1,0:T(8,128)(2,1)S(1)} %copy-done.13, bf16[512,3072]{1,0:T(8,128)(2,1)S(1)} %copy-done.2, bf16[512,3072]{1,0:T(8,128)(2,1)S(1)} %copy-done.2, f32[512,384]{1,0:T(8,128)S(1)} %copy-done.23, ...), custom_call_target="tpu_custom_call" | custom-call | flops 1000000 | bytes 1000000 | tf_op jit(solution)/shard_map/ssm_backward/pallas_call | solution.py:409
  180.2 3.8 add_convert_fusion.1
  194.6 5.4 %rest_grads.1 = (bf16[512,2688]{1,0:T(8,128)(2,1)}, bf16[512,2688]{1,0:T(8,128)(2,1)S(1)}) custom-call(s32[1]{0:T(128)} %bitcast.position, bf16[512,1024]{1,0:T(8,128)(2,1)S(1)} %copy-done.18, bf16[512,512]{1,0:T(8,128)(2,1)S(1)} %copy-done.32, bf16[512,256]{1,0:T(8,128)(2,1)S(1)} %add_convert_fusion.20.d_kv, bf16[512,1536]{1,0:T(8,128)(2,1)S(1)} %copy-done.9, ...), custom_call_target="tpu_custom_call" | custom-call | flops 1000000 | bytes 1000000 | tf_op jit(solution)/shard_map/rest_grads/pallas_call | solution.py:1354
  209.2 3.9 %early_back.1.d_normed = f32[512,1024]{1,0:T(8,128)S(1)} custom-call(s32[1]{0:T(128)} %bitcast.position, bf16[512,512]{1,0:T(8,128)(2,1)S(1)} %copy-done.33, bf16[512,256]{1,0:T(8,128)(2,1)S(1)} %add_convert_fusion.20.d_kv, bf16[512,1536]{1,0:T(8,128)(2,1)S(1)} %copy-done.12, bf16[512,512]{1,0:T(8,128)(2,1)S(1)} %copy-done.14, ...), custom_call_target="tpu_custom_call" | custom-call | flops 1000000 | bytes 1000000 | tf_op jit(solution)/shard_map/early_back/pallas_call | solution.py:1295
  226.8 5.6 %collective-permute-done.25 = bf16[64,7168]{1,0:T(8,128)(2,1)S(1)} collective-permute-done((bf16[64,7168]{1,0:T(8,128)(2,1)S(1)}, bf16[64,7168]{1,0:T(8,128)(2,1)S(1)}, u32[]{:S(2)}, u32[]{:S(2)}) %collective-permute-start.25) | collective-permute-done | bytes 917536 | tf_op jit(solution)/shard_map/ppermute | solution.py:645
  234.2 14.5 %collective-permute-done.32 = bf16[64,4096]{1,0:T(8,128)(2,1)S(1)} collective-permute-done((bf16[64,4096]{1,0:T(8,128)(2,1)S(1)}, bf16[64,4096]{1,0:T(8,128)(2,1)S(1)}, u32[]{:S(2)}, u32[]{:S(2)}) %collective-permute-start.32) | collective-permute-done | bytes 524320 | tf_op jit(solution)/shard_map/ppermute | solution.py:645
  251.5 2.9 collective-permute-done.30
  257.5 6.4 %collective-permute-done.36 = bf16[64,4096]{1,0:T(8,128)(2,1)S(1)} collective-permute-done((bf16[64,4096]{1,0:T(8,128)(2,1)S(1)}, bf16[64,4096]{1,0:T(8,128)(2,1)S(1)}, u32[]{:S(2)}, u32[]{:S(2)}) %collective-permute-start.36) | collective-permute-done | bytes 524320 | tf_op jit(solution)/shard_map/ppermute | solution.py:645
  264.9 3.2 collective-permute-done.35
  270.6 4.6 %collective-permute-done.34 = bf16[256,1024]{1,0:T(8,128)(2,1)S(1)} collective-permute-done((bf16[256,1024]{1,0:T(8,128)(2,1)S(1)}, bf16[256,1024]{1,0:T(8,128)(2,1)S(1)}, u32[]{:S(2)}, u32[]{:S(2)}) %collective-permute-start.34) | collective-permute-done | bytes 524320 | tf_op jit(solution)/shard_map/ppermute | solution.py:645
  277.6 8.8 %collective-permute-done.40 = bf16[128,4096]{1,0:T(8,128)(2,1)S(1)} collective-permute-done((bf16[128,4096]{1,0:T(8,128)(2,1)S(1)}, bf16[128,4096]{1,0:T(8,128)(2,1)S(1)}, u32[]{:S(2)}, u32[]{:S(2)}) %collective-permute-start.40) | collective-permute-done | bytes 1048608 | tf_op jit(solution)/shard_map/ppermute | solution.py:645
  288.1 5.2 %collective-permute-done.39 = bf16[128,2688]{1,0:T(8,128)(2,1)S(1)} collective-permute-done((bf16[128,2688]{1,0:T(8,128)(2,1)S(1)}, bf16[128,2688]{1,0:T(8,128)(2,1)S(1)}, u32[]{:S(2)}, u32[]{:S(2)}) %collective-permute-start.39) | collective-permute-done | bytes 688160 | tf_op jit(solution)/shard_map/ppermute | solution.py:645
  294.2 26.7 %collective-permute-done.38.refs_1_ = bf16[512,1024]{1,0:T(8,128)(2,1)S(1)} collective-permute-done((bf16[512,1024]{1,0:T(8,128)(2,1)S(1)}, bf16[512,1024]{1,0:T(8,128)(2,1)S(1)}, u32[]{:S(2)}, u32[]{:S(2)}) %collective-permute-start.38) | collective-permute-done | bytes 1048608 | tf_op jit(solution)/shard_map/ppermute | solution.py:645
  320.9 3.1 unpack.5
  327.0 4.4 %late_back.1 = f32[512,1024]{1,0:T(8,128)} custom-call(s32[1]{0:T(128)} %bitcast.position, bf16[512,1024]{1,0:T(8,128)(2,1)S(1)} %copy-done.41, f32[1,1024]{1,0:T(1,128)S(1)} %copy-done.55, f32[512,1024]{1,0:T(8,128)S(1)} %copy-done.30, f32[512,1024]{1,0:T(8,128)S(1)} %early_back.1.d_normed, bf16[512,1536]{1,0:T(8,128)(2,1)S(1)} %copy-done.10, ...), custom_call_target="tpu_custom_call" | custom-call | flops 1000000 | bytes 1000000 | tf_op jit(solution)/shard_map/late_back/pallas_call | solution.py:1403
  331.4 4.2 %unpack.6 = (f32[512,2048]{1,0:T(8,128)}, f32[512,2048]{1,0:T(8,128)}) custom-call(s32[5]{0:T(128)S(1)} %get-tuple-element.208.places, bf16[256,4096]{1,0:T(8,128)(2,1)S(1)} %pad_maximum_fusion.refs_0_, bf16[256,4096]{1,0:T(8,128)(2,1)S(1)} %collective-permute-done.42.refs_1_), custom_call_target="tpu_custom_call" | custom-call | flops 1000000 | bytes 1000000 | tf_op jit(solution)/shard_map/unpack/pallas_call | solution.py:759
  341.0 4.9 %collective-permute-done.43 = bf16[128,2688]{1,0:T(8,128)(2,1)S(1)} collective-permute-done((bf16[128,2688]{1,0:T(8,128)(2,1)S(1)}, bf16[128,2688]{1,0:T(8,128)(2,1)S(1)}, u32[]{:S(2)}, u32[]{:S(2)}) %collective-permute-start.43) | collective-permute-done | bytes 688160 | tf_op jit(solution)/shard_map/ppermute | solution.py:645
  350.4 3.4 unpack.7
  353.8 8.8 %collective-permute-done.46.refs_1_ = bf16[128,7168]{1,0:T(8,128)(2,1)} collective-permute-done((bf16[128,7168]{1,0:T(8,128)(2,1)}, bf16[128,7168]{1,0:T(8,128)(2,1)}, u32[]{:S(2)}, u32[]{:S(2)}) %collective-permute-start.46) | collective-permute-done | bytes 1835040 | tf_op jit(solution)/shard_map/ppermute | solution.py:645
  362.6 6.3 %unpack.8 = (f32[256,1024]{1,0:T(8,128)}, f32[3,256,1024]{2,1,0:T(8,128)}, f32[2,256,3072]{2,1,0:T(8,128)}) custom-call(s32[5]{0:T(128)S(1)} %get-tuple-element.209.places, bf16[128,7168]{1,0:T(8,128)(2,1)} %pad_maximum_fusion.1.refs_0_, bf16[128,7168]{1,0:T(8,128)(2,1)} %collective-permute-done.46.refs_1_, ...), custom_call_target="tpu_custom_call", output_to_operand_aliasing={{2}: (3, {})} | custom-call | flops 1000000 | bytes 1000000 | tf_op jit(solution)/shard_map/unpack/pallas_call | solution.py:759
  368.8 8.2 %collective-permute-done.45.refs_0_ = bf16[256,2688]{1,0:T(8,128)(2,1)} collective-permute-done((bf16[256,2688]{1,0:T(8,128)(2,1)}, bf16[256,2688]{1,0:T(8,128)(2,1)}, u32[]{:S(2)}, u32[]{:S(2)}) %collective-permute-start.45) | collective-permute-done | bytes 1376288 | tf_op jit(solution)/shard_map/ppermute | solution.py:645
  377.0 3.4 unpack.9
  (286 shorter events, 121.4 us)
Async XLA Ops:
  2.6 14.9 %collective-permute-start.5 = (bf16[512,3072]{1,0:T(8,128)(2,1)}, bf16[512,3072]{1,0:T(8,128)(2,1)S(1)}, u32[]{:S(2)}, u32[]{:S(2)}) collective-permute-start(bf16[512,3072]{1,0:T(8,128)(2,1)} %refs_4_.3), channel_id=1, source_target_pairs={{0,1},{1,0},{2,3},{3,2},{4,5},{5,4},{6,7},{7,6},{8,9},{9,8},{10,11... | collective-permute-start | bytes 9437192 | tf_op jit(solution)/shard_map/ppermute | solution.py:562
  10.1 46.0 %collective-permute-start.12 = (bf16[512,2048]{1,0:T(8,128)(2,1)}, bf16[512,2048]{1,0:T(8,128)(2,1)}, u32[]{:S(2)}, u32[]{:S(2)}) collective-permute-start(bf16[512,2048]{1,0:T(8,128)(2,1)} %gate_mine.1), channel_id=1, source_target_pairs={{0,1},{1,0},{2,3},{3,2},{4,5},{5,4},{6,7},{7,6},{8,9},{9,8},{10,11... | collective-permute-start | bytes 6291464 | tf_op jit(solution)/shard_map/ppermute | solution.py:562
  10.5 45.6 %collective-permute-start.13 = (bf16[512,2048]{1,0:T(8,128)(2,1)}, bf16[512,2048]{1,0:T(8,128)(2,1)}, u32[]{:S(2)}, u32[]{:S(2)}) collective-permute-start(bf16[512,2048]{1,0:T(8,128)(2,1)} %up_mine.1), channel_id=1, source_target_pairs={{0,1},{1,0},{2,3},{3,2},{4,5},{5,4},{6,7},{7,6},{8,9},{9,8},{10,11... | collective-permute-start | bytes 6291464 | tf_op jit(solution)/shard_map/ppermute | solution.py:562
  11.7 44.3 %collective-permute-start.14 = (bf16[1024,1024]{1,0:T(8,128)(2,1)}, bf16[1024,1024]{1,0:T(8,128)(2,1)}, u32[]{:S(2)}, u32[]{:S(2)}) collective-permute-start(bf16[1024,1024]{1,0:T(8,128)(2,1)} %down_mine.1), channel_id=1, source_target_pairs={{0,1},{1,0},{2,3},{3,2},{4,5},{5,4},{6,7},{7,6},{8,9},{9,8},{10,11... | collective-permute-start | bytes 6291464 | tf_op jit(solution)/shard_map/ppermute | solution.py:562
  11.9 44.2 %collective-permute-start.11 = (bf16[768,1024]{1,0:T(8,128)(2,1)}, bf16[768,1024]{1,0:T(8,128)(2,1)}, u32[]{:S(2)}, u32[]{:S(2)}) collective-permute-start(bf16[768,1024]{1,0:T(8,128)(2,1)} %ssm_mine.5), channel_id=1, source_target_pairs={{0,1},{1,0},{2,3},{3,2},{4,5},{5,4},{6,7},{7,6},{8,9},{9,8},{10,11... | collective-permute-start | bytes 4718600 | tf_op jit(solution)/shard_map/ppermute | solution.py:562
  17.5 13.1 %collective-permute-start.4 = (bf16[512,256]{1,0:T(8,128)(2,1)}, bf16[512,256]{1,0:T(8,128)(2,1)}, u32[]{:S(2)}, u32[]{:S(2)}) collective-permute-start(bf16[512,256]{1,0:T(8,128)(2,1)} %get-tuple-element.109.here_ref), channel_id=1, source_target_pairs={{0,1},{2,3},{4,5},{6,7},{8,9},{10,11},{12,13},{14,15},{16,17},{18,... | collective-permute-start | bytes 786440 | tf_op jit(solution)/shard_map/ppermute | solution.py:1469
  41.7 14.3 %collective-permute-start.10 = (bf16[256,1024]{1,0:T(8,128)(2,1)S(1)}, bf16[256,1024]{1,0:T(8,128)(2,1)S(1)}, u32[]{:S(2)}, u32[]{:S(2)}) collective-permute-start(bf16[256,1024]{1,0:T(8,128)(2,1)S(1)} %copy-done.66), channel_id=1, source_target_pairs={{0,1},{1,0},{2,3},{3,2},{4,5},{5,4},{6,7},{7,6},{8,9},{9,8},{10,11... | collective-permute-start | bytes 1572872 | tf_op jit(solution)/shard_map/ppermute | solution.py:562
  111.5 32.0 %collective-permute-start.18 = (bf16[256,4096]{1,0:T(8,128)(2,1)}, bf16[256,4096]{1,0:T(8,128)(2,1)}, u32[]{:S(2)}, u32[]{:S(2)}) collective-permute-start(bf16[256,4096]{1,0:T(8,128)(2,1)} %add_convert_fusion), channel_id=1, source_target_pairs={{0,2},{1,5},{2,0},{3,7},{4,6},{5,1},{6,4},{7,3},{8,10},{9,13},{10,... | collective-permute-start | bytes 6291464 | tf_op jit(solution)/shard_map/ppermute | solution.py:645
  116.0 27.5 %collective-permute-start.19 = (bf16[512,1024]{1,0:T(8,128)(2,1)S(1)}, bf16[512,1024]{1,0:T(8,128)(2,1)}, u32[]{:S(2)}, u32[]{:S(2)}) collective-permute-start(bf16[512,1024]{1,0:T(8,128)(2,1)S(1)} %add_convert_fusion.4), channel_id=1, source_target_pairs={{0,8},{1,9},{2,10},{3,11},{4,12},{5,13},{6,14},{7,15},{8,0},{9,1},... | collective-permute-start | bytes 3145736 | tf_op jit(solution)/shard_map/ppermute | solution.py:645
  143.5 36.6 %collective-permute-start.21 = (bf16[256,7168]{1,0:T(8,128)(2,1)}, bf16[256,7168]{1,0:T(8,128)(2,1)}, u32[]{:S(2)}, u32[]{:S(2)}) collective-permute-start(bf16[256,7168]{1,0:T(8,128)(2,1)} %fence.4), channel_id=1, source_target_pairs={{0,1},{1,0},{2,3},{3,2},{4,5},{5,4},{6,7},{7,6},{8,9},{9,8},{10,11... | collective-permute-start | bytes 11010056 | tf_op jit(solution)/shard_map/ppermute | solution.py:562
  147.9 32.2 %collective-permute-start.20 = (bf16[128,4096]{1,0:T(8,128)(2,1)}, bf16[128,4096]{1,0:T(8,128)(2,1)}, u32[]{:S(2)}, u32[]{:S(2)}) collective-permute-start(bf16[128,4096]{1,0:T(8,128)(2,1)} %add_convert_fusion.3), channel_id=1, source_target_pairs={{0,4},{1,3},{2,6},{3,1},{4,0},{5,7},{6,2},{7,5},{8,12},{9,11},{10,... | collective-permute-start | bytes 3145736 | tf_op jit(solution)/shard_map/ppermute | solution.py:645
  151.0 29.1 %collective-permute-start.23 = (bf16[256,1024]{1,0:T(8,128)(2,1)}, bf16[256,1024]{1,0:T(8,128)(2,1)}, u32[]{:S(2)}, u32[]{:S(2)}) collective-permute-start(bf16[256,1024]{1,0:T(8,128)(2,1)} %add_convert_fusion.16), channel_id=1, source_target_pairs={{0,4},{1,3},{2,6},{3,1},{4,0},{5,7},{6,2},{7,5},{8,12},{9,11},{10,... | collective-permute-start | bytes 1572872 | tf_op jit(solution)/shard_map/ppermute | solution.py:645
  183.9 32.4 %collective-permute-start.24 = (bf16[128,7168]{1,0:T(8,128)(2,1)}, bf16[128,7168]{1,0:T(8,128)(2,1)}, u32[]{:S(2)}, u32[]{:S(2)}) collective-permute-start(bf16[128,7168]{1,0:T(8,128)(2,1)} %add_convert_fusion.1), channel_id=1, source_target_pairs={{0,8},{1,5},{2,10},{3,7},{4,12},{5,1},{6,14},{7,3},{8,0},{9,13},{1... | collective-permute-start | bytes 5505032 | tf_op jit(solution)/shard_map/ppermute | solution.py:645
  201.5 21.9 %collective-permute-start.27 = (bf16[512,2688]{1,0:T(8,128)(2,1)}, bf16[512,2688]{1,0:T(8,128)(2,1)}, u32[]{:S(2)}, u32[]{:S(2)}) collective-permute-start(bf16[512,2688]{1,0:T(8,128)(2,1)} %get-tuple-element.154), channel_id=1, source_target_pairs={{0,1},{1,0},{2,3},{3,2},{4,5},{5,4},{6,7},{7,6},{8,9},{9,8},{10,11... | collective-permute-start | bytes 8257544 | tf_op jit(solution)/shard_map/ppermute | solution.py:562
  201.5 17.2 %collective-permute-start.28 = (bf16[64,4096]{1,0:T(8,128)(2,1)}, bf16[64,4096]{1,0:T(8,128)(2,1)S(1)}, u32[]{:S(2)}, u32[]{:S(2)}) collective-permute-start(bf16[64,4096]{1,0:T(8,128)(2,1)} %add_convert_fusion.15), channel_id=1, source_target_pairs={{0,16},{1,9},{2,18},{3,11},{4,20},{5,13},{6,22},{7,15},{8,24},{9,1... | collective-permute-start | bytes 1572872 | tf_op jit(solution)/shard_map/ppermute | solution.py:645
  218.4 14.0 %collective-permute-start.25 = (bf16[64,7168]{1,0:T(8,128)(2,1)S(1)}, bf16[64,7168]{1,0:T(8,128)(2,1)S(1)}, u32[]{:S(2)}, u32[]{:S(2)}) collective-permute-start(bf16[64,7168]{1,0:T(8,128)(2,1)S(1)} %add_convert_fusion.5), channel_id=1, source_target_pairs={{0,4},{1,3},{2,6},{3,1},{4,0},{5,7},{6,2},{7,5},{8,12},{9,11},{10,... | collective-permute-start | bytes 2752520 | tf_op jit(solution)/shard_map/ppermute | solution.py:645
  221.0 27.7 %collective-permute-start.32 = (bf16[64,4096]{1,0:T(8,128)(2,1)S(1)}, bf16[64,4096]{1,0:T(8,128)(2,1)S(1)}, u32[]{:S(2)}, u32[]{:S(2)}) collective-permute-start(bf16[64,4096]{1,0:T(8,128)(2,1)S(1)} %add_convert_fusion.13), channel_id=1, source_target_pairs={{0,8},{1,17},{2,10},{3,19},{4,12},{5,21},{6,14},{7,23},{8,0},{9,25... | collective-permute-start | bytes 1572872 | tf_op jit(solution)/shard_map/ppermute | solution.py:645
  225.1 23.8 %collective-permute-start.31 = (bf16[256,2688]{1,0:T(8,128)(2,1)S(1)}, bf16[256,2688]{1,0:T(8,128)(2,1)S(1)}, u32[]{:S(2)}, u32[]{:S(2)}) collective-permute-start(bf16[256,2688]{1,0:T(8,128)(2,1)S(1)} %add_convert_fusion.2), channel_id=1, source_target_pairs={{0,2},{1,5},{2,0},{3,7},{4,6},{5,1},{6,4},{7,3},{8,10},{9,13},{10,... | collective-permute-start | bytes 4128776 | tf_op jit(solution)/shard_map/ppermute | solution.py:645
  226.1 28.4 %collective-permute-start.30 = (bf16[256,1024]{1,0:T(8,128)(2,1)S(1)}, bf16[256,1024]{1,0:T(8,128)(2,1)S(1)}, u32[]{:S(2)}, u32[]{:S(2)}) collective-permute-start(bf16[256,1024]{1,0:T(8,128)(2,1)S(1)} %add_convert_fusion.12), channel_id=1, source_target_pairs={{0,2},{1,17},{2,0},{3,19},{4,6},{5,21},{6,4},{7,23},{8,10},{9,25},... | collective-permute-start | bytes 1572872 | tf_op jit(solution)/shard_map/ppermute | solution.py:645
  234.1 21.6 %collective-permute-start.29 = (bf16[32,7168]{1,0:T(8,128)(2,1)S(1)}, bf16[32,7168]{1,0:T(8,128)(2,1)S(1)}, u32[]{:S(2)}, u32[]{:S(2)}) collective-permute-start(bf16[32,7168]{1,0:T(8,128)(2,1)S(1)} %add_convert_fusion.19), channel_id=1, source_target_pairs={{0,2},{1,9},{2,0},{3,11},{4,6},{5,13},{6,4},{7,15},{8,10},{9,1},{1... | collective-permute-start | bytes 1376264 | tf_op jit(solution)/shard_map/ppermute | solution.py:645
  248.9 15.0 %collective-permute-start.36 = (bf16[64,4096]{1,0:T(8,128)(2,1)S(1)}, bf16[64,4096]{1,0:T(8,128)(2,1)S(1)}, u32[]{:S(2)}, u32[]{:S(2)}) collective-permute-start(bf16[64,4096]{1,0:T(8,128)(2,1)S(1)} %add_convert_fusion.11), channel_id=1, source_target_pairs={{0,16},{1,9},{2,18},{3,11},{4,20},{5,13},{6,22},{7,15},{8,24},{9,1... | collective-permute-start | bytes 1572872 | tf_op jit(solution)/shard_map/ppermute | solution.py:645
  250.5 17.6 %collective-permute-start.35 = (bf16[128,2688]{1,0:T(8,128)(2,1)S(1)}, bf16[128,2688]{1,0:T(8,128)(2,1)S(1)}, u32[]{:S(2)}, u32[]{:S(2)}) collective-permute-start(bf16[128,2688]{1,0:T(8,128)(2,1)S(1)} %add_convert_fusion.9), channel_id=1, source_target_pairs={{0,8},{1,3},{2,10},{3,1},{4,12},{5,7},{6,14},{7,5},{8,0},{9,11},{1... | collective-permute-start | bytes 2064392 | tf_op jit(solution)/shard_map/ppermute | solution.py:645
  254.6 20.5 %collective-permute-start.34 = (bf16[256,1024]{1,0:T(8,128)(2,1)S(1)}, bf16[256,1024]{1,0:T(8,128)(2,1)S(1)}, u32[]{:S(2)}, u32[]{:S(2)}) collective-permute-start(bf16[256,1024]{1,0:T(8,128)(2,1)S(1)} %add_convert_fusion.10), channel_id=1, source_target_pairs={{0,4},{1,3},{2,6},{3,1},{4,0},{5,7},{6,2},{7,5},{8,12},{9,11},{10,... | collective-permute-start | bytes 1572872 | tf_op jit(solution)/shard_map/ppermute | solution.py:645
  257.4 20.1 %collective-permute-start.33 = (bf16[32,7168]{1,0:T(8,128)(2,1)S(1)}, bf16[32,7168]{1,0:T(8,128)(2,1)S(1)}, u32[]{:S(2)}, u32[]{:S(2)}) collective-permute-start(bf16[32,7168]{1,0:T(8,128)(2,1)S(1)} %add_convert_fusion.18), channel_id=1, source_target_pairs={{0,16},{1,17},{2,18},{3,19},{4,20},{5,21},{6,22},{7,23},{8,24},{9,... | collective-permute-start | bytes 1376264 | tf_op jit(solution)/shard_map/ppermute | solution.py:645
  263.9 22.5 %collective-permute-start.40 = (bf16[128,4096]{1,0:T(8,128)(2,1)S(1)}, bf16[128,4096]{1,0:T(8,128)(2,1)S(1)}, u32[]{:S(2)}, u32[]{:S(2)}) collective-permute-start(bf16[128,4096]{1,0:T(8,128)(2,1)S(1)} %pad_maximum_fusion.3), channel_id=1, source_target_pairs={{0,4},{1,3},{2,6},{3,1},{4,0},{5,7},{6,2},{7,5},{8,12},{9,11},{10,... | collective-permute-start | bytes 3145736 | tf_op jit(solution)/shard_map/ppermute | solution.py:645
  269.7 23.5 %collective-permute-start.39 = (bf16[128,2688]{1,0:T(8,128)(2,1)S(1)}, bf16[128,2688]{1,0:T(8,128)(2,1)S(1)}, u32[]{:S(2)}, u32[]{:S(2)}) collective-permute-start(bf16[128,2688]{1,0:T(8,128)(2,1)S(1)} %add_convert_fusion.8), channel_id=1, source_target_pairs={{0,4},{1,9},{2,6},{3,11},{4,0},{5,13},{6,2},{7,15},{8,12},{9,1},{1... | collective-permute-start | bytes 2064392 | tf_op jit(solution)/shard_map/ppermute | solution.py:645
  275.2 45.7 %collective-permute-start.38 = (bf16[512,1024]{1,0:T(8,128)(2,1)S(1)}, bf16[512,1024]{1,0:T(8,128)(2,1)S(1)}, u32[]{:S(2)}, u32[]{:S(2)}) collective-permute-start(bf16[512,1024]{1,0:T(8,128)(2,1)S(1)} %pad_maximum_fusion.4.refs_0_), channel_id=1, source_target_pairs={{0,8},{1,9},{2,10},{3,11},{4,12},{5,13},{6,14},{7,15},{8,0},{9,1},... | collective-permute-start | bytes 3145736 | tf_op jit(solution)/shard_map/ppermute | solution.py:645
  286.6 44.8 %collective-permute-start.42 = (bf16[256,4096]{1,0:T(8,128)(2,1)S(1)}, bf16[256,4096]{1,0:T(8,128)(2,1)S(1)}, u32[]{:S(2)}, u32[]{:S(2)}) collective-permute-start(bf16[256,4096]{1,0:T(8,128)(2,1)S(1)} %pad_maximum_fusion.refs_0_), channel_id=1, source_target_pairs={{0,2},{1,5},{2,0},{3,7},{4,6},{5,1},{6,4},{7,3},{8,10},{9,13},{10,... | collective-permute-start | bytes 6291464 | tf_op jit(solution)/shard_map/ppermute | solution.py:645
  288.1 37.8 %collective-permute-start.37 = (bf16[32,7168]{1,0:T(8,128)(2,1)S(1)}, bf16[32,7168]{1,0:T(8,128)(2,1)S(1)}, u32[]{:S(2)}, u32[]{:S(2)}) collective-permute-start(bf16[32,7168]{1,0:T(8,128)(2,1)S(1)} %add_convert_fusion.17), channel_id=1, source_target_pairs={{0,2},{1,9},{2,0},{3,11},{4,6},{5,13},{6,4},{7,15},{8,10},{9,1},{1... | collective-permute-start | bytes 1376264 | tf_op jit(solution)/shard_map/ppermute | solution.py:645
  293.5 42.1 %collective-permute-start.41 = (bf16[128,2688]{1,0:T(8,128)(2,1)S(1)}, bf16[128,2688]{1,0:T(8,128)(2,1)S(1)}, u32[]{:S(2)}, u32[]{:S(2)}) collective-permute-start(bf16[128,2688]{1,0:T(8,128)(2,1)S(1)} %add_convert_fusion.7), channel_id=1, source_target_pairs={{0,16},{1,17},{2,18},{3,19},{4,20},{5,21},{6,22},{7,23},{8,24},{9,... | collective-permute-start | bytes 2064392 | tf_op jit(solution)/shard_map/ppermute | solution.py:645
  339.9 22.7 %collective-permute-start.46 = (bf16[128,7168]{1,0:T(8,128)(2,1)}, bf16[128,7168]{1,0:T(8,128)(2,1)}, u32[]{:S(2)}, u32[]{:S(2)}) collective-permute-start(bf16[128,7168]{1,0:T(8,128)(2,1)} %pad_maximum_fusion.1.refs_0_), channel_id=1, source_target_pairs={{0,8},{1,5},{2,10},{3,7},{4,12},{5,1},{6,14},{7,3},{8,0},{9,13},{1... | collective-permute-start | bytes 5505032 | tf_op jit(solution)/shard_map/ppermute | solution.py:645
  347.1 29.9 %collective-permute-start.45 = (bf16[256,2688]{1,0:T(8,128)(2,1)}, bf16[256,2688]{1,0:T(8,128)(2,1)}, u32[]{:S(2)}, u32[]{:S(2)}) collective-permute-start(bf16[256,2688]{1,0:T(8,128)(2,1)} %pad_maximum_fusion.2.refs_0_), channel_id=1, source_target_pairs={{0,2},{1,5},{2,0},{3,7},{4,6},{5,1},{6,4},{7,3},{8,10},{9,13},{10,... | collective-permute-start | bytes 4128776 | tf_op jit(solution)/shard_map/ppermute | solution.py:645
  (85 other events, 628.4 us)
